TPU v7x, 32 devices: a whole 2x2x4 slice. The times are simulated.
32 devices in a mesh: space: 8 (over y, x, core), filt: 4 (over z).
Axes of the slice: x: 2, y: 2, z: 4, core: 2. Of those that a mesh axis runs over, the one named last changes fastest.
Arguments:
- volume: bfloat16 [32, 64, 16, 128], P('space', 'filt'), may hold values from -6 to 6
- w_early: bfloat16 [27, 128, 128], replicated, may hold values from -0.109375 to 0.109375
- w_deep: bfloat16 [27, 128, 256], P(None, None, 'filt'), may hold values from -0.109375 to 0.109375
- cotangent: bfloat16 [16, 32, 8, 256], P('space', None, None, 'filt'), may hold values from -6 to 6
Outputs:
- block_out: bfloat16 [16, 32, 8, 256], P('space', None, None, 'filt')
- grad_early: float32 [27, 128, 128], replicated
- grad_deep: float32 [27, 128, 256], P(None, None, 'filt')
All inputs are finite; a program needn't handle non-finite values.
Results may differ from a plain program's by a relative error of at most 0.0059.
Values may be sent and summed in bfloat16 or wider, within the bound.
No kernel may reach another device: no remote copies, remote signals or barrier semaphores. Data moves between devices by JAX's collectives and lax.ppermute only.
A program may use at most 128 MiB of HBM per device.

v0:
```python
import functools
import math

import jax
import jax.numpy as jnp
from jax import lax
from jax.experimental import pallas as pl
from jax.experimental.pallas import tpu as pltpu
from jax.sharding import PartitionSpec as P

F32 = jnp.float32
BF16 = jnp.bfloat16
HOLD = 1 << 32
VMEM_LIMIT = 24 * 1024 * 1024
VMEM = pl.BlockSpec(memory_space=pltpu.VMEM)
HBM = pl.BlockSpec(memory_space=pltpu.HBM)
DMA = pltpu.SemaphoreType.DMA


def call(
    body, name, out_shape, operands, scratch=(), flops=0, moved=1 << 20, hbm=(), outs=VMEM, alias=()
):
    return pl.pallas_call(
        body,
        name=name,
        out_shape=out_shape,
        in_specs=[HBM if i in hbm else VMEM for i in range(len(operands))],
        out_specs=outs if isinstance(outs, list) else jax.tree.map(lambda _: outs, out_shape),
        scratch_shapes=list(scratch),
        input_output_aliases=dict(alias),
        compiler_params=pltpu.CompilerParams(vmem_limit_bytes=VMEM_LIMIT),
        cost_estimate=pl.CostEstimate(flops=flops, bytes_accessed=moved, transcendentals=0),
    )(*operands)


def struct(shape, dtype=BF16):
    return jax.ShapeDtypeStruct(shape, dtype)


def ceil_to(value, step):
    return -(-value // step) * step


def sigmoid(value):
    return 1.0 / (1.0 + jnp.exp(-value))


def is_even(axis):
    return lax.rem(lax.axis_index(axis), 2) == 0


def edges_body(edges, copied):
    copied[...] = edges[...]


def has_both(axis):
    here = lax.axis_index(axis)
    return (here > 0) & (here < lax.axis_size(axis) - 1)


def spread_body(center, yeven, yodd, copied, sides, near, far):
    copied[...] = center[...]
    nx, ny, _, _ = center.shape
    even = is_even("filt")
    beyond = jnp.where(has_both("filt"), yodd[...], jnp.zeros(yodd.shape, BF16))
    sides[:, 0:1] = jnp.where(even, beyond[:, 1:2], yeven[:, 1:2])
    sides[:, 1:2] = jnp.where(even, yeven[:, 0:1], beyond[:, 0:1])
    odd = lax.rem(lax.axis_index("space"), 2)
    for out, start in ((near, (1 - odd) * (nx - 3)), (far, odd * (nx - 3))):
        rows = pl.ds(start, 3)
        out[:, 0:1] = sides[rows, 0:1]
        out[:, 1 : ny + 1] = center[rows]
        out[:, ny + 1 :] = sides[rows, 1:2]


def fill_windows(field, windows):
    count, wide_y, _, cin = field.shape
    ny = wide_y - 2
    half = windows.shape[2] // ny
    for x in range(count):
        for group in range(4):
            plane = field[x, :, pl.ds(7 + group, half, stride=2), :]
            for b in range(3):
                windows[b, x, :, group * cin : (group + 1) * cin] = (
                    plane[b : b + ny].reshape(ny * half, cin).astype(BF16)
                )


def clear_ends(field, nz):
    count, wide_y, _, cin = field.shape
    field[:, :, 0:8] = jnp.zeros((count, wide_y, 8, cin), F32)
    field[:, :, 8 + nz : 16 + nz] = jnp.zeros((count, wide_y, 8, cin), F32)


def early_rows_of(windows, start, wide, ny, keep):
    rows = windows.shape[2]
    cout = wide.shape[2] // 2
    acc = jnp.zeros((2 * rows, 2 * cout), F32)
    for ab in range(9):
        a, b = ab // 3, ab % 3
        left = windows[b, pl.ds(start + a, 2)].reshape(2 * rows, windows.shape[3])
        acc = acc + jnp.dot(left, wide[ab], preferred_element_type=F32)
    sig = sigmoid(acc)
    slope = (sig * (1.0 + acc * (1.0 - sig)) * keep).reshape(2, rows, 2 * cout)
    act = acc * sig
    act = act[:rows] + act[rows:]
    act = act[:, :cout] + act[:, cout:]
    act = act.reshape(ny // 2, 2, rows // ny, cout)
    act = (act[:, 0] + act[:, 1]) * keep
    return slope, act.reshape(rows // 2, cout).astype(BF16)


def near_body(center, sides, near, w, windows, sg, pooled, wide, field):
    nx, ny, nz, cin = center.shape
    cout = w.shape[2]
    for ab in range(9):
        for group in range(4):
            for side in range(2):
                tap = group - side
                value = w[3 * ab + tap] if 0 <= tap <= 2 else jnp.zeros((cin, cout), BF16)
                wide[
                    ab, group * cin : (group + 1) * cin, side * cout : (side + 1) * cout
                ] = value
    odd = lax.rem(lax.axis_index("space"), 2)
    clear_ends(field, nz)
    cells = slice(8, 8 + nz)
    own = pl.ds(3 * odd, nx)
    field[own, 1 : ny + 1, cells] = center[...].astype(F32)
    field[own, 0:1, cells] = sides[:, 0:1].astype(F32)
    field[own, ny + 1 :, cells] = sides[:, 1:2].astype(F32)
    field[pl.ds((1 - odd) * nx, 3), :, cells] = near[...].astype(F32)
    fill_windows(field, windows)
    for chunk in range(nx // 2):
        slope, pool = early_rows_of(windows, 1 - odd + 2 * chunk, wide, ny, 0.125)
        sg[2 * chunk : 2 * chunk + 2] = slope
        pooled[chunk] = pool


def far_body(windows, far, wide, far_windows, sg, pooled, field, held):
    _, wide_y, nz, _ = far.shape
    odd = lax.rem(lax.axis_index("space"), 2)
    clear_ends(field, nz)
    inside = jnp.where(has_both("space"), 1.0, 0.0).astype(F32)
    field[:, :, 8 : 8 + nz] = far[...].astype(F32) * inside
    fill_windows(field, far_windows)
    for b in range(3):
        held[b, pl.ds(3 * odd, 3)] = far_windows[b]
        held[b, pl.ds(3 - 3 * odd, 3)] = windows[b, pl.ds(4 * odd, 3)]
    first = jnp.where(odd == 0, inside, 1.0)
    second = jnp.where(odd == 1, inside, 1.0)
    for chunk, flag in enumerate((first, second)):
        slope, pool = early_rows_of(held, 2 * chunk, wide, wide_y - 2, 0.125 * flag)
        sg[2 * chunk : 2 * chunk + 2] = slope
        pooled[chunk] = pool


def transpose_body(windows, far_windows, turned):
    rows = windows.shape[2]
    part = turned.shape[2] // 4
    odd = lax.rem(lax.axis_index("space"), 2)
    for source, first in ((windows, 3 * (1 - odd)), (far_windows, windows.shape[1] * odd)):
        for b in range(3):
            for x in range(source.shape[1]):
                value = source[b, x].T
                spot = pl.multiple_of((first + x) * rows, rows)
                for group in range(4):
                    for side in range(2):
                        row = (2 * group + side) * part
                        turned[
                            b, side, group * part : (group + 1) * part, pl.ds(spot, rows)
                        ] = value[row : row + part]


def roll_z(value, shift):
    size = value.shape[-2]
    rolled = pltpu.roll(value, shift % size, value.ndim - 2)
    spot = lax.broadcasted_iota(jnp.int32, value.shape, value.ndim - 2)
    edge = 0 if shift == 1 else size - 1
    return jnp.where(spot == edge, 0.0, rolled)


def deep_body(parts_n, *refs):
    far, near, refs = refs[:parts_n], refs[parts_n : 2 * parts_n], refs[2 * parts_n :]
    wt, cot, block_out, grad, windows = refs[:5]
    sends = refs[5 : parts_n + 5]
    field, wide, slopes, turned, terms = refs[parts_n + 5 :]
    nx, ny, nz, filters = cot.shape
    width = wt.shape[2]
    rows = ny * nz
    py = ny // parts_n
    mine = lax.axis_index("filt")
    for ab in range(9):
        for c in range(3):
            wide[ab, :, c * width : (c + 1) * width] = wt[
                ab, c * filters : (c + 1) * filters
            ]
    field[:, 0:1] = jnp.zeros((nx + 2, 1, nz, width), F32)
    field[:, ny + 1 : ny + 2] = jnp.zeros((nx + 2, 1, nz, width), F32)
    odd = lax.rem(lax.axis_index("space"), 2)
    for parts, first in ((near, 2 * (1 - odd)), (far, 2 * odd)):
        for j in range(parts_n):
            spot = lax.bitwise_xor(mine, j) * py + 1
            field[pl.ds(first, 2), pl.ds(spot, py)] = (
                parts[-j][...].astype(F32).reshape(2, py, nz, width)
            )
    for x in range(nx + 2):
        plane = field[x]
        for c in range(3):
            moved = plane if c == 1 else roll_z(plane, 1 - c)
            for b in range(3):
                windows[b, x, :, c * width : (c + 1) * width] = (
                    moved[b : b + ny].reshape(rows, width).astype(BF16)
                )
    slopes[:, 0:1] = jnp.zeros((nx, 1, nz, filters), F32)
    slopes[:, ny + 1 :] = jnp.zeros((nx, 1, nz, filters), F32)
    for x in range(nx):
        acc = jnp.zeros((rows, filters), F32)
        for ab in range(9):
            a, b = ab // 3, ab % 3
            acc = acc + lax.dot_general(
                windows[b, x + a], wide[ab], (((1,), (1,)), ((), ())), preferred_element_type=F32
            )
        sig = sigmoid(acc)
        block_out[x] = (acc * sig).reshape(ny, nz, filters).astype(BF16)
        slope = sig * (1.0 + acc * (1.0 - sig))
        value = (cot[x].astype(F32).reshape(rows, filters) * slope).astype(BF16)
        grad[x] = value
        slopes[x, 1 : ny + 1] = value.astype(F32).reshape(ny, nz, filters)
    for x in range(nx):
        plane = slopes[x]
        plane = jnp.concatenate([roll_z(plane, -1), plane, roll_z(plane, 1)], axis=2)
        for b in range(3):
            turned[b, x] = (
                plane[2 - b : 2 - b + ny].reshape(rows, 3 * filters).astype(BF16)
            )
    for r in range(nx + 2):
        total = jnp.zeros((rows, width), F32)
        for ab in range(9):
            a, b = ab // 3, ab % 3
            if 0 <= r - a < nx:
                total = total + jnp.dot(turned[b, r - a], wt[ab], preferred_element_type=F32)
        terms[r] = total.reshape(ny, nz, width)
    for j in range(parts_n):
        spot = lax.bitwise_xor(mine, j) * py
        value = terms[:, pl.ds(spot, py)]
        sends[j][...] = value.reshape(nx + 2, py * nz, width).astype(sends[j].dtype)


def deep_grad_body(windows, grad, theirs, mine, held):
    nx, rows, filters = grad.shape
    width = windows.shape[3] // 3
    turned = grad[...].reshape(nx * rows, filters).astype(F32).T.astype(BF16)
    chips, step, _ = mine.shape
    part = filters // 2
    total = 27 * part
    if chips * step > total:
        held[:, total:] = jnp.zeros((2, chips * step - total, width), F32)
    for ab in range(9):
        a, b = ab // 3, ab % 3
        value = jnp.dot(
            turned,
            windows[b, a : a + nx].reshape(nx * rows, 3 * width),
            preferred_element_type=F32,
        )
        for c in range(3):
            spot = (3 * ab + c) * part
            for side in range(2):
                held[side, spot : spot + part] = value[
                    side * part : (side + 1) * part, c * width : (c + 1) * width
                ]
    core = lax.rem(lax.axis_index("space"), 2)
    for q in range(chips):
        theirs[q] = held[1 - core, q * step : (q + 1) * step].astype(theirs.dtype)
        mine[q] = held[core, q * step : (q + 1) * step]


def early_grad_body(nz, *refs):
    parts, (sg, far_sg, turned, deep, out, grad, held, spread) = refs[:-8], refs[-8:]
    count, rows, wide = sg.shape
    total = parts[0][...]
    for part in parts[1:]:
        total = total + part[...].astype(F32)
    px, prow, _ = total.shape
    py = prow // nz
    total = jnp.concatenate([total, total], axis=2).reshape(px, py, 1, nz, wide)
    spread[...] = jnp.broadcast_to(total, (px, py, 2, nz, wide)).reshape(px, rows, wide)
    odd = lax.rem(lax.axis_index("space"), 2)
    for source, first in ((sg, count * (1 - odd)), (far_sg, count * odd)):
        for x in range(count):
            grad[first + x] = (spread[lax.div(first, 2) + x // 2] * source[x]).astype(BF16)
    early_grad_half(1 - odd, grad, turned, deep, out, held)


def early_grad_rest_body(grad, turned, deep, out, held):
    early_grad_half(lax.rem(lax.axis_index("space"), 2), grad, turned, deep, out, held)


def early_grad_half(side, grad, turned, deep, out, held):
    ext, rows, wide = grad.shape
    width = wide // 2
    part = turned.shape[2] // 4
    right = grad[...].reshape(ext * rows, wide)
    for ab in range(9):
        a, b = ab // 3, ab % 3
        value = jnp.dot(
            turned[b, side, :, a * rows : (a + ext) * rows], right, preferred_element_type=F32
        )
        for c in range(3):
            spot = (3 * ab + c) * part
            held[spot : spot + part] = (
                value[c * part : (c + 1) * part, :width]
                + value[(c + 1) * part : (c + 2) * part, width:]
            )
    step = held.shape[0] // out.shape[0]
    for q in range(out.shape[0]):
        out[q, :step] = held[q * step : (q + 1) * step].astype(out.dtype)
        out[q, step:] = deep[q].astype(out.dtype)


def core_sum_body(first, mine, other, *outs):
    chip = lax.div(lax.axis_index("space"), 2)
    rows = slice(first, first + outs[0].shape[0])
    for j, out in enumerate(outs):
        q = lax.bitwise_xor(chip, j)
        out[...] = (mine[q, rows] + other[q, rows].astype(F32)).astype(out.dtype)


def chip_sum_body(count, *refs):
    others, outs = refs[:count], refs[count:]
    total = others[0][...]
    for ref in others[1:]:
        total = total + ref[...].astype(F32)
    row = 0
    for out in outs:
        size = out.shape[0]
        out[...] = total[row : row + size].astype(BF16)
        row += size


def filt_sum_body(count, *refs):
    parts, rest, out = refs[:count], refs[count:-1], refs[-1]
    values = [part[...].astype(F32) for part in parts]
    while len(values) > 1:
        values = [low + high for low, high in zip(values[::2], values[1::2])]
    size = values[0].shape[0]
    out[:size] = values[0].astype(BF16)
    for ref in rest:
        out[size:] = ref[...]


def stack_body(step, *refs):
    *parts, out = refs
    chips = out.shape[0]
    chip = lax.div(lax.axis_index("space"), 2)
    for j in range(chips):
        first, second = parts[j], parts[chips + j]
        q = lax.bitwise_xor(chip, j)
        cut = step - second.shape[0]
        out[q, :cut] = first[:cut]
        out[q, cut:step] = second[...]
        out[q, step:] = first[cut:]


def finish_body(own, early_scale, deep_scale, early_rows, deep_rows, pieces, *refs):
    early, deep, early_held, deep_held, sem = refs[-5:]
    core = lax.rem(lax.axis_index("space"), 2)
    side = core if own else 1 - core
    copies = []
    for out, held, first, step, scale in (
        (early, early_held, 0, early_rows, early_scale),
        (deep, deep_held, pieces.shape[1] - deep_rows, deep_rows, deep_scale),
    ):
        part = held.shape[1]
        for tap in range(27):
            row = tap * part
            while row < (tap + 1) * part:
                q, inner = row // step, row % step
                size = min(step - inner, (tap + 1) * part - row)
                spot = row - tap * part
                held[tap, spot : spot + size] = (
                    pieces[q, first + inner : first + inner + size].astype(F32) * scale
                )
                row += size
            if tap % 9 == 8:
                taps = pl.ds(tap - 8, 9)
                copy = pltpu.make_async_copy(
                    held.at[taps], out.at[taps, pl.ds(side * part, part)], sem.at[len(copies)]
                )
                copy.start()
                copies.append(copy)
    for copy in copies:
        copy.wait()


def paired(values, axis, step=1):
    count = lax.axis_size(axis)
    got = {
        j: lax.ppermute(values[j], axis, [(i, i ^ (step * j)) for i in range(count)])
        for j in reversed(range(1, len(values)))
    }
    return [values[0]] + [got[j] for j in range(1, len(values))]


def exchange(value, axis, step):
    return lax.ppermute(value, axis, [(i, i ^ step) for i in range(lax.axis_size(axis))])


def backward(values):
    return [values[0]] + values[:0:-1]


def swap(value, axis, first):
    count = lax.axis_size(axis)
    pairs = [(i, (i + 1) % count) for i in range(first, count, 2)]
    return lax.ppermute(value, axis, pairs + [(b, a) for a, b in pairs])


def shards(volume, w_early, w_deep, cotangent):
    nx, ny, nz, cin = volume.shape
    width = w_early.shape[2]
    filters = w_deep.shape[2]
    space = lax.axis_size("space")
    filt = lax.axis_size("filt")
    chips = space // 2
    half = nz // 2
    ext = nx + 6
    rows = ny * half
    edges = jnp.concatenate([volume[:, :1], volume[:, ny - 1 :]], axis=1)
    edges = call(edges_body, "edges", struct(edges.shape), (edges,), flops=1 << 32)
    yeven, yodd = swap(edges, "filt", 0), swap(edges, "filt", 1)
    rim = struct((3, ny + 2, nz, cin))
    volume, sides, near, far = call(
        spread_body,
        "spread",
        [struct(volume.shape), struct((nx, 2, nz, cin)), rim, rim],
        (volume, yeven, yodd),
        flops=HOLD,
        moved=1 << 24,
    )
    far = swap(far, "space", 1)
    near = swap(near, "space", 0)
    windows, sg, near_pooled, wide = call(
        near_body,
        "early_near",
        (
            struct((3, nx + 3, rows, 4 * cin)),
            struct((nx, rows, 2 * width), F32),
            struct((nx // 2, rows // 2, width)),
            struct((9, 4 * cin, 2 * width)),
        ),
        (volume, sides, near, w_early),
        [pltpu.VMEM((nx + 3, ny + 2, nz + 16, cin), F32)],
        flops=2 * nx * rows * 36 * cin * 2 * width,
    )
    near_parts = paired([near_pooled] * filt, "filt")
    far_windows, far_sg, pooled = call(
        far_body,
        "early_far",
        (
            struct((3, 3, rows, 4 * cin)),
            struct((nx, rows, 2 * width), F32),
            struct((nx // 2, rows // 2, width)),
        ),
        (windows, far, wide),
        [
            pltpu.VMEM((3, ny + 2, nz + 16, cin), F32),
            pltpu.VMEM((3, 6, rows, 4 * cin), BF16),
        ],
        flops=2 * nx * rows * 36 * cin * 2 * width,
    )
    parts = backward(paired([pooled] * filt, "filt"))
    near_parts = backward(near_parts)
    windows, *near_parts = lax.optimization_barrier((windows, *near_parts))
    turned = call(
        transpose_body,
        "turn_windows",
        struct((3, 2, 2 * cin, ext * rows)),
        (windows, far_windows),
        flops=1 << 30,
    )
    *parts, turned = lax.optimization_barrier((*parts, turned))
    dx, dy, dz, _ = cotangent.shape
    px = dx + 2
    prow = rows // 2
    deep = call(
        functools.partial(deep_body, filt),
        "deep_conv",
        [
            struct(cotangent.shape),
            struct((dx, dy * dz, filters)),
            struct((3, px, dy * dz, 3 * width)),
            struct((px, prow, width), F32),
        ]
        + [struct((px, prow, width))] * (filt - 1),
        (*parts, *near_parts, jnp.swapaxes(w_deep, 1, 2).reshape(9, 3 * filters, width), cotangent),
        [
            pltpu.VMEM((px, dy + 2, dz, width), F32),
            pltpu.VMEM((9, filters, 3 * width), BF16),
            pltpu.VMEM((dx, dy + 2, dz, filters), F32),
            pltpu.VMEM((3, dx, dy * dz, 3 * filters), BF16),
            pltpu.VMEM((px, dy, dz, width), F32),
        ],
        flops=4 * dx * dy * dz * 27 * width * filters,
    )
    block_out, grad, deep_windows = deep[:3]
    terms = paired(deep[3:], "filt")

    early_rows = 27 * cin // space
    deep_rows = ceil_to(-(-27 * filters // space), 16)
    deep_first, deep_second = call(
        deep_grad_body,
        "deep_grad",
        [struct((chips, deep_rows, width)), struct((chips, deep_rows, width), F32)],
        (deep_windows, grad),
        [pltpu.VMEM((2, chips * deep_rows, width), F32)],
        flops=2 * dx * dy * dz * 27 * width * filters,
    )
    piece = (chips, early_rows + deep_rows, width)
    held = pltpu.VMEM((27 * cin // 2, width), F32)
    flops = (nx + 4) * rows * 36 * cin * 2 * width
    theirs, grad = call(
        functools.partial(early_grad_body, half),
        "early_grad",
        [struct(piece), struct((nx + 4, rows, 2 * width))],
        (*backward(terms), sg, far_sg, turned, deep_first),
        [held, pltpu.VMEM((px, rows, 2 * width), F32)],
        flops=flops,
    )
    theirs = lax.ppermute(theirs, "space", [(i, i ^ 1) for i in range(space)])
    mine = call(
        early_grad_rest_body,
        "early_grad_rest",
        struct(piece, F32),
        (grad, turned, deep_second),
        [held],
        flops=flops,
    )
    cut = ceil_to(early_rows // 2, 16)
    sums = [
        call(
            functools.partial(core_sum_body, start),
            name,
            [struct((size, width), F32 if j == 0 else BF16) for j in range(chips)],
            (mine, theirs),
            flops=flops,
        )
        for name, start, size, flops in (
            ("core_sum", 0, cut, 0),
            ("core_sum_rest", cut, early_rows - cut + deep_rows, HOLD),
        )
    ]
    first = backward(paired(sums[0], "space", 2))
    *sums[1], first = lax.optimization_barrier((*sums[1], first))
    second = backward(paired(sums[1], "space", 2))
    (early,) = call(
        functools.partial(chip_sum_body, chips), "chip_sum", [struct((cut, width))], first
    )
    first = paired([early] * filt, "filt")
    *second, first[0] = lax.optimization_barrier((*second, first[0]))
    early, deep = call(
        functools.partial(chip_sum_body, chips),
        "chip_sum_rest",
        [struct((early_rows - cut, width)), struct((deep_rows, width))],
        second,
        flops=HOLD,
    )
    second = paired([early] * filt, "filt")
    *first, second[0] = lax.optimization_barrier((*first, second[0]))
    sum_body = functools.partial(filt_sum_body, filt)
    first = call(
        sum_body, "filt_sum", struct((cut + deep_rows, width)), (*first, deep), flops=HOLD
    )
    first = paired([first] * chips, "space", 2)
    *second, first[0] = lax.optimization_barrier((*second, first[0]))
    second = call(
        sum_body, "filt_sum_rest", struct((early_rows - cut, width)), second, flops=HOLD
    )
    late, first[1] = lax.optimization_barrier((second, first[1]))
    second = paired([second, late] + [second] * (chips - 2), "space", 2)

    own = call(functools.partial(stack_body, early_rows), "stack", struct(piece), (*first, *second))
    other = exchange(own, "space", 1)
    early_total = nx * ny * nz * space * filt
    deep_total = dx * dy * dz * space
    results = [struct((27, cin, width), F32), struct((27, filters, width), F32)]
    scales = (1.0 / math.sqrt(early_total), 1.0 / math.sqrt(deep_total), early_rows, deep_rows)
    scratch = [
        pltpu.VMEM((27, cin // 2, width), F32),
        pltpu.VMEM((27, filters // 2, width), F32),
        DMA((6,)),
    ]
    results = call(
        functools.partial(finish_body, True, *scales),
        "finish_own",
        results,
        (own,),
        scratch,
        outs=HBM,
    )
    grad_early, grad_deep = call(
        functools.partial(finish_body, False, *scales),
        "finish_other",
        [struct(value.shape, F32) for value in results],
        (other, *results),
        scratch,
        hbm=(1, 2),
        outs=HBM,
        alias=((1, 0), (2, 1)),
    )
    return (block_out, grad_early, jnp.swapaxes(grad_deep, 1, 2))


def solution(mesh):
    return jax.shard_map(
        shards,
        mesh=mesh,
        in_specs=(
            P("space", "filt", None, None),
            P(),
            P(None, None, "filt"),
            P("space", None, None, "filt"),
        ),
        out_specs=(P("space", None, None, "filt"), P(), P(None, None, "filt")),
        check_vma=False,
    )
```

profile of v0, /device:TPU:0, one launch (start us, length us, event | category | flops | bytes accessed | tf_op | source)
XLA Modules:
  0.0 76.5 jit_solution(17758776617070225511)
XLA Ops:
  0.6 0.7 fusion
  1.4 3.1 %collective-permute-start = (bf16[4,2,16,128]{3,2,1,0:T(8,128)(2,1)S(1)}, bf16[4,2,16,128]{3,2,1,0:T(8,128)(2,1)S(1)}, u32[]{:S(2)}, u32[]{:S(2)}) collective-permute-start(bf16[4,2,16,128]{3,2,1,0:T(8,128)(2,1)S(1)} %edges.1), channel_id=1, source_target_pairs={{0,1},{2,3},{1,0},{3,2},{4,5},{6,7},{5,4},{7,6},{8,9},{10,11},{9,8... | collective-permute-start | bytes 98312 | tf_op jit(solution)/shard_map/ppermute | solution.py:415
  4.5 2.5 %collective-permute-start.1 = (bf16[4,2,16,128]{3,2,1,0:T(8,128)(2,1)S(1)}, bf16[4,2,16,128]{3,2,1,0:T(8,128)(2,1)S(1)}, u32[]{:S(2)}, u32[]{:S(2)}) collective-permute-start(bf16[4,2,16,128]{3,2,1,0:T(8,128)(2,1)S(1)} %edges.1), channel_id=1, source_target_pairs={{1,2},{3,0},{2,1},{0,3},{5,6},{7,4},{6,5},{4,7},{9,10},{11,8},{10,... | collective-permute-start | bytes 98312 | tf_op jit(solution)/shard_map/ppermute | solution.py:415
  7.0 3.2 %collective-permute-done.1.yodd = bf16[4,2,16,128]{3,2,1,0:T(8,128)(2,1)S(1)} collective-permute-done((bf16[4,2,16,128]{3,2,1,0:T(8,128)(2,1)S(1)}, bf16[4,2,16,128]{3,2,1,0:T(8,128)(2,1)S(1)}, u32[]{:S(2)}, u32[]{:S(2)}) %collective-permute-start.1) | collective-permute-done | bytes 32800 | tf_op jit(solution)/shard_map/ppermute | solution.py:415
  10.4 2.5 %collective-permute-start.3 = (bf16[3,18,16,128]{3,2,1,0:T(8,128)(2,1)S(1)}, bf16[3,18,16,128]{3,2,1,0:T(8,128)(2,1)S(1)}, u32[]{:S(2)}, u32[]{:S(2)}) collective-permute-start(bf16[3,18,16,128]{3,2,1,0:T(8,128)(2,1)S(1)} %get-tuple-element.78), channel_id=1, source_target_pairs={{4,8},{12,16},{20,24},{28,0},{8,4},{16,12},{24,20},{0,28},{5,9},{1... | collective-permute-start | bytes 663560 | tf_op jit(solution)/shard_map/ppermute | solution.py:415
  12.9 2.2 %early_near.1 = (bf16[3,7,128,512]{3,2,1,0:T(8,128)(2,1)S(1)}, f32[4,128,256]{2,1,0:T(8,128)S(1)}, bf16[2,64,128]{2,1,0:T(8,128)(2,1)S(1)}, bf16[9,512,256]{2,1,0:T(8,128)(2,1)S(1)}) custom-call(bf16[4,16,16,128]{3,2,1,0:T(8,128)(2,1)S(1)} %get-tuple-element.74.center, bf16[4,2,16,128]{3,2,1,0:T(8,128)(2,1)S(1)} %get-tuple-element.75.sides, ...), custom_call_target="tpu_custom_call" | custom-call | flops 1207959552 | bytes 1048576 | tf_op jit(solution)/shard_map/early_near/pallas_call | solution.py:23
  15.1 2.5 %collective-permute-start.7 = (bf16[2,64,128]{2,1,0:T(8,128)(2,1)S(1)}, bf16[2,64,128]{2,1,0:T(8,128)(2,1)S(1)}, u32[]{:S(2)}, u32[]{:S(2)}) collective-permute-start(bf16[2,64,128]{2,1,0:T(8,128)(2,1)S(1)} %get-tuple-element.88.refs_4_), channel_id=1, source_target_pairs={{0,3},{1,2},{2,1},{3,0},{4,7},{5,6},{6,5},{7,4},{8,11},{9,10},{10,... | collective-permute-start | bytes 98312 | tf_op jit(solution)/shard_map/ppermute | solution.py:398
  17.7 1.9 %collective-permute-start.9 = (bf16[2,64,128]{2,1,0:T(8,128)(2,1)S(1)}, bf16[2,64,128]{2,1,0:T(8,128)(2,1)S(1)}, u32[]{:S(2)}, u32[]{:S(2)}) collective-permute-start(bf16[2,64,128]{2,1,0:T(8,128)(2,1)S(1)} %get-tuple-element.88.refs_4_), channel_id=1, source_target_pairs={{0,1},{1,0},{2,3},{3,2},{4,5},{5,4},{6,7},{7,6},{8,9},{9,8},{10,11... | collective-permute-start | bytes 98312 | tf_op jit(solution)/shard_map/ppermute | solution.py:398
  19.6 1.9 %early_far.1 = (bf16[3,3,128,512]{3,2,1,0:T(8,128)(2,1)S(1)}, f32[4,128,256]{2,1,0:T(8,128)S(1)}, bf16[2,64,128]{2,1,0:T(8,128)(2,1)S(1)}) custom-call(bf16[3,7,128,512]{3,2,1,0:T(8,128)(2,1)S(1)} %get-tuple-element.82.windows, bf16[3,18,16,128]{3,2,1,0:T(8,128)(2,1)S(1)} %collective-permute-done.3.far, bf16[9,512,256]{2,1,0:T(8,128)(2,1)S(1)} %get-tuple-element.79.wide), custom_call_target="tpu_custom_call" | custom-call | flops 1207959552 | bytes 1048576 | tf_op jit(solution)/shard_map/early_far/pallas_call | solution.py:23
  21.5 2.5 %collective-permute-start.4 = (bf16[2,64,128]{2,1,0:T(8,128)(2,1)S(1)}, bf16[2,64,128]{2,1,0:T(8,128)(2,1)S(1)}, u32[]{:S(2)}, u32[]{:S(2)}) collective-permute-start(bf16[2,64,128]{2,1,0:T(8,128)(2,1)S(1)} %get-tuple-element.84.refs_0_), channel_id=1, source_target_pairs={{0,3},{1,2},{2,1},{3,0},{4,7},{5,6},{6,5},{7,4},{8,11},{9,10},{10,... | collective-permute-start | bytes 98312 | tf_op jit(solution)/shard_map/ppermute | solution.py:398
  24.1 1.9 %collective-permute-start.6 = (bf16[2,64,128]{2,1,0:T(8,128)(2,1)S(1)}, bf16[2,64,128]{2,1,0:T(8,128)(2,1)S(1)}, u32[]{:S(2)}, u32[]{:S(2)}) collective-permute-start(bf16[2,64,128]{2,1,0:T(8,128)(2,1)S(1)} %get-tuple-element.84.refs_0_), channel_id=1, source_target_pairs={{0,1},{1,0},{2,3},{3,2},{4,5},{5,4},{6,7},{7,6},{8,9},{9,8},{10,11... | collective-permute-start | bytes 98312 | tf_op jit(solution)/shard_map/ppermute | solution.py:398
  26.0 1.1 %turn_windows.1.refs_6_.turned = bf16[3,2,256,1280]{3,2,1,0:T(8,128)(2,1)S(1)} custom-call(bf16[3,7,128,512]{3,2,1,0:T(8,128)(2,1)S(1)} %get-tuple-element.82.windows, bf16[3,3,128,512]{3,2,1,0:T(8,128)(2,1)S(1)} %get-tuple-element.83.far_windows), custom_call_target="tpu_custom_call" | custom-call | flops 1073741824 | bytes 1048576 | tf_op jit(solution)/shard_map/turn_windows/pallas_call | solution.py:23
  27.3 1.6 %collective-permute-done.5.refs_2_ = bf16[2,64,128]{2,1,0:T(8,128)(2,1)S(1)} collective-permute-done((bf16[2,64,128]{2,1,0:T(8,128)(2,1)S(1)}, bf16[2,64,128]{2,1,0:T(8,128)(2,1)S(1)}, u32[]{:S(2)}, u32[]{:S(2)}) %collective-permute-start.5) | collective-permute-done | bytes 32800 | tf_op jit(solution)/shard_map/ppermute | solution.py:398
  28.9 2.1 %deep_conv.1 = (bf16[2,32,8,64]{3,2,1,0:T(8,128)(2,1)}, bf16[2,256,64]{2,1,0:T(8,128)(2,1)S(1)}, bf16[3,4,256,384]{3,2,1,0:T(8,128)(2,1)S(1)}, f32[4,64,128]{2,1...) custom-call(bf16[2,64,128]{2,1,0:T(8,128)(2,1)S(1)} %get-tuple-eleme, ...), custom_call_target="tpu_custom_call" | custom-call | flops 452984832 | bytes 1048576 | tf_op jit(solution)/shard_map/deep_conv/pallas_call | solution.py:23
  31.0 1.9 %collective-permute-start.10 = (bf16[4,64,128]{2,1,0:T(8,128)(2,1)S(1)}, bf16[4,64,128]{2,1,0:T(8,128)(2,1)S(1)}, u32[]{:S(2)}, u32[]{:S(2)}) collective-permute-start(bf16[4,64,128]{2,1,0:T(8,128)(2,1)S(1)} %get-tuple-element.94), channel_id=1, source_target_pairs={{0,3},{1,2},{2,1},{3,0},{4,7},{5,6},{6,5},{7,4},{8,11},{9,10},{10,... | collective-permute-start | bytes 196616 | tf_op jit(solution)/shard_map/ppermute | solution.py:398
  32.9 0.7 collective-permute-start.11
  33.6 1.9 %collective-permute-start.12 = (bf16[4,64,128]{2,1,0:T(8,128)(2,1)S(1)}, bf16[4,64,128]{2,1,0:T(8,128)(2,1)S(1)}, u32[]{:S(2)}, u32[]{:S(2)}) collective-permute-start(bf16[4,64,128]{2,1,0:T(8,128)(2,1)S(1)} %get-tuple-element.96), channel_id=1, source_target_pairs={{0,1},{1,0},{2,3},{3,2},{4,5},{5,4},{6,7},{7,6},{8,9},{9,8},{10,11... | collective-permute-start | bytes 196616 | tf_op jit(solution)/shard_map/ppermute | solution.py:398
  35.5 0.7 deep_grad.1
  36.2 0.9 %collective-permute-done.10.refs_1_ = bf16[4,64,128]{2,1,0:T(8,128)(2,1)S(1)} collective-permute-done((bf16[4,64,128]{2,1,0:T(8,128)(2,1)S(1)}, bf16[4,64,128]{2,1,0:T(8,128)(2,1)S(1)}, u32[]{:S(2)}, u32[]{:S(2)}) %collective-permute-start.10) | collective-permute-done | bytes 65568 | tf_op jit(solution)/shard_map/ppermute | solution.py:398
  37.2 1.6 %collective-permute-done.11.refs_2_ = bf16[4,64,128]{2,1,0:T(8,128)(2,1)S(1)} collective-permute-done((bf16[4,64,128]{2,1,0:T(8,128)(2,1)S(1)}, bf16[4,64,128]{2,1,0:T(8,128)(2,1)S(1)}, u32[]{:S(2)}, u32[]{:S(2)}) %collective-permute-start.11) | collective-permute-done | bytes 65568 | tf_op jit(solution)/shard_map/ppermute | solution.py:398
  38.8 1.6 %early_grad.1 = (bf16[4,656,128]{2,1,0:T(8,128)(2,1)S(1)}, bf16[8,128,256]{2,1,0:T(8,128)(2,1)S(1)}) custom-call(f32[4,64,128]{2,1,0:T(8,128)S(1)} %get-tuple-element.93.refs_0_, bf16[4,64,128]{2,1,0:T(8,128)(2,1)S(1)} %collective-permute-done.10.refs_1_, bf16[4,64,128]{2,1,0:T(8,128)(2,1)S(1)} %collective-permute-done.11.refs_2_, ...), custom_call_target="tpu_custom_call" | custom-call | flops 1207959552 | bytes 1048576 | tf_op jit(solution)/shard_map/early_grad/pallas_call | solution.py:23
  40.4 1.4 %early_grad_rest.1.mine = f32[4,656,128]{2,1,0:T(8,128)S(1)} custom-call(bf16[8,128,256]{2,1,0:T(8,128)(2,1)S(1)} %get-tuple-element.103.grad, bf16[3,2,256,1280]{3,2,1,0:T(8,128)(2,1)S(1)} %turn_windows.1.refs_6_.turned, f32[4,224,128]{2,1,0:T(8,128)S(1)} %get-tuple-element.104.deep), custom_call_target="tpu_custom_call" | custom-call | flops 1207959552 | bytes 1048576 | tf_op jit(solution)/shard_map/early_grad_rest/pallas_call | solution.py:23
  41.8 0.7 collective-permute-done.13.other
  42.6 1.8 %collective-permute-start.14 = (bf16[224,128]{1,0:T(8,128)(2,1)S(1)}, bf16[224,128]{1,0:T(8,128)(2,1)S(1)}, u32[]{:S(2)}, u32[]{:S(2)}) collective-permute-start(bf16[224,128]{1,0:T(8,128)(2,1)S(1)} %get-tuple-element.111), channel_id=1, source_target_pairs={{0,24},{4,28},{8,16},{12,20},{16,8},{20,12},{24,0},{28,4},{1,25},{... | collective-permute-start | bytes 172040 | tf_op jit(solution)/shard_map/ppermute | solution.py:398
  44.4 1.0 %collective-permute-start.15 = (bf16[224,128]{1,0:T(8,128)(2,1)S(1)}, bf16[224,128]{1,0:T(8,128)(2,1)S(1)}, u32[]{:S(2)}, u32[]{:S(2)}) collective-permute-start(bf16[224,128]{1,0:T(8,128)(2,1)S(1)} %get-tuple-element.112), channel_id=1, source_target_pairs={{0,16},{4,20},{8,24},{12,28},{16,0},{20,4},{24,8},{28,12},{1,17},{... | collective-permute-start | bytes 172040 | tf_op jit(solution)/shard_map/ppermute | solution.py:398
  45.3 0.8 %collective-permute-start.16 = (bf16[224,128]{1,0:T(8,128)(2,1)S(1)}, bf16[224,128]{1,0:T(8,128)(2,1)S(1)}, u32[]{:S(2)}, u32[]{:S(2)}) collective-permute-start(bf16[224,128]{1,0:T(8,128)(2,1)S(1)} %get-tuple-element.113), channel_id=1, source_target_pairs={{0,8},{4,12},{8,0},{12,4},{16,24},{20,28},{24,16},{28,20},{1,9},{5... | collective-permute-start | bytes 172040 | tf_op jit(solution)/shard_map/ppermute | solution.py:398
  46.3 1.5 %collective-permute-done.14.refs_1_ = bf16[224,128]{1,0:T(8,128)(2,1)S(1)} collective-permute-done((bf16[224,128]{1,0:T(8,128)(2,1)S(1)}, bf16[224,128]{1,0:T(8,128)(2,1)S(1)}, u32[]{:S(2)}, u32[]{:S(2)}) %collective-permute-start.14) | collective-permute-done | bytes 57376 | tf_op jit(solution)/shard_map/ppermute | solution.py:398
  47.8 1.0 %collective-permute-done.15.refs_2_ = bf16[224,128]{1,0:T(8,128)(2,1)S(1)} collective-permute-done((bf16[224,128]{1,0:T(8,128)(2,1)S(1)}, bf16[224,128]{1,0:T(8,128)(2,1)S(1)}, u32[]{:S(2)}, u32[]{:S(2)}) %collective-permute-start.15) | collective-permute-done | bytes 57376 | tf_op jit(solution)/shard_map/ppermute | solution.py:398
  48.8 0.7 collective-permute-done.16.refs_3_
  49.5 1.3 %collective-permute-start.17 = (bf16[432,128]{1,0:T(8,128)(2,1)S(1)}, bf16[432,128]{1,0:T(8,128)(2,1)S(1)}, u32[]{:S(2)}, u32[]{:S(2)}) collective-permute-start(bf16[432,128]{1,0:T(8,128)(2,1)S(1)} %get-tuple-element.115), channel_id=1, source_target_pairs={{0,24},{4,28},{8,16},{12,20},{16,8},{20,12},{24,0},{28,4},{1,25},{... | collective-permute-start | bytes 331784 | tf_op jit(solution)/shard_map/ppermute | solution.py:398
  50.8 1.0 %collective-permute-start.18 = (bf16[432,128]{1,0:T(8,128)(2,1)S(1)}, bf16[432,128]{1,0:T(8,128)(2,1)S(1)}, u32[]{:S(2)}, u32[]{:S(2)}) collective-permute-start(bf16[432,128]{1,0:T(8,128)(2,1)S(1)} %get-tuple-element.116), channel_id=1, source_target_pairs={{0,16},{4,20},{8,24},{12,28},{16,0},{20,4},{24,8},{28,12},{1,17},{... | collective-permute-start | bytes 331784 | tf_op jit(solution)/shard_map/ppermute | solution.py:398
  51.8 1.2 %collective-permute-start.19 = (bf16[432,128]{1,0:T(8,128)(2,1)S(1)}, bf16[432,128]{1,0:T(8,128)(2,1)S(1)}, u32[]{:S(2)}, u32[]{:S(2)}) collective-permute-start(bf16[432,128]{1,0:T(8,128)(2,1)S(1)} %get-tuple-element.117), channel_id=1, source_target_pairs={{0,8},{4,12},{8,0},{12,4},{16,24},{20,28},{24,16},{28,20},{1,9},{5... | collective-permute-start | bytes 331784 | tf_op jit(solution)/shard_map/ppermute | solution.py:398
  53.0 0.6 collective-permute-start.20
  53.6 2.6 %collective-permute-start.21 = (bf16[224,128]{1,0:T(8,128)(2,1)S(1)}, bf16[224,128]{1,0:T(8,128)(2,1)S(1)}, u32[]{:S(2)}, u32[]{:S(2)}) collective-permute-start(bf16[224,128]{1,0:T(8,128)(2,1)S(1)} %chip_sum.1.refs_0_), channel_id=1, source_target_pairs={{0,2},{1,3},{2,0},{3,1},{4,6},{5,7},{6,4},{7,5},{8,10},{9,11},{10,... | collective-permute-start | bytes 172040 | tf_op jit(solution)/shard_map/ppermute | solution.py:398
  56.3 1.8 %collective-permute-start.22 = (bf16[224,128]{1,0:T(8,128)(2,1)S(1)}, bf16[224,128]{1,0:T(8,128)(2,1)S(1)}, u32[]{:S(2)}, u32[]{:S(2)}) collective-permute-start(bf16[224,128]{1,0:T(8,128)(2,1)S(1)} %chip_sum.1.refs_0_), channel_id=1, source_target_pairs={{0,3},{1,2},{2,1},{3,0},{4,7},{5,6},{6,5},{7,4},{8,11},{9,10},{10,... | collective-permute-start | bytes 172040 | tf_op jit(solution)/shard_map/ppermute | solution.py:398
  58.2 2.6 %collective-permute-start.24 = (bf16[208,128]{1,0:T(8,128)(2,1)S(1)}, bf16[208,128]{1,0:T(8,128)(2,1)S(1)}, u32[]{:S(2)}, u32[]{:S(2)}) collective-permute-start(bf16[208,128]{1,0:T(8,128)(2,1)S(1)} %get-tuple-element.135.refs_0_), channel_id=1, source_target_pairs={{0,2},{1,3},{2,0},{3,1},{4,6},{5,7},{6,4},{7,5},{8,10},{9,11},{10,... | collective-permute-start | bytes 159752 | tf_op jit(solution)/shard_map/ppermute | solution.py:398
  60.8 1.8 %collective-permute-start.25 = (bf16[208,128]{1,0:T(8,128)(2,1)S(1)}, bf16[208,128]{1,0:T(8,128)(2,1)S(1)}, u32[]{:S(2)}, u32[]{:S(2)}) collective-permute-start(bf16[208,128]{1,0:T(8,128)(2,1)S(1)} %get-tuple-element.135.refs_0_), channel_id=1, source_target_pairs={{0,3},{1,2},{2,1},{3,0},{4,7},{5,6},{6,5},{7,4},{8,11},{9,10},{10,... | collective-permute-start | bytes 159752 | tf_op jit(solution)/shard_map/ppermute | solution.py:398
  62.7 1.1 %collective-permute-start.26 = (bf16[448,128]{1,0:T(8,128)(2,1)S(1)}, bf16[448,128]{1,0:T(8,128)(2,1)S(1)}, u32[]{:S(2)}, u32[]{:S(2)}) collective-permute-start(bf16[448,128]{1,0:T(8,128)(2,1)S(1)} %filt_sum.1.refs_0_), channel_id=1, source_target_pairs={{0,8},{4,12},{8,0},{12,4},{16,24},{20,28},{24,16},{28,20},{1,9},{5... | collective-permute-start | bytes 344072 | tf_op jit(solution)/shard_map/ppermute | solution.py:398
  63.8 0.8 %collective-permute-start.27 = (bf16[448,128]{1,0:T(8,128)(2,1)S(1)}, bf16[448,128]{1,0:T(8,128)(2,1)S(1)}, u32[]{:S(2)}, u32[]{:S(2)}) collective-permute-start(bf16[448,128]{1,0:T(8,128)(2,1)S(1)} %filt_sum.1.refs_0_), channel_id=1, source_target_pairs={{0,16},{4,20},{8,24},{12,28},{16,0},{20,4},{24,8},{28,12},{1,17},{... | collective-permute-start | bytes 344072 | tf_op jit(solution)/shard_map/ppermute | solution.py:398
  64.6 1.7 %collective-permute-start.28 = (bf16[448,128]{1,0:T(8,128)(2,1)S(1)}, bf16[448,128]{1,0:T(8,128)(2,1)S(1)}, u32[]{:S(2)}, u32[]{:S(2)}) collective-permute-start(bf16[448,128]{1,0:T(8,128)(2,1)S(1)} %filt_sum.1.refs_0_), channel_id=1, source_target_pairs={{0,24},{4,28},{8,16},{12,20},{16,8},{20,12},{24,0},{28,4},{1,25},{... | collective-permute-start | bytes 344072 | tf_op jit(solution)/shard_map/ppermute | solution.py:398
  66.8 1.0 %collective-permute-start.30 = (bf16[208,128]{1,0:T(8,128)(2,1)S(1)}, bf16[208,128]{1,0:T(8,128)(2,1)S(1)}, u32[]{:S(2)}, u32[]{:S(2)}) collective-permute-start(bf16[208,128]{1,0:T(8,128)(2,1)S(1)} %filt_sum_rest.1.refs_4_), channel_id=1, source_target_pairs={{0,16},{4,20},{8,24},{12,28},{16,0},{20,4},{24,8},{28,12},{1,17},{... | collective-permute-start | bytes 159752 | tf_op jit(solution)/shard_map/ppermute | solution.py:398
  67.8 1.2 %collective-permute-start.31 = (bf16[208,128]{1,0:T(8,128)(2,1)S(1)}, bf16[208,128]{1,0:T(8,128)(2,1)S(1)}, u32[]{:S(2)}, u32[]{:S(2)}) collective-permute-start(bf16[208,128]{1,0:T(8,128)(2,1)S(1)} %filt_sum_rest.1.refs_4_), channel_id=1, source_target_pairs={{0,24},{4,28},{8,16},{12,20},{16,8},{20,12},{24,0},{28,4},{1,25},{... | collective-permute-start | bytes 159752 | tf_op jit(solution)/shard_map/ppermute | solution.py:398
  69.0 1.3 %collective-permute-start.29 = (bf16[208,128]{1,0:T(8,128)(2,1)S(1)}, bf16[208,128]{1,0:T(8,128)(2,1)S(1)}, u32[]{:S(2)}, u32[]{:S(2)}) collective-permute-start(bf16[208,128]{1,0:T(8,128)(2,1)S(1)} %filt_sum_rest.1.refs_4_), channel_id=1, source_target_pairs={{0,8},{4,12},{8,0},{12,4},{16,24},{20,28},{24,16},{28,20},{1,9},{5... | collective-permute-start | bytes 159752 | tf_op jit(solution)/shard_map/ppermute | solution.py:398
  70.4 0.6 collective-permute-done.30.refs_6_
  71.0 1.8 %collective-permute-done.31.refs_7_ = bf16[208,128]{1,0:T(8,128)(2,1)S(1)} collective-permute-done((bf16[208,128]{1,0:T(8,128)(2,1)S(1)}, bf16[208,128]{1,0:T(8,128)(2,1)S(1)}, u32[]{:S(2)}, u32[]{:S(2)}) %collective-permute-start.31) | collective-permute-done | bytes 53280 | tf_op jit(solution)/shard_map/ppermute | solution.py:398
  73.3 1.1 %finish_own.1 = (f32[27,128,128]{2,1,0:T(8,128)}, f32[27,64,128]{2,1,0:T(8,128)}) custom-call(bf16[4,656,128]{2,1,0:T(8,128)(2,1)S(1)} %stack.1.pieces), custom_call_target="tpu_custom_call" | custom-call | bytes 1048576 | tf_op jit(solution)/shard_map/finish_own/pallas_call | solution.py:23
  74.4 1.0 %collective-permute-done.32.pieces = bf16[4,656,128]{2,1,0:T(8,128)(2,1)S(1)} collective-permute-done((bf16[4,656,128]{2,1,0:T(8,128)(2,1)S(1)}, bf16[4,656,128]{2,1,0:T(8,128)(2,1)S(1)}, u32[]{:S(2)}, u32[]{:S(2)}) %collective-permute-start.32) | collective-permute-done | bytes 671776 | tf_op jit(solution)/shard_map/ppermute | solution.py:405
  75.4 1.1 %finish_other.1 = (f32[27,128,128]{2,1,0:T(8,128)}, f32[27,64,128]{2,1,0:T(8,128)}) custom-call(bf16[4,656,128]{2,1,0:T(8,128)(2,1)S(1)} %collective-permute-done.32.pieces, f32[27,128,128]{2,1,0:T(8,128)} %get-tuple-element.141.refs_0_, f32[27,64,128]{2,1,0:T(8,128)} %get-tuple-element.142.refs_1_), custom_call_target="tpu_custom_call", output_to_operand_aliasing={{0}: (1, {}), {1}: (2, {})} | custom-call | bytes 1048576 | tf_op jit(solution)/shard_map/finish_other/pallas_call | solution.py:23
  (46 shorter events, 1.9 us)
Async XLA Ops:
  1.4 8.8 %copy-start = (bf16[4,16,16,128]{3,2,1,0:T(8,128)(2,1)S(1)}, bf16[4,16,16,128]{3,2,1,0:T(8,128)(2,1)}, u32[]{:S(2)}) copy-start(bf16[4,16,16,128]{3,2,1,0:T(8,128)(2,1)} %center.1) | copy-start | bytes 786436
  1.4 11.5 %copy-start.1 = (bf16[27,128,128]{2,1,0:T(8,128)(2,1)S(1)}, bf16[27,128,128]{2,1,0:T(8,128)(2,1)}, u32[]{:S(2)}) copy-start(bf16[27,128,128]{2,1,0:T(8,128)(2,1)} %w.1) | copy-start | bytes 2654212
  1.4 5.6 %collective-permute-start = (bf16[4,2,16,128]{3,2,1,0:T(8,128)(2,1)S(1)}, bf16[4,2,16,128]{3,2,1,0:T(8,128)(2,1)S(1)}, u32[]{:S(2)}, u32[]{:S(2)}) collective-permute-start(bf16[4,2,16,128]{3,2,1,0:T(8,128)(2,1)S(1)} %edges.1), channel_id=1, source_target_pairs={{0,1},{2,3},{1,0},{3,2},{4,5},{6,7},{5,4},{7,6},{8,9},{10,11},{9,8... | collective-permute-start | bytes 98312 | tf_op jit(solution)/shard_map/ppermute | solution.py:415
  4.5 5.7 %collective-permute-start.1 = (bf16[4,2,16,128]{3,2,1,0:T(8,128)(2,1)S(1)}, bf16[4,2,16,128]{3,2,1,0:T(8,128)(2,1)S(1)}, u32[]{:S(2)}, u32[]{:S(2)}) collective-permute-start(bf16[4,2,16,128]{3,2,1,0:T(8,128)(2,1)S(1)} %edges.1), channel_id=1, source_target_pairs={{1,2},{3,0},{2,1},{0,3},{5,6},{7,4},{6,5},{4,7},{9,10},{11,8},{10,... | collective-permute-start | bytes 98312 | tf_op jit(solution)/shard_map/ppermute | solution.py:415
  10.3 2.6 %collective-permute-start.2 = (bf16[3,18,16,128]{3,2,1,0:T(8,128)(2,1)S(1)}, bf16[3,18,16,128]{3,2,1,0:T(8,128)(2,1)S(1)}, u32[]{:S(2)}, u32[]{:S(2)}) collective-permute-start(bf16[3,18,16,128]{3,2,1,0:T(8,128)(2,1)S(1)} %get-tuple-element.76), channel_id=1, source_target_pairs={{0,4},{8,12},{16,20},{24,28},{4,0},{12,8},{20,16},{28,24},{1,5},{9... | collective-permute-start | bytes 663560 | tf_op jit(solution)/shard_map/ppermute | solution.py:415
  10.4 9.2 %collective-permute-start.3 = (bf16[3,18,16,128]{3,2,1,0:T(8,128)(2,1)S(1)}, bf16[3,18,16,128]{3,2,1,0:T(8,128)(2,1)S(1)}, u32[]{:S(2)}, u32[]{:S(2)}) collective-permute-start(bf16[3,18,16,128]{3,2,1,0:T(8,128)(2,1)S(1)} %get-tuple-element.78), channel_id=1, source_target_pairs={{4,8},{12,16},{20,24},{28,0},{8,4},{16,12},{24,20},{0,28},{5,9},{1... | collective-permute-start | bytes 663560 | tf_op jit(solution)/shard_map/ppermute | solution.py:415
  15.1 9.0 %collective-permute-start.7 = (bf16[2,64,128]{2,1,0:T(8,128)(2,1)S(1)}, bf16[2,64,128]{2,1,0:T(8,128)(2,1)S(1)}, u32[]{:S(2)}, u32[]{:S(2)}) collective-permute-start(bf16[2,64,128]{2,1,0:T(8,128)(2,1)S(1)} %get-tuple-element.88.refs_4_), channel_id=1, source_target_pairs={{0,3},{1,2},{2,1},{3,0},{4,7},{5,6},{6,5},{7,4},{8,11},{9,10},{10,... | collective-permute-start | bytes 98312 | tf_op jit(solution)/shard_map/ppermute | solution.py:398
  17.7 8.3 %collective-permute-start.8 = (bf16[2,64,128]{2,1,0:T(8,128)(2,1)S(1)}, bf16[2,64,128]{2,1,0:T(8,128)(2,1)S(1)}, u32[]{:S(2)}, u32[]{:S(2)}) collective-permute-start(bf16[2,64,128]{2,1,0:T(8,128)(2,1)S(1)} %get-tuple-element.88.refs_4_), channel_id=1, source_target_pairs={{0,2},{1,3},{2,0},{3,1},{4,6},{5,7},{6,4},{7,5},{8,10},{9,11},{10,... | collective-permute-start | bytes 98312 | tf_op jit(solution)/shard_map/ppermute | solution.py:398
  17.7 8.3 %collective-permute-start.9 = (bf16[2,64,128]{2,1,0:T(8,128)(2,1)S(1)}, bf16[2,64,128]{2,1,0:T(8,128)(2,1)S(1)}, u32[]{:S(2)}, u32[]{:S(2)}) collective-permute-start(bf16[2,64,128]{2,1,0:T(8,128)(2,1)S(1)} %get-tuple-element.88.refs_4_), channel_id=1, source_target_pairs={{0,1},{1,0},{2,3},{3,2},{4,5},{5,4},{6,7},{7,6},{8,9},{9,8},{10,11... | collective-permute-start | bytes 98312 | tf_op jit(solution)/shard_map/ppermute | solution.py:398
  21.5 5.8 %collective-permute-start.4 = (bf16[2,64,128]{2,1,0:T(8,128)(2,1)S(1)}, bf16[2,64,128]{2,1,0:T(8,128)(2,1)S(1)}, u32[]{:S(2)}, u32[]{:S(2)}) collective-permute-start(bf16[2,64,128]{2,1,0:T(8,128)(2,1)S(1)} %get-tuple-element.84.refs_0_), channel_id=1, source_target_pairs={{0,3},{1,2},{2,1},{3,0},{4,7},{5,6},{6,5},{7,4},{8,11},{9,10},{10,... | collective-permute-start | bytes 98312 | tf_op jit(solution)/shard_map/ppermute | solution.py:398
  24.1 4.8 %collective-permute-start.5 = (bf16[2,64,128]{2,1,0:T(8,128)(2,1)S(1)}, bf16[2,64,128]{2,1,0:T(8,128)(2,1)S(1)}, u32[]{:S(2)}, u32[]{:S(2)}) collective-permute-start(bf16[2,64,128]{2,1,0:T(8,128)(2,1)S(1)} %get-tuple-element.84.refs_0_), channel_id=1, source_target_pairs={{0,2},{1,3},{2,0},{3,1},{4,6},{5,7},{6,4},{7,5},{8,10},{9,11},{10,... | collective-permute-start | bytes 98312 | tf_op jit(solution)/shard_map/ppermute | solution.py:398
  24.1 4.8 %collective-permute-start.6 = (bf16[2,64,128]{2,1,0:T(8,128)(2,1)S(1)}, bf16[2,64,128]{2,1,0:T(8,128)(2,1)S(1)}, u32[]{:S(2)}, u32[]{:S(2)}) collective-permute-start(bf16[2,64,128]{2,1,0:T(8,128)(2,1)S(1)} %get-tuple-element.84.refs_0_), channel_id=1, source_target_pairs={{0,1},{1,0},{2,3},{3,2},{4,5},{5,4},{6,7},{7,6},{8,9},{9,8},{10,11... | collective-permute-start | bytes 98312 | tf_op jit(solution)/shard_map/ppermute | solution.py:398
  26.0 2.9 %copy-start.2 = (bf16[27,128,64]{1,2,0:T(8,128)(2,1)S(1)}, bf16[27,128,64]{1,2,0:T(8,128)(2,1)}, u32[]{:S(2)}) copy-start(bf16[27,128,64]{1,2,0:T(8,128)(2,1)} %param.6) | copy-start | bytes 1327108
  26.0 2.9 %copy-start.3 = (bf16[2,32,8,64]{3,2,1,0:T(8,128)(2,1)S(1)}, bf16[2,32,8,64]{3,2,1,0:T(8,128)(2,1)}, u32[]{:S(2)}) copy-start(bf16[2,32,8,64]{3,2,1,0:T(8,128)(2,1)} %refs_9_.1) | copy-start | bytes 196612
  31.0 6.1 %collective-permute-start.10 = (bf16[4,64,128]{2,1,0:T(8,128)(2,1)S(1)}, bf16[4,64,128]{2,1,0:T(8,128)(2,1)S(1)}, u32[]{:S(2)}, u32[]{:S(2)}) collective-permute-start(bf16[4,64,128]{2,1,0:T(8,128)(2,1)S(1)} %get-tuple-element.94), channel_id=1, source_target_pairs={{0,3},{1,2},{2,1},{3,0},{4,7},{5,6},{6,5},{7,4},{8,11},{9,10},{10,... | collective-permute-start | bytes 196616 | tf_op jit(solution)/shard_map/ppermute | solution.py:398
  32.9 5.9 %collective-permute-start.11 = (bf16[4,64,128]{2,1,0:T(8,128)(2,1)S(1)}, bf16[4,64,128]{2,1,0:T(8,128)(2,1)S(1)}, u32[]{:S(2)}, u32[]{:S(2)}) collective-permute-start(bf16[4,64,128]{2,1,0:T(8,128)(2,1)S(1)} %get-tuple-element.95), channel_id=1, source_target_pairs={{0,2},{1,3},{2,0},{3,1},{4,6},{5,7},{6,4},{7,5},{8,10},{9,11},{10,... | collective-permute-start | bytes 196616 | tf_op jit(solution)/shard_map/ppermute | solution.py:398
  33.6 5.2 %collective-permute-start.12 = (bf16[4,64,128]{2,1,0:T(8,128)(2,1)S(1)}, bf16[4,64,128]{2,1,0:T(8,128)(2,1)S(1)}, u32[]{:S(2)}, u32[]{:S(2)}) collective-permute-start(bf16[4,64,128]{2,1,0:T(8,128)(2,1)S(1)} %get-tuple-element.96), channel_id=1, source_target_pairs={{0,1},{1,0},{2,3},{3,2},{4,5},{5,4},{6,7},{7,6},{8,9},{9,8},{10,11... | collective-permute-start | bytes 196616 | tf_op jit(solution)/shard_map/ppermute | solution.py:398
  40.4 2.2 %collective-permute-start.13 = (bf16[4,656,128]{2,1,0:T(8,128)(2,1)S(1)}, bf16[4,656,128]{2,1,0:T(8,128)(2,1)S(1)}, u32[]{:S(2)}, u32[]{:S(2)}) collective-permute-start(bf16[4,656,128]{2,1,0:T(8,128)(2,1)S(1)} %get-tuple-element.105), channel_id=1, source_target_pairs={{0,4},{4,0},{8,12},{12,8},{16,20},{20,16},{24,28},{28,24},{1,5},{5... | collective-permute-start | bytes 2015240 | tf_op jit(solution)/shard_map/ppermute | solution.py:529
  42.6 5.2 %collective-permute-start.14 = (bf16[224,128]{1,0:T(8,128)(2,1)S(1)}, bf16[224,128]{1,0:T(8,128)(2,1)S(1)}, u32[]{:S(2)}, u32[]{:S(2)}) collective-permute-start(bf16[224,128]{1,0:T(8,128)(2,1)S(1)} %get-tuple-element.111), channel_id=1, source_target_pairs={{0,24},{4,28},{8,16},{12,20},{16,8},{20,12},{24,0},{28,4},{1,25},{... | collective-permute-start | bytes 172040 | tf_op jit(solution)/shard_map/ppermute | solution.py:398
  44.4 4.4 %collective-permute-start.15 = (bf16[224,128]{1,0:T(8,128)(2,1)S(1)}, bf16[224,128]{1,0:T(8,128)(2,1)S(1)}, u32[]{:S(2)}, u32[]{:S(2)}) collective-permute-start(bf16[224,128]{1,0:T(8,128)(2,1)S(1)} %get-tuple-element.112), channel_id=1, source_target_pairs={{0,16},{4,20},{8,24},{12,28},{16,0},{20,4},{24,8},{28,12},{1,17},{... | collective-permute-start | bytes 172040 | tf_op jit(solution)/shard_map/ppermute | solution.py:398
  45.3 4.2 %collective-permute-start.16 = (bf16[224,128]{1,0:T(8,128)(2,1)S(1)}, bf16[224,128]{1,0:T(8,128)(2,1)S(1)}, u32[]{:S(2)}, u32[]{:S(2)}) collective-permute-start(bf16[224,128]{1,0:T(8,128)(2,1)S(1)} %get-tuple-element.113), channel_id=1, source_target_pairs={{0,8},{4,12},{8,0},{12,4},{16,24},{20,28},{24,16},{28,20},{1,9},{5... | collective-permute-start | bytes 172040 | tf_op jit(solution)/shard_map/ppermute | solution.py:398
  49.5 6.8 %collective-permute-start.17 = (bf16[432,128]{1,0:T(8,128)(2,1)S(1)}, bf16[432,128]{1,0:T(8,128)(2,1)S(1)}, u32[]{:S(2)}, u32[]{:S(2)}) collective-permute-start(bf16[432,128]{1,0:T(8,128)(2,1)S(1)} %get-tuple-element.115), channel_id=1, source_target_pairs={{0,24},{4,28},{8,16},{12,20},{16,8},{20,12},{24,0},{28,4},{1,25},{... | collective-permute-start | bytes 331784 | tf_op jit(solution)/shard_map/ppermute | solution.py:398
  50.8 7.3 %collective-permute-start.18 = (bf16[432,128]{1,0:T(8,128)(2,1)S(1)}, bf16[432,128]{1,0:T(8,128)(2,1)S(1)}, u32[]{:S(2)}, u32[]{:S(2)}) collective-permute-start(bf16[432,128]{1,0:T(8,128)(2,1)S(1)} %get-tuple-element.116), channel_id=1, source_target_pairs={{0,16},{4,20},{8,24},{12,28},{16,0},{20,4},{24,8},{28,12},{1,17},{... | collective-permute-start | bytes 331784 | tf_op jit(solution)/shard_map/ppermute | solution.py:398
  51.8 6.3 %collective-permute-start.19 = (bf16[432,128]{1,0:T(8,128)(2,1)S(1)}, bf16[432,128]{1,0:T(8,128)(2,1)S(1)}, u32[]{:S(2)}, u32[]{:S(2)}) collective-permute-start(bf16[432,128]{1,0:T(8,128)(2,1)S(1)} %get-tuple-element.117), channel_id=1, source_target_pairs={{0,8},{4,12},{8,0},{12,4},{16,24},{20,28},{24,16},{28,20},{1,9},{5... | collective-permute-start | bytes 331784 | tf_op jit(solution)/shard_map/ppermute | solution.py:398
  53.0 7.8 %collective-permute-start.20 = (bf16[224,128]{1,0:T(8,128)(2,1)S(1)}, bf16[224,128]{1,0:T(8,128)(2,1)S(1)}, u32[]{:S(2)}, u32[]{:S(2)}) collective-permute-start(bf16[224,128]{1,0:T(8,128)(2,1)S(1)} %chip_sum.1.refs_0_), channel_id=1, source_target_pairs={{0,1},{1,0},{2,3},{3,2},{4,5},{5,4},{6,7},{7,6},{8,9},{9,8},{10,11... | collective-permute-start | bytes 172040 | tf_op jit(solution)/shard_map/ppermute | solution.py:398
  53.6 9.0 %collective-permute-start.21 = (bf16[224,128]{1,0:T(8,128)(2,1)S(1)}, bf16[224,128]{1,0:T(8,128)(2,1)S(1)}, u32[]{:S(2)}, u32[]{:S(2)}) collective-permute-start(bf16[224,128]{1,0:T(8,128)(2,1)S(1)} %chip_sum.1.refs_0_), channel_id=1, source_target_pairs={{0,2},{1,3},{2,0},{3,1},{4,6},{5,7},{6,4},{7,5},{8,10},{9,11},{10,... | collective-permute-start | bytes 172040 | tf_op jit(solution)/shard_map/ppermute | solution.py:398
  56.3 6.3 %collective-permute-start.22 = (bf16[224,128]{1,0:T(8,128)(2,1)S(1)}, bf16[224,128]{1,0:T(8,128)(2,1)S(1)}, u32[]{:S(2)}, u32[]{:S(2)}) collective-permute-start(bf16[224,128]{1,0:T(8,128)(2,1)S(1)} %chip_sum.1.refs_0_), channel_id=1, source_target_pairs={{0,3},{1,2},{2,1},{3,0},{4,7},{5,6},{6,5},{7,4},{8,11},{9,10},{10,... | collective-permute-start | bytes 172040 | tf_op jit(solution)/shard_map/ppermute | solution.py:398
  58.2 6.4 %collective-permute-start.23 = (bf16[208,128]{1,0:T(8,128)(2,1)S(1)}, bf16[208,128]{1,0:T(8,128)(2,1)S(1)}, u32[]{:S(2)}, u32[]{:S(2)}) collective-permute-start(bf16[208,128]{1,0:T(8,128)(2,1)S(1)} %get-tuple-element.135.refs_0_), channel_id=1, source_target_pairs={{0,1},{1,0},{2,3},{3,2},{4,5},{5,4},{6,7},{7,6},{8,9},{9,8},{10,11... | collective-permute-start | bytes 159752 | tf_op jit(solution)/shard_map/ppermute | solution.py:398
  58.2 8.0 %collective-permute-start.24 = (bf16[208,128]{1,0:T(8,128)(2,1)S(1)}, bf16[208,128]{1,0:T(8,128)(2,1)S(1)}, u32[]{:S(2)}, u32[]{:S(2)}) collective-permute-start(bf16[208,128]{1,0:T(8,128)(2,1)S(1)} %get-tuple-element.135.refs_0_), channel_id=1, source_target_pairs={{0,2},{1,3},{2,0},{3,1},{4,6},{5,7},{6,4},{7,5},{8,10},{9,11},{10,... | collective-permute-start | bytes 159752 | tf_op jit(solution)/shard_map/ppermute | solution.py:398
  60.8 5.9 %collective-permute-start.25 = (bf16[208,128]{1,0:T(8,128)(2,1)S(1)}, bf16[208,128]{1,0:T(8,128)(2,1)S(1)}, u32[]{:S(2)}, u32[]{:S(2)}) collective-permute-start(bf16[208,128]{1,0:T(8,128)(2,1)S(1)} %get-tuple-element.135.refs_0_), channel_id=1, source_target_pairs={{0,3},{1,2},{2,1},{3,0},{4,7},{5,6},{6,5},{7,4},{8,11},{9,10},{10,... | collective-permute-start | bytes 159752 | tf_op jit(solution)/shard_map/ppermute | solution.py:398
  62.7 6.4 %collective-permute-start.26 = (bf16[448,128]{1,0:T(8,128)(2,1)S(1)}, bf16[448,128]{1,0:T(8,128)(2,1)S(1)}, u32[]{:S(2)}, u32[]{:S(2)}) collective-permute-start(bf16[448,128]{1,0:T(8,128)(2,1)S(1)} %filt_sum.1.refs_0_), channel_id=1, source_target_pairs={{0,8},{4,12},{8,0},{12,4},{16,24},{20,28},{24,16},{28,20},{1,9},{5... | collective-permute-start | bytes 344072 | tf_op jit(solution)/shard_map/ppermute | solution.py:398
  63.8 9.0 %collective-permute-start.27 = (bf16[448,128]{1,0:T(8,128)(2,1)S(1)}, bf16[448,128]{1,0:T(8,128)(2,1)S(1)}, u32[]{:S(2)}, u32[]{:S(2)}) collective-permute-start(bf16[448,128]{1,0:T(8,128)(2,1)S(1)} %filt_sum.1.refs_0_), channel_id=1, source_target_pairs={{0,16},{4,20},{8,24},{12,28},{16,0},{20,4},{24,8},{28,12},{1,17},{... | collective-permute-start | bytes 344072 | tf_op jit(solution)/shard_map/ppermute | solution.py:398
  64.6 8.3 %collective-permute-start.28 = (bf16[448,128]{1,0:T(8,128)(2,1)S(1)}, bf16[448,128]{1,0:T(8,128)(2,1)S(1)}, u32[]{:S(2)}, u32[]{:S(2)}) collective-permute-start(bf16[448,128]{1,0:T(8,128)(2,1)S(1)} %filt_sum.1.refs_0_), channel_id=1, source_target_pairs={{0,24},{4,28},{8,16},{12,20},{16,8},{20,12},{24,0},{28,4},{1,25},{... | collective-permute-start | bytes 344072 | tf_op jit(solution)/shard_map/ppermute | solution.py:398
  66.8 4.2 %collective-permute-start.30 = (bf16[208,128]{1,0:T(8,128)(2,1)S(1)}, bf16[208,128]{1,0:T(8,128)(2,1)S(1)}, u32[]{:S(2)}, u32[]{:S(2)}) collective-permute-start(bf16[208,128]{1,0:T(8,128)(2,1)S(1)} %filt_sum_rest.1.refs_4_), channel_id=1, source_target_pairs={{0,16},{4,20},{8,24},{12,28},{16,0},{20,4},{24,8},{28,12},{1,17},{... | collective-permute-start | bytes 159752 | tf_op jit(solution)/shard_map/ppermute | solution.py:398
  67.8 5.0 %collective-permute-start.31 = (bf16[208,128]{1,0:T(8,128)(2,1)S(1)}, bf16[208,128]{1,0:T(8,128)(2,1)S(1)}, u32[]{:S(2)}, u32[]{:S(2)}) collective-permute-start(bf16[208,128]{1,0:T(8,128)(2,1)S(1)} %filt_sum_rest.1.refs_4_), channel_id=1, source_target_pairs={{0,24},{4,28},{8,16},{12,20},{16,8},{20,12},{24,0},{28,4},{1,25},{... | collective-permute-start | bytes 159752 | tf_op jit(solution)/shard_map/ppermute | solution.py:398
  69.0 4.1 %collective-permute-start.29 = (bf16[208,128]{1,0:T(8,128)(2,1)S(1)}, bf16[208,128]{1,0:T(8,128)(2,1)S(1)}, u32[]{:S(2)}, u32[]{:S(2)}) collective-permute-start(bf16[208,128]{1,0:T(8,128)(2,1)S(1)} %filt_sum_rest.1.refs_4_), channel_id=1, source_target_pairs={{0,8},{4,12},{8,0},{12,4},{16,24},{20,28},{24,16},{28,20},{1,9},{5... | collective-permute-start | bytes 159752 | tf_op jit(solution)/shard_map/ppermute | solution.py:398
  73.2 2.2 %collective-permute-start.32 = (bf16[4,656,128]{2,1,0:T(8,128)(2,1)S(1)}, bf16[4,656,128]{2,1,0:T(8,128)(2,1)S(1)}, u32[]{:S(2)}, u32[]{:S(2)}) collective-permute-start(bf16[4,656,128]{2,1,0:T(8,128)(2,1)S(1)} %stack.1.pieces), channel_id=1, source_target_pairs={{0,4},{4,0},{8,12},{12,8},{16,20},{20,16},{24,28},{28,24},{1,5},{5... | collective-permute-start | bytes 2015240 | tf_op jit(solution)/shard_map/ppermute | solution.py:405
where the time goes:
time: 76.7 us; the launch traced here: 76.5 us
  starting transfers between devices  45.3 us (59%)
  waiting for transfers between devices  15.9 us (21%)
  Pallas kernels  13.7 us (18%)
  between operations  0.8 us (1%)
    ppermute x27, starting transfers between devices, paired(): lax.ppermute(values[j], axis, [(i, i ^ step * j) for i in range(count)])  37 us
    pallas_call x18, Pallas kernels, call(): pl.pallas_call(body, name=name, out_shape=out_shape, in_specs=[HBM if i i...  13.7 us
    ppermute x27, waiting for transfers between devices, paired(): lax.ppermute(values[j], axis, [(i, i ^ step * j) for i in range(count)])  11 us
    ppermute x4, starting transfers between devices, swap(): return lax.ppermute(value, axis, pairs + [(b, a) for a, b in pairs])  8.18 us
    ppermute x4, waiting for transfers between devices, swap(): return lax.ppermute(value, axis, pairs + [(b, a) for a, b in pairs])  3.24 us
  transfers between devices with their start and end apart: 33, of which 14 were waited for; matrix products, arithmetic and copies ran while one was open for 0% of the time, Pallas kernels for 11%

commit v1 on v0

--- a/solution.py
+++ b/solution.py
@@ -274,8 +274,8 @@
         mine[q] = held[core, q * step : (q + 1) * step]
 
 
-def early_grad_body(nz, *refs):
-    parts, (sg, far_sg, turned, deep, out, grad, held, spread) = refs[:-8], refs[-8:]
+def early_grad_body(nz, taps, *refs):
+    parts, (sg, far_sg, turned, out, grad, held, spread) = refs[:-7], refs[-7:]
     count, rows, wide = sg.shape
     total = parts[0][...]
     for part in parts[1:]:
@@ -288,25 +288,30 @@
     for source, first in ((sg, count * (1 - odd)), (far_sg, count * odd)):
         for x in range(count):
             grad[first + x] = (spread[lax.div(first, 2) + x // 2] * source[x]).astype(BF16)
-    early_grad_half(1 - odd, grad, turned, deep, out, held)
-
-
-def early_grad_rest_body(grad, turned, deep, out, held):
-    early_grad_half(lax.rem(lax.axis_index("space"), 2), grad, turned, deep, out, held)
-
-
-def early_grad_half(side, grad, turned, deep, out, held):
+    early_grad_half(1 - odd, taps, grad, turned, out, held)
+
+
+def early_grad_rest_body(own, taps, *refs):
+    grad, turned, *deep, out, held = refs
+    core = lax.rem(lax.axis_index("space"), 2)
+    early_grad_half(core if own else 1 - core, taps, grad, turned, out, held)
+    step = out.shape[1] - (deep[0].shape[1] if deep else 0)
+    for ref in deep:
+        out[:, step:] = ref[...].astype(out.dtype)
+
+
+def early_grad_half(side, taps, grad, turned, out, held):
     ext, rows, wide = grad.shape
     width = wide // 2
     part = turned.shape[2] // 4
     right = grad[...].reshape(ext * rows, wide)
-    for ab in range(9):
+    for ab in range(*taps):
         a, b = ab // 3, ab % 3
         value = jnp.dot(
             turned[b, side, :, a * rows : (a + ext) * rows], right, preferred_element_type=F32
         )
         for c in range(3):
-            spot = (3 * ab + c) * part
+            spot = (3 * (ab - taps[0]) + c) * part
             held[spot : spot + part] = (
                 value[c * part : (c + 1) * part, :width]
                 + value[(c + 1) * part : (c + 2) * part, width:]
@@ -314,15 +319,13 @@
     step = held.shape[0] // out.shape[0]
     for q in range(out.shape[0]):
         out[q, :step] = held[q * step : (q + 1) * step].astype(out.dtype)
-        out[q, step:] = deep[q].astype(out.dtype)
-
-
-def core_sum_body(first, mine, other, *outs):
+
+
+def core_sum_body(mine, other, *outs):
     chip = lax.div(lax.axis_index("space"), 2)
-    rows = slice(first, first + outs[0].shape[0])
     for j, out in enumerate(outs):
         q = lax.bitwise_xor(chip, j)
-        out[...] = (mine[q, rows] + other[q, rows].astype(F32)).astype(out.dtype)
+        out[...] = (mine[q] + other[q].astype(F32)).astype(out.dtype)
 
 
 def chip_sum_body(count, *refs):
@@ -339,7 +342,7 @@
 
 def filt_sum_body(count, *refs):
     parts, rest, out = refs[:count], refs[count:-1], refs[-1]
-    values = [part[...].astype(F32) for part in parts]
+    values = [part[...].astype(F32) for part in backward(list(parts))]
     while len(values) > 1:
         values = [low + high for low, high in zip(values[::2], values[1::2])]
     size = values[0].shape[0]
@@ -361,33 +364,37 @@
         out[q, step:] = first[cut:]
 
 
-def finish_body(own, early_scale, deep_scale, early_rows, deep_rows, pieces, *refs):
+def finish_body(own, early_scale, deep_scale, steps, cut, pieces, *refs):
     early, deep, early_held, deep_held, sem = refs[-5:]
     core = lax.rem(lax.axis_index("space"), 2)
     side = core if own else 1 - core
     copies = []
-    for out, held, first, step, scale in (
-        (early, early_held, 0, early_rows, early_scale),
-        (deep, deep_held, pieces.shape[1] - deep_rows, deep_rows, deep_scale),
+    first = 0
+    for out, held, begin, end, step, scale in (
+        (early, early_held, 0, cut, steps[0], early_scale),
+        (early, early_held, cut, 27, steps[1], early_scale),
+        (deep, deep_held, 0, 27, steps[2], deep_scale),
     ):
         part = held.shape[1]
-        for tap in range(27):
-            row = tap * part
-            while row < (tap + 1) * part:
+        for tap in range(begin, end):
+            row = (tap - begin) * part
+            stop = row + part
+            while row < stop:
                 q, inner = row // step, row % step
-                size = min(step - inner, (tap + 1) * part - row)
-                spot = row - tap * part
+                size = min(step - inner, stop - row)
+                spot = part - (stop - row)
                 held[tap, spot : spot + size] = (
                     pieces[q, first + inner : first + inner + size].astype(F32) * scale
                 )
                 row += size
-            if tap % 9 == 8:
-                taps = pl.ds(tap - 8, 9)
+            if tap % 3 == 2:
+                taps = pl.ds(tap - 2, 3)
                 copy = pltpu.make_async_copy(
                     held.at[taps], out.at[taps, pl.ds(side * part, part)], sem.at[len(copies)]
                 )
                 copy.start()
                 copies.append(copy)
+        first += step
     for copy in copies:
         copy.wait()
 
@@ -505,7 +512,6 @@
     block_out, grad, deep_windows = deep[:3]
     terms = paired(deep[3:], "filt")
 
-    early_rows = 27 * cin // space
     deep_rows = ceil_to(-(-27 * filters // space), 16)
     deep_first, deep_second = call(
         deep_grad_body,
@@ -515,79 +521,99 @@
         [pltpu.VMEM((2, chips * deep_rows, width), F32)],
         flops=2 * dx * dy * dz * 27 * width * filters,
     )
-    piece = (chips, early_rows + deep_rows, width)
-    held = pltpu.VMEM((27 * cin // 2, width), F32)
-    flops = (nx + 4) * rows * 36 * cin * 2 * width
+    cuts = ((0, 5), (5, 9))
+    steps = [3 * (end - begin) * (cin // 2) // chips for begin, end in cuts]
+    flops = 2 * (nx + 4) * rows * 18 * cin * 2 * width
+    helds = [pltpu.VMEM((step * chips, width), F32) for step in steps]
+
+    def core_sums(name, mine, theirs):
+        size = mine.shape[1:]
+        shapes = [struct(size, F32)] + [struct(size)] * (chips - 1)
+        return list(call(core_sum_body, name, shapes, (mine, theirs)))
+
     theirs, grad = call(
-        functools.partial(early_grad_body, half),
+        functools.partial(early_grad_body, half, cuts[0]),
         "early_grad",
-        [struct(piece), struct((nx + 4, rows, 2 * width))],
-        (*backward(terms), sg, far_sg, turned, deep_first),
-        [held, pltpu.VMEM((px, rows, 2 * width), F32)],
+        [struct((chips, steps[0], width)), struct((nx + 4, rows, 2 * width))],
+        (*backward(terms), sg, far_sg, turned),
+        [helds[0], pltpu.VMEM((px, rows, 2 * width), F32)],
         flops=flops,
     )
-    theirs = lax.ppermute(theirs, "space", [(i, i ^ 1) for i in range(space)])
+    theirs = exchange(theirs, "space", 1)
     mine = call(
-        early_grad_rest_body,
+        functools.partial(early_grad_rest_body, True, cuts[0]),
+        "early_grad_own",
+        struct((chips, steps[0], width), F32),
+        (grad, turned),
+        [helds[0]],
+        flops=flops,
+    )
+    sums = core_sums("core_sum", mine, theirs)
+    grad, sums[0] = lax.optimization_barrier((grad, sums[0]))
+    size = (chips, steps[1] + deep_rows, width)
+    theirs = call(
+        functools.partial(early_grad_rest_body, False, cuts[1]),
         "early_grad_rest",
-        struct(piece, F32),
+        struct(size),
+        (grad, turned, deep_first),
+        [helds[1]],
+        flops=flops,
+    )
+    theirs = exchange(theirs, "space", 1)
+    mine = call(
+        functools.partial(early_grad_rest_body, True, cuts[1]),
+        "early_grad_rest_own",
+        struct(size, F32),
         (grad, turned, deep_second),
-        [held],
+        [helds[1]],
         flops=flops,
     )
-    cut = ceil_to(early_rows // 2, 16)
-    sums = [
-        call(
-            functools.partial(core_sum_body, start),
-            name,
-            [struct((size, width), F32 if j == 0 else BF16) for j in range(chips)],
-            (mine, theirs),
-            flops=flops,
-        )
-        for name, start, size, flops in (
-            ("core_sum", 0, cut, 0),
-            ("core_sum_rest", cut, early_rows - cut + deep_rows, HOLD),
-        )
-    ]
+    sums = [sums, core_sums("core_sum_rest", mine, theirs)]
     first = backward(paired(sums[0], "space", 2))
     *sums[1], first = lax.optimization_barrier((*sums[1], first))
     second = backward(paired(sums[1], "space", 2))
     (early,) = call(
-        functools.partial(chip_sum_body, chips), "chip_sum", [struct((cut, width))], first
-    )
-    first = paired([early] * filt, "filt")
+        functools.partial(chip_sum_body, chips), "chip_sum", [struct((steps[0], width))], first
+    )
+    first = backward(paired([early] * filt, "filt"))
     *second, first[0] = lax.optimization_barrier((*second, first[0]))
     early, deep = call(
         functools.partial(chip_sum_body, chips),
         "chip_sum_rest",
-        [struct((early_rows - cut, width)), struct((deep_rows, width))],
+        [struct((steps[1], width)), struct((deep_rows, width))],
         second,
         flops=HOLD,
     )
-    second = paired([early] * filt, "filt")
+    second = backward(paired([early] * filt, "filt"))
     *first, second[0] = lax.optimization_barrier((*first, second[0]))
     sum_body = functools.partial(filt_sum_body, filt)
     first = call(
-        sum_body, "filt_sum", struct((cut + deep_rows, width)), (*first, deep), flops=HOLD
+        sum_body, "filt_sum", struct((steps[0] + deep_rows, width)), (*first, deep), flops=HOLD
     )
     first = paired([first] * chips, "space", 2)
     *second, first[0] = lax.optimization_barrier((*second, first[0]))
     second = call(
-        sum_body, "filt_sum_rest", struct((early_rows - cut, width)), second, flops=HOLD
+        sum_body, "filt_sum_rest", struct((steps[1], width)), second, flops=HOLD
     )
     late, first[1] = lax.optimization_barrier((second, first[1]))
     second = paired([second, late] + [second] * (chips - 2), "space", 2)
 
-    own = call(functools.partial(stack_body, early_rows), "stack", struct(piece), (*first, *second))
+    own = call(
+        functools.partial(stack_body, sum(steps)),
+        "stack",
+        struct((chips, sum(steps) + deep_rows, width)),
+        (*first, *second),
+    )
     other = exchange(own, "space", 1)
     early_total = nx * ny * nz * space * filt
     deep_total = dx * dy * dz * space
     results = [struct((27, cin, width), F32), struct((27, filters, width), F32)]
-    scales = (1.0 / math.sqrt(early_total), 1.0 / math.sqrt(deep_total), early_rows, deep_rows)
+    scales = (1.0 / math.sqrt(early_total), 1.0 / math.sqrt(deep_total))
+    scales += ((*steps, deep_rows), 3 * cuts[0][1])
     scratch = [
         pltpu.VMEM((27, cin // 2, width), F32),
         pltpu.VMEM((27, filters // 2, width), F32),
-        DMA((6,)),
+        DMA((18,)),
     ]
     results = call(
         functools.partial(finish_body, True, *scales),

time: 76.7 us -> 76.3 us (level)
    ppermute x27, starting transfers between devices: 37 us -> 35.8 us  [paired(): lax.ppermute(values[j], axis, [(i, i ^ step * j) for i in range(count)])]
    pallas_call x18 -> x20, Pallas kernels: 13.7 us -> 14.2 us  [call(): pl.pallas_call(body, name=name, out_shape=out_shape, in_specs=[HBM if i i...]
  transfers between devices with their start and end apart: 33 -> 34, of which waited for: 14 -> 14; matrix products, arithmetic and copies ran while one was open for 0% -> 0% of each run, Pallas kernels for 11% -> 12%
where the time goes in v1:
time: 76.3 us; the launch traced here: 76.1 us
  starting transfers between devices  44.7 us (59%)
  waiting for transfers between devices  15.5 us (20%)
  Pallas kernels  14.2 us (19%)
  between operations  0.83 us (1%)
    ppermute x27, starting transfers between devices, paired(): lax.ppermute(values[j], axis, [(i, i ^ step * j) for i in range(count)])  35.8 us
    pallas_call x20, Pallas kernels, call(): pl.pallas_call(body, name=name, out_shape=out_shape, in_specs=[HBM if i i...  14.2 us
    ppermute x27, waiting for transfers between devices, paired(): lax.ppermute(values[j], axis, [(i, i ^ step * j) for i in range(count)])  11.4 us
    ppermute x4, starting transfers between devices, swap(): return lax.ppermute(value, axis, pairs + [(b, a) for a, b in pairs])  8.18 us
    ppermute x4, waiting for transfers between devices, swap(): return lax.ppermute(value, axis, pairs + [(b, a) for a, b in pairs])  3.24 us
  transfers between devices with their start and end apart: 34, of which 14 were waited for; matrix products, arithmetic and copies ran while one was open for 0% of the time, Pallas kernels for 12%

profile of v1, /device:TPU:0, one launch (start us, length us, event | category | flops | bytes accessed | tf_op | source)
XLA Modules:
  0.0 76.1 jit_solution(6190923177625662481)
XLA Ops:
  0.6 0.7 fusion
  1.4 3.1 %collective-permute-start = (bf16[4,2,16,128]{3,2,1,0:T(8,128)(2,1)S(1)}, bf16[4,2,16,128]{3,2,1,0:T(8,128)(2,1)S(1)}, u32[]{:S(2)}, u32[]{:S(2)}) collective-permute-start(bf16[4,2,16,128]{3,2,1,0:T(8,128)(2,1)S(1)} %edges.1), channel_id=1, source_target_pairs={{0,1},{2,3},{1,0},{3,2},{4,5},{6,7},{5,4},{7,6},{8,9},{10,11},{9,8... | collective-permute-start | bytes 98312 | tf_op jit(solution)/shard_map/ppermute | solution.py:422
  4.5 2.5 %collective-permute-start.1 = (bf16[4,2,16,128]{3,2,1,0:T(8,128)(2,1)S(1)}, bf16[4,2,16,128]{3,2,1,0:T(8,128)(2,1)S(1)}, u32[]{:S(2)}, u32[]{:S(2)}) collective-permute-start(bf16[4,2,16,128]{3,2,1,0:T(8,128)(2,1)S(1)} %edges.1), channel_id=1, source_target_pairs={{1,2},{3,0},{2,1},{0,3},{5,6},{7,4},{6,5},{4,7},{9,10},{11,8},{10,... | collective-permute-start | bytes 98312 | tf_op jit(solution)/shard_map/ppermute | solution.py:422
  7.0 3.2 %collective-permute-done.1.yodd = bf16[4,2,16,128]{3,2,1,0:T(8,128)(2,1)S(1)} collective-permute-done((bf16[4,2,16,128]{3,2,1,0:T(8,128)(2,1)S(1)}, bf16[4,2,16,128]{3,2,1,0:T(8,128)(2,1)S(1)}, u32[]{:S(2)}, u32[]{:S(2)}) %collective-permute-start.1) | collective-permute-done | bytes 32800 | tf_op jit(solution)/shard_map/ppermute | solution.py:422
  10.4 2.5 %collective-permute-start.3 = (bf16[3,18,16,128]{3,2,1,0:T(8,128)(2,1)S(1)}, bf16[3,18,16,128]{3,2,1,0:T(8,128)(2,1)S(1)}, u32[]{:S(2)}, u32[]{:S(2)}) collective-permute-start(bf16[3,18,16,128]{3,2,1,0:T(8,128)(2,1)S(1)} %get-tuple-element.80), channel_id=1, source_target_pairs={{4,8},{12,16},{20,24},{28,0},{8,4},{16,12},{24,20},{0,28},{5,9},{1... | collective-permute-start | bytes 663560 | tf_op jit(solution)/shard_map/ppermute | solution.py:422
  12.9 2.2 %early_near.1 = (bf16[3,7,128,512]{3,2,1,0:T(8,128)(2,1)S(1)}, f32[4,128,256]{2,1,0:T(8,128)S(1)}, bf16[2,64,128]{2,1,0:T(8,128)(2,1)S(1)}, bf16[9,512,256]{2,1,0:T(8,128)(2,1)S(1)}) custom-call(bf16[4,16,16,128]{3,2,1,0:T(8,128)(2,1)S(1)} %get-tuple-element.76.center, bf16[4,2,16,128]{3,2,1,0:T(8,128)(2,1)S(1)} %get-tuple-element.77.sides, ...), custom_call_target="tpu_custom_call" | custom-call | flops 1207959552 | bytes 1048576 | tf_op jit(solution)/shard_map/early_near/pallas_call | solution.py:23
  15.1 2.5 %collective-permute-start.7 = (bf16[2,64,128]{2,1,0:T(8,128)(2,1)S(1)}, bf16[2,64,128]{2,1,0:T(8,128)(2,1)S(1)}, u32[]{:S(2)}, u32[]{:S(2)}) collective-permute-start(bf16[2,64,128]{2,1,0:T(8,128)(2,1)S(1)} %get-tuple-element.90.refs_4_), channel_id=1, source_target_pairs={{0,3},{1,2},{2,1},{3,0},{4,7},{5,6},{6,5},{7,4},{8,11},{9,10},{10,... | collective-permute-start | bytes 98312 | tf_op jit(solution)/shard_map/ppermute | solution.py:405
  17.7 1.9 %collective-permute-start.9 = (bf16[2,64,128]{2,1,0:T(8,128)(2,1)S(1)}, bf16[2,64,128]{2,1,0:T(8,128)(2,1)S(1)}, u32[]{:S(2)}, u32[]{:S(2)}) collective-permute-start(bf16[2,64,128]{2,1,0:T(8,128)(2,1)S(1)} %get-tuple-element.90.refs_4_), channel_id=1, source_target_pairs={{0,1},{1,0},{2,3},{3,2},{4,5},{5,4},{6,7},{7,6},{8,9},{9,8},{10,11... | collective-permute-start | bytes 98312 | tf_op jit(solution)/shard_map/ppermute | solution.py:405
  19.6 1.9 %early_far.1 = (bf16[3,3,128,512]{3,2,1,0:T(8,128)(2,1)S(1)}, f32[4,128,256]{2,1,0:T(8,128)S(1)}, bf16[2,64,128]{2,1,0:T(8,128)(2,1)S(1)}) custom-call(bf16[3,7,128,512]{3,2,1,0:T(8,128)(2,1)S(1)} %get-tuple-element.84.windows, bf16[3,18,16,128]{3,2,1,0:T(8,128)(2,1)S(1)} %collective-permute-done.3.far, bf16[9,512,256]{2,1,0:T(8,128)(2,1)S(1)} %get-tuple-element.81.wide), custom_call_target="tpu_custom_call" | custom-call | flops 1207959552 | bytes 1048576 | tf_op jit(solution)/shard_map/early_far/pallas_call | solution.py:23
  21.5 2.5 %collective-permute-start.4 = (bf16[2,64,128]{2,1,0:T(8,128)(2,1)S(1)}, bf16[2,64,128]{2,1,0:T(8,128)(2,1)S(1)}, u32[]{:S(2)}, u32[]{:S(2)}) collective-permute-start(bf16[2,64,128]{2,1,0:T(8,128)(2,1)S(1)} %get-tuple-element.86.refs_0_), channel_id=1, source_target_pairs={{0,3},{1,2},{2,1},{3,0},{4,7},{5,6},{6,5},{7,4},{8,11},{9,10},{10,... | collective-permute-start | bytes 98312 | tf_op jit(solution)/shard_map/ppermute | solution.py:405
  24.1 1.9 %collective-permute-start.6 = (bf16[2,64,128]{2,1,0:T(8,128)(2,1)S(1)}, bf16[2,64,128]{2,1,0:T(8,128)(2,1)S(1)}, u32[]{:S(2)}, u32[]{:S(2)}) collective-permute-start(bf16[2,64,128]{2,1,0:T(8,128)(2,1)S(1)} %get-tuple-element.86.refs_0_), channel_id=1, source_target_pairs={{0,1},{1,0},{2,3},{3,2},{4,5},{5,4},{6,7},{7,6},{8,9},{9,8},{10,11... | collective-permute-start | bytes 98312 | tf_op jit(solution)/shard_map/ppermute | solution.py:405
  26.0 1.1 %turn_windows.1.refs_6_.refs_1_ = bf16[3,2,256,1280]{3,2,1,0:T(8,128)(2,1)S(1)} custom-call(bf16[3,7,128,512]{3,2,1,0:T(8,128)(2,1)S(1)} %get-tuple-element.84.windows, bf16[3,3,128,512]{3,2,1,0:T(8,128)(2,1)S(1)} %get-tuple-element.85.far_windows), custom_call_target="tpu_custom_call" | custom-call | flops 1073741824 | bytes 1048576 | tf_op jit(solution)/shard_map/turn_windows/pallas_call | solution.py:23
  27.3 1.6 %collective-permute-done.5.refs_2_ = bf16[2,64,128]{2,1,0:T(8,128)(2,1)S(1)} collective-permute-done((bf16[2,64,128]{2,1,0:T(8,128)(2,1)S(1)}, bf16[2,64,128]{2,1,0:T(8,128)(2,1)S(1)}, u32[]{:S(2)}, u32[]{:S(2)}) %collective-permute-start.5) | collective-permute-done | bytes 32800 | tf_op jit(solution)/shard_map/ppermute | solution.py:405
  28.9 2.1 %deep_conv.1 = (bf16[2,32,8,64]{3,2,1,0:T(8,128)(2,1)}, bf16[2,256,64]{2,1,0:T(8,128)(2,1)S(1)}, bf16[3,4,256,384]{3,2,1,0:T(8,128)(2,1)S(1)}, f32[4,64,128]{2,1...) custom-call(bf16[2,64,128]{2,1,0:T(8,128)(2,1)S(1)} %get-tuple-eleme, ...), custom_call_target="tpu_custom_call" | custom-call | flops 452984832 | bytes 1048576 | tf_op jit(solution)/shard_map/deep_conv/pallas_call | solution.py:23
  31.0 1.9 %collective-permute-start.10 = (bf16[4,64,128]{2,1,0:T(8,128)(2,1)S(1)}, bf16[4,64,128]{2,1,0:T(8,128)(2,1)S(1)}, u32[]{:S(2)}, u32[]{:S(2)}) collective-permute-start(bf16[4,64,128]{2,1,0:T(8,128)(2,1)S(1)} %get-tuple-element.96), channel_id=1, source_target_pairs={{0,3},{1,2},{2,1},{3,0},{4,7},{5,6},{6,5},{7,4},{8,11},{9,10},{10,... | collective-permute-start | bytes 196616 | tf_op jit(solution)/shard_map/ppermute | solution.py:405
  32.9 0.7 collective-permute-start.11
  33.6 1.9 %collective-permute-start.12 = (bf16[4,64,128]{2,1,0:T(8,128)(2,1)S(1)}, bf16[4,64,128]{2,1,0:T(8,128)(2,1)S(1)}, u32[]{:S(2)}, u32[]{:S(2)}) collective-permute-start(bf16[4,64,128]{2,1,0:T(8,128)(2,1)S(1)} %get-tuple-element.98), channel_id=1, source_target_pairs={{0,1},{1,0},{2,3},{3,2},{4,5},{5,4},{6,7},{7,6},{8,9},{9,8},{10,11... | collective-permute-start | bytes 196616 | tf_op jit(solution)/shard_map/ppermute | solution.py:405
  35.5 1.7 %collective-permute-done.10.refs_1_ = bf16[4,64,128]{2,1,0:T(8,128)(2,1)S(1)} collective-permute-done((bf16[4,64,128]{2,1,0:T(8,128)(2,1)S(1)}, bf16[4,64,128]{2,1,0:T(8,128)(2,1)S(1)}, u32[]{:S(2)}, u32[]{:S(2)}) %collective-permute-start.10) | collective-permute-done | bytes 65568 | tf_op jit(solution)/shard_map/ppermute | solution.py:405
  37.2 1.6 %collective-permute-done.11.refs_2_ = bf16[4,64,128]{2,1,0:T(8,128)(2,1)S(1)} collective-permute-done((bf16[4,64,128]{2,1,0:T(8,128)(2,1)S(1)}, bf16[4,64,128]{2,1,0:T(8,128)(2,1)S(1)}, u32[]{:S(2)}, u32[]{:S(2)}) %collective-permute-start.11) | collective-permute-done | bytes 65568 | tf_op jit(solution)/shard_map/ppermute | solution.py:405
  38.8 1.0 %early_grad.1 = (bf16[4,240,128]{2,1,0:T(8,128)(2,1)S(1)}, bf16[8,128,256]{2,1,0:T(8,128)(2,1)S(1)}) custom-call(f32[4,64,128]{2,1,0:T(8,128)S(1)} %get-tuple-element.95.refs_0_, bf16[4,64,128]{2,1,0:T(8,128)(2,1)S(1)} %collective-permute-done.10.refs_1_, bf16[4,64,128]{2,1,0:T(8,128)(2,1)S(1)} %collective-permute-done.11.refs_2_, ...), custom_call_target="tpu_custom_call" | custom-call | flops 1207959552 | bytes 1048576 | tf_op jit(solution)/shard_map/early_grad/pallas_call | solution.py:23
  39.9 0.7 deep_grad.1
  40.6 0.8 %early_grad_own.1.mine = f32[4,240,128]{2,1,0:T(8,128)S(1)} custom-call(bf16[8,128,256]{2,1,0:T(8,128)(2,1)S(1)} %get-tuple-element.105.refs_0_, bf16[3,2,256,1280]{3,2,1,0:T(8,128)(2,1)S(1)} %turn_windows.1.refs_6_.refs_1_), custom_call_target="tpu_custom_call" | custom-call | flops 1207959552 | bytes 1048576 | tf_op jit(solution)/shard_map/early_grad_own/pallas_call | solution.py:23
  41.6 0.7 early_grad_rest.1
  42.9 1.7 %collective-permute-start.15 = (bf16[240,128]{1,0:T(8,128)(2,1)S(1)}, bf16[240,128]{1,0:T(8,128)(2,1)S(1)}, u32[]{:S(2)}, u32[]{:S(2)}) collective-permute-start(bf16[240,128]{1,0:T(8,128)(2,1)S(1)} %get-tuple-element.115), channel_id=1, source_target_pairs={{0,24},{4,28},{8,16},{12,20},{16,8},{20,12},{24,0},{28,4},{1,25},{... | collective-permute-start | bytes 184328 | tf_op jit(solution)/shard_map/ppermute | solution.py:405
  44.5 1.0 %collective-permute-start.16 = (bf16[240,128]{1,0:T(8,128)(2,1)S(1)}, bf16[240,128]{1,0:T(8,128)(2,1)S(1)}, u32[]{:S(2)}, u32[]{:S(2)}) collective-permute-start(bf16[240,128]{1,0:T(8,128)(2,1)S(1)} %get-tuple-element.116), channel_id=1, source_target_pairs={{0,16},{4,20},{8,24},{12,28},{16,0},{20,4},{24,8},{28,12},{1,17},{... | collective-permute-start | bytes 184328 | tf_op jit(solution)/shard_map/ppermute | solution.py:405
  45.5 0.8 %collective-permute-start.17 = (bf16[240,128]{1,0:T(8,128)(2,1)S(1)}, bf16[240,128]{1,0:T(8,128)(2,1)S(1)}, u32[]{:S(2)}, u32[]{:S(2)}) collective-permute-start(bf16[240,128]{1,0:T(8,128)(2,1)S(1)} %get-tuple-element.117), channel_id=1, source_target_pairs={{0,8},{4,12},{8,0},{12,4},{16,24},{20,28},{24,16},{28,20},{1,9},{5... | collective-permute-start | bytes 184328 | tf_op jit(solution)/shard_map/ppermute | solution.py:405
  46.3 0.7 early_grad_rest_own.1.mine
  47.2 0.9 %collective-permute-done.15.refs_1_ = bf16[240,128]{1,0:T(8,128)(2,1)S(1)} collective-permute-done((bf16[240,128]{1,0:T(8,128)(2,1)S(1)}, bf16[240,128]{1,0:T(8,128)(2,1)S(1)}, u32[]{:S(2)}, u32[]{:S(2)}) %collective-permute-start.15) | collective-permute-done | bytes 61472 | tf_op jit(solution)/shard_map/ppermute | solution.py:405
  48.0 1.0 %collective-permute-done.16.refs_2_ = bf16[240,128]{1,0:T(8,128)(2,1)S(1)} collective-permute-done((bf16[240,128]{1,0:T(8,128)(2,1)S(1)}, bf16[240,128]{1,0:T(8,128)(2,1)S(1)}, u32[]{:S(2)}, u32[]{:S(2)}) %collective-permute-start.16) | collective-permute-done | bytes 61472 | tf_op jit(solution)/shard_map/ppermute | solution.py:405
  49.1 0.7 collective-permute-done.17.refs_3_
  49.7 1.3 %collective-permute-start.18 = (bf16[416,128]{1,0:T(8,128)(2,1)S(1)}, bf16[416,128]{1,0:T(8,128)(2,1)S(1)}, u32[]{:S(2)}, u32[]{:S(2)}) collective-permute-start(bf16[416,128]{1,0:T(8,128)(2,1)S(1)} %get-tuple-element.119), channel_id=1, source_target_pairs={{0,24},{4,28},{8,16},{12,20},{16,8},{20,12},{24,0},{28,4},{1,25},{... | collective-permute-start | bytes 319496 | tf_op jit(solution)/shard_map/ppermute | solution.py:405
  51.1 0.9 %collective-permute-start.19 = (bf16[416,128]{1,0:T(8,128)(2,1)S(1)}, bf16[416,128]{1,0:T(8,128)(2,1)S(1)}, u32[]{:S(2)}, u32[]{:S(2)}) collective-permute-start(bf16[416,128]{1,0:T(8,128)(2,1)S(1)} %get-tuple-element.120), channel_id=1, source_target_pairs={{0,16},{4,20},{8,24},{12,28},{16,0},{20,4},{24,8},{28,12},{1,17},{... | collective-permute-start | bytes 319496 | tf_op jit(solution)/shard_map/ppermute | solution.py:405
  52.0 1.2 %collective-permute-start.20 = (bf16[416,128]{1,0:T(8,128)(2,1)S(1)}, bf16[416,128]{1,0:T(8,128)(2,1)S(1)}, u32[]{:S(2)}, u32[]{:S(2)}) collective-permute-start(bf16[416,128]{1,0:T(8,128)(2,1)S(1)} %get-tuple-element.121), channel_id=1, source_target_pairs={{0,8},{4,12},{8,0},{12,4},{16,24},{20,28},{24,16},{28,20},{1,9},{5... | collective-permute-start | bytes 319496 | tf_op jit(solution)/shard_map/ppermute | solution.py:405
  53.3 2.7 %collective-permute-start.21 = (bf16[240,128]{1,0:T(8,128)(2,1)S(1)}, bf16[240,128]{1,0:T(8,128)(2,1)S(1)}, u32[]{:S(2)}, u32[]{:S(2)}) collective-permute-start(bf16[240,128]{1,0:T(8,128)(2,1)S(1)} %chip_sum.1.refs_0_), channel_id=1, source_target_pairs={{0,3},{1,2},{2,1},{3,0},{4,7},{5,6},{6,5},{7,4},{8,11},{9,10},{10,... | collective-permute-start | bytes 184328 | tf_op jit(solution)/shard_map/ppermute | solution.py:405
  56.5 1.2 %collective-permute-start.23 = (bf16[240,128]{1,0:T(8,128)(2,1)S(1)}, bf16[240,128]{1,0:T(8,128)(2,1)S(1)}, u32[]{:S(2)}, u32[]{:S(2)}) collective-permute-start(bf16[240,128]{1,0:T(8,128)(2,1)S(1)} %chip_sum.1.refs_0_), channel_id=1, source_target_pairs={{0,1},{1,0},{2,3},{3,2},{4,5},{5,4},{6,7},{7,6},{8,9},{9,8},{10,11... | collective-permute-start | bytes 184328 | tf_op jit(solution)/shard_map/ppermute | solution.py:405
  57.8 2.7 %collective-permute-start.24 = (bf16[192,128]{1,0:T(8,128)(2,1)S(1)}, bf16[192,128]{1,0:T(8,128)(2,1)S(1)}, u32[]{:S(2)}, u32[]{:S(2)}) collective-permute-start(bf16[192,128]{1,0:T(8,128)(2,1)S(1)} %get-tuple-element.139.refs_0_), channel_id=1, source_target_pairs={{0,3},{1,2},{2,1},{3,0},{4,7},{5,6},{6,5},{7,4},{8,11},{9,10},{10,... | collective-permute-start | bytes 147464 | tf_op jit(solution)/shard_map/ppermute | solution.py:405
  60.5 1.7 %collective-permute-start.26 = (bf16[192,128]{1,0:T(8,128)(2,1)S(1)}, bf16[192,128]{1,0:T(8,128)(2,1)S(1)}, u32[]{:S(2)}, u32[]{:S(2)}) collective-permute-start(bf16[192,128]{1,0:T(8,128)(2,1)S(1)} %get-tuple-element.139.refs_0_), channel_id=1, source_target_pairs={{0,1},{1,0},{2,3},{3,2},{4,5},{5,4},{6,7},{7,6},{8,9},{9,8},{10,11... | collective-permute-start | bytes 147464 | tf_op jit(solution)/shard_map/ppermute | solution.py:405
  62.7 0.8 %collective-permute-start.27 = (bf16[464,128]{1,0:T(8,128)(2,1)S(1)}, bf16[464,128]{1,0:T(8,128)(2,1)S(1)}, u32[]{:S(2)}, u32[]{:S(2)}) collective-permute-start(bf16[464,128]{1,0:T(8,128)(2,1)S(1)} %filt_sum.1.refs_0_), channel_id=1, source_target_pairs={{0,8},{4,12},{8,0},{12,4},{16,24},{20,28},{24,16},{28,20},{1,9},{5... | collective-permute-start | bytes 356360 | tf_op jit(solution)/shard_map/ppermute | solution.py:405
  63.5 0.8 %collective-permute-start.28 = (bf16[464,128]{1,0:T(8,128)(2,1)S(1)}, bf16[464,128]{1,0:T(8,128)(2,1)S(1)}, u32[]{:S(2)}, u32[]{:S(2)}) collective-permute-start(bf16[464,128]{1,0:T(8,128)(2,1)S(1)} %filt_sum.1.refs_0_), channel_id=1, source_target_pairs={{0,16},{4,20},{8,24},{12,28},{16,0},{20,4},{24,8},{28,12},{1,17},{... | collective-permute-start | bytes 356360 | tf_op jit(solution)/shard_map/ppermute | solution.py:405
  64.3 2.0 %collective-permute-start.29 = (bf16[464,128]{1,0:T(8,128)(2,1)S(1)}, bf16[464,128]{1,0:T(8,128)(2,1)S(1)}, u32[]{:S(2)}, u32[]{:S(2)}) collective-permute-start(bf16[464,128]{1,0:T(8,128)(2,1)S(1)} %filt_sum.1.refs_0_), channel_id=1, source_target_pairs={{0,24},{4,28},{8,16},{12,20},{16,8},{20,12},{24,0},{28,4},{1,25},{... | collective-permute-start | bytes 356360 | tf_op jit(solution)/shard_map/ppermute | solution.py:405
  66.3 1.0 %collective-permute-start.31 = (bf16[192,128]{1,0:T(8,128)(2,1)S(1)}, bf16[192,128]{1,0:T(8,128)(2,1)S(1)}, u32[]{:S(2)}, u32[]{:S(2)}) collective-permute-start(bf16[192,128]{1,0:T(8,128)(2,1)S(1)} %filt_sum_rest.1.refs_4_), channel_id=1, source_target_pairs={{0,16},{4,20},{8,24},{12,28},{16,0},{20,4},{24,8},{28,12},{1,17},{... | collective-permute-start | bytes 147464 | tf_op jit(solution)/shard_map/ppermute | solution.py:405
  67.3 1.3 %collective-permute-start.32 = (bf16[192,128]{1,0:T(8,128)(2,1)S(1)}, bf16[192,128]{1,0:T(8,128)(2,1)S(1)}, u32[]{:S(2)}, u32[]{:S(2)}) collective-permute-start(bf16[192,128]{1,0:T(8,128)(2,1)S(1)} %filt_sum_rest.1.refs_4_), channel_id=1, source_target_pairs={{0,24},{4,28},{8,16},{12,20},{16,8},{20,12},{24,0},{28,4},{1,25},{... | collective-permute-start | bytes 147464 | tf_op jit(solution)/shard_map/ppermute | solution.py:405
  68.6 1.3 %collective-permute-start.30 = (bf16[192,128]{1,0:T(8,128)(2,1)S(1)}, bf16[192,128]{1,0:T(8,128)(2,1)S(1)}, u32[]{:S(2)}, u32[]{:S(2)}) collective-permute-start(bf16[192,128]{1,0:T(8,128)(2,1)S(1)} %filt_sum_rest.1.refs_4_), channel_id=1, source_target_pairs={{0,8},{4,12},{8,0},{12,4},{16,24},{20,28},{24,16},{28,20},{1,9},{5... | collective-permute-start | bytes 147464 | tf_op jit(solution)/shard_map/ppermute | solution.py:405
  69.9 1.0 %collective-permute-done.31.refs_6_ = bf16[192,128]{1,0:T(8,128)(2,1)S(1)} collective-permute-done((bf16[192,128]{1,0:T(8,128)(2,1)S(1)}, bf16[192,128]{1,0:T(8,128)(2,1)S(1)}, u32[]{:S(2)}, u32[]{:S(2)}) %collective-permute-start.31) | collective-permute-done | bytes 49184 | tf_op jit(solution)/shard_map/ppermute | solution.py:405
  70.9 1.4 %collective-permute-done.32.refs_7_ = bf16[192,128]{1,0:T(8,128)(2,1)S(1)} collective-permute-done((bf16[192,128]{1,0:T(8,128)(2,1)S(1)}, bf16[192,128]{1,0:T(8,128)(2,1)S(1)}, u32[]{:S(2)}, u32[]{:S(2)}) %collective-permute-start.32) | collective-permute-done | bytes 49184 | tf_op jit(solution)/shard_map/ppermute | solution.py:405
  72.8 1.2 %finish_own.1 = (f32[27,128,128]{2,1,0:T(8,128)}, f32[27,64,128]{2,1,0:T(8,128)}) custom-call(bf16[4,656,128]{2,1,0:T(8,128)(2,1)S(1)} %stack.1.pieces), custom_call_target="tpu_custom_call" | custom-call | bytes 1048576 | tf_op jit(solution)/shard_map/finish_own/pallas_call | solution.py:23
  74.0 0.9 %collective-permute-done.33.pieces = bf16[4,656,128]{2,1,0:T(8,128)(2,1)S(1)} collective-permute-done((bf16[4,656,128]{2,1,0:T(8,128)(2,1)S(1)}, bf16[4,656,128]{2,1,0:T(8,128)(2,1)S(1)}, u32[]{:S(2)}, u32[]{:S(2)}) %collective-permute-start.33) | collective-permute-done | bytes 671776 | tf_op jit(solution)/shard_map/ppermute | solution.py:412
  74.9 1.2 %finish_other.1 = (f32[27,128,128]{2,1,0:T(8,128)}, f32[27,64,128]{2,1,0:T(8,128)}) custom-call(bf16[4,656,128]{2,1,0:T(8,128)(2,1)S(1)} %collective-permute-done.33.pieces, f32[27,128,128]{2,1,0:T(8,128)} %get-tuple-element.145.refs_0_, f32[27,64,128]{2,1,0:T(8,128)} %get-tuple-element.146.refs_1_), custom_call_target="tpu_custom_call", output_to_operand_aliasing={{0}: (1, {}), {1}: (2, {})} | custom-call | bytes 1048576 | tf_op jit(solution)/shard_map/finish_other/pallas_call | solution.py:23
  (50 shorter events, 2.9 us)
Async XLA Ops:
  1.4 8.8 %copy-start = (bf16[4,16,16,128]{3,2,1,0:T(8,128)(2,1)S(1)}, bf16[4,16,16,128]{3,2,1,0:T(8,128)(2,1)}, u32[]{:S(2)}) copy-start(bf16[4,16,16,128]{3,2,1,0:T(8,128)(2,1)} %center.1) | copy-start | bytes 786436
  1.4 11.5 %copy-start.1 = (bf16[27,128,128]{2,1,0:T(8,128)(2,1)S(1)}, bf16[27,128,128]{2,1,0:T(8,128)(2,1)}, u32[]{:S(2)}) copy-start(bf16[27,128,128]{2,1,0:T(8,128)(2,1)} %w.1) | copy-start | bytes 2654212
  1.4 5.6 %collective-permute-start = (bf16[4,2,16,128]{3,2,1,0:T(8,128)(2,1)S(1)}, bf16[4,2,16,128]{3,2,1,0:T(8,128)(2,1)S(1)}, u32[]{:S(2)}, u32[]{:S(2)}) collective-permute-start(bf16[4,2,16,128]{3,2,1,0:T(8,128)(2,1)S(1)} %edges.1), channel_id=1, source_target_pairs={{0,1},{2,3},{1,0},{3,2},{4,5},{6,7},{5,4},{7,6},{8,9},{10,11},{9,8... | collective-permute-start | bytes 98312 | tf_op jit(solution)/shard_map/ppermute | solution.py:422
  4.5 5.7 %collective-permute-start.1 = (bf16[4,2,16,128]{3,2,1,0:T(8,128)(2,1)S(1)}, bf16[4,2,16,128]{3,2,1,0:T(8,128)(2,1)S(1)}, u32[]{:S(2)}, u32[]{:S(2)}) collective-permute-start(bf16[4,2,16,128]{3,2,1,0:T(8,128)(2,1)S(1)} %edges.1), channel_id=1, source_target_pairs={{1,2},{3,0},{2,1},{0,3},{5,6},{7,4},{6,5},{4,7},{9,10},{11,8},{10,... | collective-permute-start | bytes 98312 | tf_op jit(solution)/shard_map/ppermute | solution.py:422
  10.3 2.6 %collective-permute-start.2 = (bf16[3,18,16,128]{3,2,1,0:T(8,128)(2,1)S(1)}, bf16[3,18,16,128]{3,2,1,0:T(8,128)(2,1)S(1)}, u32[]{:S(2)}, u32[]{:S(2)}) collective-permute-start(bf16[3,18,16,128]{3,2,1,0:T(8,128)(2,1)S(1)} %get-tuple-element.78), channel_id=1, source_target_pairs={{0,4},{8,12},{16,20},{24,28},{4,0},{12,8},{20,16},{28,24},{1,5},{9... | collective-permute-start | bytes 663560 | tf_op jit(solution)/shard_map/ppermute | solution.py:422
  10.4 9.2 %collective-permute-start.3 = (bf16[3,18,16,128]{3,2,1,0:T(8,128)(2,1)S(1)}, bf16[3,18,16,128]{3,2,1,0:T(8,128)(2,1)S(1)}, u32[]{:S(2)}, u32[]{:S(2)}) collective-permute-start(bf16[3,18,16,128]{3,2,1,0:T(8,128)(2,1)S(1)} %get-tuple-element.80), channel_id=1, source_target_pairs={{4,8},{12,16},{20,24},{28,0},{8,4},{16,12},{24,20},{0,28},{5,9},{1... | collective-permute-start | bytes 663560 | tf_op jit(solution)/shard_map/ppermute | solution.py:422
  15.1 9.0 %collective-permute-start.7 = (bf16[2,64,128]{2,1,0:T(8,128)(2,1)S(1)}, bf16[2,64,128]{2,1,0:T(8,128)(2,1)S(1)}, u32[]{:S(2)}, u32[]{:S(2)}) collective-permute-start(bf16[2,64,128]{2,1,0:T(8,128)(2,1)S(1)} %get-tuple-element.90.refs_4_), channel_id=1, source_target_pairs={{0,3},{1,2},{2,1},{3,0},{4,7},{5,6},{6,5},{7,4},{8,11},{9,10},{10,... | collective-permute-start | bytes 98312 | tf_op jit(solution)/shard_map/ppermute | solution.py:405
  17.7 8.3 %collective-permute-start.8 = (bf16[2,64,128]{2,1,0:T(8,128)(2,1)S(1)}, bf16[2,64,128]{2,1,0:T(8,128)(2,1)S(1)}, u32[]{:S(2)}, u32[]{:S(2)}) collective-permute-start(bf16[2,64,128]{2,1,0:T(8,128)(2,1)S(1)} %get-tuple-element.90.refs_4_), channel_id=1, source_target_pairs={{0,2},{1,3},{2,0},{3,1},{4,6},{5,7},{6,4},{7,5},{8,10},{9,11},{10,... | collective-permute-start | bytes 98312 | tf_op jit(solution)/shard_map/ppermute | solution.py:405
  17.7 8.3 %collective-permute-start.9 = (bf16[2,64,128]{2,1,0:T(8,128)(2,1)S(1)}, bf16[2,64,128]{2,1,0:T(8,128)(2,1)S(1)}, u32[]{:S(2)}, u32[]{:S(2)}) collective-permute-start(bf16[2,64,128]{2,1,0:T(8,128)(2,1)S(1)} %get-tuple-element.90.refs_4_), channel_id=1, source_target_pairs={{0,1},{1,0},{2,3},{3,2},{4,5},{5,4},{6,7},{7,6},{8,9},{9,8},{10,11... | collective-permute-start | bytes 98312 | tf_op jit(solution)/shard_map/ppermute | solution.py:405
  21.5 5.8 %collective-permute-start.4 = (bf16[2,64,128]{2,1,0:T(8,128)(2,1)S(1)}, bf16[2,64,128]{2,1,0:T(8,128)(2,1)S(1)}, u32[]{:S(2)}, u32[]{:S(2)}) collective-permute-start(bf16[2,64,128]{2,1,0:T(8,128)(2,1)S(1)} %get-tuple-element.86.refs_0_), channel_id=1, source_target_pairs={{0,3},{1,2},{2,1},{3,0},{4,7},{5,6},{6,5},{7,4},{8,11},{9,10},{10,... | collective-permute-start | bytes 98312 | tf_op jit(solution)/shard_map/ppermute | solution.py:405
  24.1 4.8 %collective-permute-start.5 = (bf16[2,64,128]{2,1,0:T(8,128)(2,1)S(1)}, bf16[2,64,128]{2,1,0:T(8,128)(2,1)S(1)}, u32[]{:S(2)}, u32[]{:S(2)}) collective-permute-start(bf16[2,64,128]{2,1,0:T(8,128)(2,1)S(1)} %get-tuple-element.86.refs_0_), channel_id=1, source_target_pairs={{0,2},{1,3},{2,0},{3,1},{4,6},{5,7},{6,4},{7,5},{8,10},{9,11},{10,... | collective-permute-start | bytes 98312 | tf_op jit(solution)/shard_map/ppermute | solution.py:405
  24.1 4.8 %collective-permute-start.6 = (bf16[2,64,128]{2,1,0:T(8,128)(2,1)S(1)}, bf16[2,64,128]{2,1,0:T(8,128)(2,1)S(1)}, u32[]{:S(2)}, u32[]{:S(2)}) collective-permute-start(bf16[2,64,128]{2,1,0:T(8,128)(2,1)S(1)} %get-tuple-element.86.refs_0_), channel_id=1, source_target_pairs={{0,1},{1,0},{2,3},{3,2},{4,5},{5,4},{6,7},{7,6},{8,9},{9,8},{10,11... | collective-permute-start | bytes 98312 | tf_op jit(solution)/shard_map/ppermute | solution.py:405
  26.0 2.9 %copy-start.2 = (bf16[27,128,64]{1,2,0:T(8,128)(2,1)S(1)}, bf16[27,128,64]{1,2,0:T(8,128)(2,1)}, u32[]{:S(2)}) copy-start(bf16[27,128,64]{1,2,0:T(8,128)(2,1)} %param.6) | copy-start | bytes 1327108
  26.0 2.9 %copy-start.3 = (bf16[2,32,8,64]{3,2,1,0:T(8,128)(2,1)S(1)}, bf16[2,32,8,64]{3,2,1,0:T(8,128)(2,1)}, u32[]{:S(2)}) copy-start(bf16[2,32,8,64]{3,2,1,0:T(8,128)(2,1)} %refs_9_.1) | copy-start | bytes 196612
  31.0 6.1 %collective-permute-start.10 = (bf16[4,64,128]{2,1,0:T(8,128)(2,1)S(1)}, bf16[4,64,128]{2,1,0:T(8,128)(2,1)S(1)}, u32[]{:S(2)}, u32[]{:S(2)}) collective-permute-start(bf16[4,64,128]{2,1,0:T(8,128)(2,1)S(1)} %get-tuple-element.96), channel_id=1, source_target_pairs={{0,3},{1,2},{2,1},{3,0},{4,7},{5,6},{6,5},{7,4},{8,11},{9,10},{10,... | collective-permute-start | bytes 196616 | tf_op jit(solution)/shard_map/ppermute | solution.py:405
  32.9 5.9 %collective-permute-start.11 = (bf16[4,64,128]{2,1,0:T(8,128)(2,1)S(1)}, bf16[4,64,128]{2,1,0:T(8,128)(2,1)S(1)}, u32[]{:S(2)}, u32[]{:S(2)}) collective-permute-start(bf16[4,64,128]{2,1,0:T(8,128)(2,1)S(1)} %get-tuple-element.97), channel_id=1, source_target_pairs={{0,2},{1,3},{2,0},{3,1},{4,6},{5,7},{6,4},{7,5},{8,10},{9,11},{10,... | collective-permute-start | bytes 196616 | tf_op jit(solution)/shard_map/ppermute | solution.py:405
  33.6 5.2 %collective-permute-start.12 = (bf16[4,64,128]{2,1,0:T(8,128)(2,1)S(1)}, bf16[4,64,128]{2,1,0:T(8,128)(2,1)S(1)}, u32[]{:S(2)}, u32[]{:S(2)}) collective-permute-start(bf16[4,64,128]{2,1,0:T(8,128)(2,1)S(1)} %get-tuple-element.98), channel_id=1, source_target_pairs={{0,1},{1,0},{2,3},{3,2},{4,5},{5,4},{6,7},{7,6},{8,9},{9,8},{10,11... | collective-permute-start | bytes 196616 | tf_op jit(solution)/shard_map/ppermute | solution.py:405
  39.8 1.7 %collective-permute-start.13 = (bf16[4,240,128]{2,1,0:T(8,128)(2,1)S(1)}, bf16[4,240,128]{2,1,0:T(8,128)(2,1)S(1)}, u32[]{:S(2)}, u32[]{:S(2)}) collective-permute-start(bf16[4,240,128]{2,1,0:T(8,128)(2,1)S(1)} %get-tuple-element.103), channel_id=1, source_target_pairs={{0,4},{4,0},{8,12},{12,8},{16,20},{20,16},{24,28},{28,24},{1,5},{5... | collective-permute-start | bytes 737288 | tf_op jit(solution)/shard_map/ppermute | solution.py:412
  42.3 4.8 %collective-permute-start.14 = (bf16[4,416,128]{2,1,0:T(8,128)(2,1)S(1)}, bf16[4,416,128]{2,1,0:T(8,128)(2,1)S(1)}, u32[]{:S(2)}, u32[]{:S(2)}) collective-permute-start(bf16[4,416,128]{2,1,0:T(8,128)(2,1)S(1)} %early_grad_rest.1), channel_id=1, source_target_pairs={{0,4},{4,0},{8,12},{12,8},{16,20},{20,16},{24,28},{28,24},{1,5},{5... | collective-permute-start | bytes 1277960 | tf_op jit(solution)/shard_map/ppermute | solution.py:412
  42.9 5.2 %collective-permute-start.15 = (bf16[240,128]{1,0:T(8,128)(2,1)S(1)}, bf16[240,128]{1,0:T(8,128)(2,1)S(1)}, u32[]{:S(2)}, u32[]{:S(2)}) collective-permute-start(bf16[240,128]{1,0:T(8,128)(2,1)S(1)} %get-tuple-element.115), channel_id=1, source_target_pairs={{0,24},{4,28},{8,16},{12,20},{16,8},{20,12},{24,0},{28,4},{1,25},{... | collective-permute-start | bytes 184328 | tf_op jit(solution)/shard_map/ppermute | solution.py:405
  44.5 4.5 %collective-permute-start.16 = (bf16[240,128]{1,0:T(8,128)(2,1)S(1)}, bf16[240,128]{1,0:T(8,128)(2,1)S(1)}, u32[]{:S(2)}, u32[]{:S(2)}) collective-permute-start(bf16[240,128]{1,0:T(8,128)(2,1)S(1)} %get-tuple-element.116), channel_id=1, source_target_pairs={{0,16},{4,20},{8,24},{12,28},{16,0},{20,4},{24,8},{28,12},{1,17},{... | collective-permute-start | bytes 184328 | tf_op jit(solution)/shard_map/ppermute | solution.py:405
  45.5 4.2 %collective-permute-start.17 = (bf16[240,128]{1,0:T(8,128)(2,1)S(1)}, bf16[240,128]{1,0:T(8,128)(2,1)S(1)}, u32[]{:S(2)}, u32[]{:S(2)}) collective-permute-start(bf16[240,128]{1,0:T(8,128)(2,1)S(1)} %get-tuple-element.117), channel_id=1, source_target_pairs={{0,8},{4,12},{8,0},{12,4},{16,24},{20,28},{24,16},{28,20},{1,9},{5... | collective-permute-start | bytes 184328 | tf_op jit(solution)/shard_map/ppermute | solution.py:405
  49.7 6.8 %collective-permute-start.18 = (bf16[416,128]{1,0:T(8,128)(2,1)S(1)}, bf16[416,128]{1,0:T(8,128)(2,1)S(1)}, u32[]{:S(2)}, u32[]{:S(2)}) collective-permute-start(bf16[416,128]{1,0:T(8,128)(2,1)S(1)} %get-tuple-element.119), channel_id=1, source_target_pairs={{0,24},{4,28},{8,16},{12,20},{16,8},{20,12},{24,0},{28,4},{1,25},{... | collective-permute-start | bytes 319496 | tf_op jit(solution)/shard_map/ppermute | solution.py:405
  51.1 6.6 %collective-permute-start.19 = (bf16[416,128]{1,0:T(8,128)(2,1)S(1)}, bf16[416,128]{1,0:T(8,128)(2,1)S(1)}, u32[]{:S(2)}, u32[]{:S(2)}) collective-permute-start(bf16[416,128]{1,0:T(8,128)(2,1)S(1)} %get-tuple-element.120), channel_id=1, source_target_pairs={{0,16},{4,20},{8,24},{12,28},{16,0},{20,4},{24,8},{28,12},{1,17},{... | collective-permute-start | bytes 319496 | tf_op jit(solution)/shard_map/ppermute | solution.py:405
  52.0 5.7 %collective-permute-start.20 = (bf16[416,128]{1,0:T(8,128)(2,1)S(1)}, bf16[416,128]{1,0:T(8,128)(2,1)S(1)}, u32[]{:S(2)}, u32[]{:S(2)}) collective-permute-start(bf16[416,128]{1,0:T(8,128)(2,1)S(1)} %get-tuple-element.121), channel_id=1, source_target_pairs={{0,8},{4,12},{8,0},{12,4},{16,24},{20,28},{24,16},{28,20},{1,9},{5... | collective-permute-start | bytes 319496 | tf_op jit(solution)/shard_map/ppermute | solution.py:405
  53.3 7.2 %collective-permute-start.21 = (bf16[240,128]{1,0:T(8,128)(2,1)S(1)}, bf16[240,128]{1,0:T(8,128)(2,1)S(1)}, u32[]{:S(2)}, u32[]{:S(2)}) collective-permute-start(bf16[240,128]{1,0:T(8,128)(2,1)S(1)} %chip_sum.1.refs_0_), channel_id=1, source_target_pairs={{0,3},{1,2},{2,1},{3,0},{4,7},{5,6},{6,5},{7,4},{8,11},{9,10},{10,... | collective-permute-start | bytes 184328 | tf_op jit(solution)/shard_map/ppermute | solution.py:405
  56.0 6.7 %collective-permute-start.22 = (bf16[240,128]{1,0:T(8,128)(2,1)S(1)}, bf16[240,128]{1,0:T(8,128)(2,1)S(1)}, u32[]{:S(2)}, u32[]{:S(2)}) collective-permute-start(bf16[240,128]{1,0:T(8,128)(2,1)S(1)} %chip_sum.1.refs_0_), channel_id=1, source_target_pairs={{0,2},{1,3},{2,0},{3,1},{4,6},{5,7},{6,4},{7,5},{8,10},{9,11},{10,... | collective-permute-start | bytes 184328 | tf_op jit(solution)/shard_map/ppermute | solution.py:405
  56.5 6.2 %collective-permute-start.23 = (bf16[240,128]{1,0:T(8,128)(2,1)S(1)}, bf16[240,128]{1,0:T(8,128)(2,1)S(1)}, u32[]{:S(2)}, u32[]{:S(2)}) collective-permute-start(bf16[240,128]{1,0:T(8,128)(2,1)S(1)} %chip_sum.1.refs_0_), channel_id=1, source_target_pairs={{0,1},{1,0},{2,3},{3,2},{4,5},{5,4},{6,7},{7,6},{8,9},{9,8},{10,11... | collective-permute-start | bytes 184328 | tf_op jit(solution)/shard_map/ppermute | solution.py:405
  57.8 6.5 %collective-permute-start.24 = (bf16[192,128]{1,0:T(8,128)(2,1)S(1)}, bf16[192,128]{1,0:T(8,128)(2,1)S(1)}, u32[]{:S(2)}, u32[]{:S(2)}) collective-permute-start(bf16[192,128]{1,0:T(8,128)(2,1)S(1)} %get-tuple-element.139.refs_0_), channel_id=1, source_target_pairs={{0,3},{1,2},{2,1},{3,0},{4,7},{5,6},{6,5},{7,4},{8,11},{9,10},{10,... | collective-permute-start | bytes 147464 | tf_op jit(solution)/shard_map/ppermute | solution.py:405
  60.5 5.8 %collective-permute-start.25 = (bf16[192,128]{1,0:T(8,128)(2,1)S(1)}, bf16[192,128]{1,0:T(8,128)(2,1)S(1)}, u32[]{:S(2)}, u32[]{:S(2)}) collective-permute-start(bf16[192,128]{1,0:T(8,128)(2,1)S(1)} %get-tuple-element.139.refs_0_), channel_id=1, source_target_pairs={{0,2},{1,3},{2,0},{3,1},{4,6},{5,7},{6,4},{7,5},{8,10},{9,11},{10,... | collective-permute-start | bytes 147464 | tf_op jit(solution)/shard_map/ppermute | solution.py:405
  60.5 5.8 %collective-permute-start.26 = (bf16[192,128]{1,0:T(8,128)(2,1)S(1)}, bf16[192,128]{1,0:T(8,128)(2,1)S(1)}, u32[]{:S(2)}, u32[]{:S(2)}) collective-permute-start(bf16[192,128]{1,0:T(8,128)(2,1)S(1)} %get-tuple-element.139.refs_0_), channel_id=1, source_target_pairs={{0,1},{1,0},{2,3},{3,2},{4,5},{5,4},{6,7},{7,6},{8,9},{9,8},{10,11... | collective-permute-start | bytes 147464 | tf_op jit(solution)/shard_map/ppermute | solution.py:405
  62.7 5.8 %collective-permute-start.27 = (bf16[464,128]{1,0:T(8,128)(2,1)S(1)}, bf16[464,128]{1,0:T(8,128)(2,1)S(1)}, u32[]{:S(2)}, u32[]{:S(2)}) collective-permute-start(bf16[464,128]{1,0:T(8,128)(2,1)S(1)} %filt_sum.1.refs_0_), channel_id=1, source_target_pairs={{0,8},{4,12},{8,0},{12,4},{16,24},{20,28},{24,16},{28,20},{1,9},{5... | collective-permute-start | bytes 356360 | tf_op jit(solution)/shard_map/ppermute | solution.py:405
  63.5 8.8 %collective-permute-start.28 = (bf16[464,128]{1,0:T(8,128)(2,1)S(1)}, bf16[464,128]{1,0:T(8,128)(2,1)S(1)}, u32[]{:S(2)}, u32[]{:S(2)}) collective-permute-start(bf16[464,128]{1,0:T(8,128)(2,1)S(1)} %filt_sum.1.refs_0_), channel_id=1, source_target_pairs={{0,16},{4,20},{8,24},{12,28},{16,0},{20,4},{24,8},{28,12},{1,17},{... | collective-permute-start | bytes 356360 | tf_op jit(solution)/shard_map/ppermute | solution.py:405
  64.3 8.0 %collective-permute-start.29 = (bf16[464,128]{1,0:T(8,128)(2,1)S(1)}, bf16[464,128]{1,0:T(8,128)(2,1)S(1)}, u32[]{:S(2)}, u32[]{:S(2)}) collective-permute-start(bf16[464,128]{1,0:T(8,128)(2,1)S(1)} %filt_sum.1.refs_0_), channel_id=1, source_target_pairs={{0,24},{4,28},{8,16},{12,20},{16,8},{20,12},{24,0},{28,4},{1,25},{... | collective-permute-start | bytes 356360 | tf_op jit(solution)/shard_map/ppermute | solution.py:405
  66.3 4.5 %collective-permute-start.31 = (bf16[192,128]{1,0:T(8,128)(2,1)S(1)}, bf16[192,128]{1,0:T(8,128)(2,1)S(1)}, u32[]{:S(2)}, u32[]{:S(2)}) collective-permute-start(bf16[192,128]{1,0:T(8,128)(2,1)S(1)} %filt_sum_rest.1.refs_4_), channel_id=1, source_target_pairs={{0,16},{4,20},{8,24},{12,28},{16,0},{20,4},{24,8},{28,12},{1,17},{... | collective-permute-start | bytes 147464 | tf_op jit(solution)/shard_map/ppermute | solution.py:405
  67.3 5.0 %collective-permute-start.32 = (bf16[192,128]{1,0:T(8,128)(2,1)S(1)}, bf16[192,128]{1,0:T(8,128)(2,1)S(1)}, u32[]{:S(2)}, u32[]{:S(2)}) collective-permute-start(bf16[192,128]{1,0:T(8,128)(2,1)S(1)} %filt_sum_rest.1.refs_4_), channel_id=1, source_target_pairs={{0,24},{4,28},{8,16},{12,20},{16,8},{20,12},{24,0},{28,4},{1,25},{... | collective-permute-start | bytes 147464 | tf_op jit(solution)/shard_map/ppermute | solution.py:405
  68.6 4.1 %collective-permute-start.30 = (bf16[192,128]{1,0:T(8,128)(2,1)S(1)}, bf16[192,128]{1,0:T(8,128)(2,1)S(1)}, u32[]{:S(2)}, u32[]{:S(2)}) collective-permute-start(bf16[192,128]{1,0:T(8,128)(2,1)S(1)} %filt_sum_rest.1.refs_4_), channel_id=1, source_target_pairs={{0,8},{4,12},{8,0},{12,4},{16,24},{20,28},{24,16},{28,20},{1,9},{5... | collective-permute-start | bytes 147464 | tf_op jit(solution)/shard_map/ppermute | solution.py:405
  72.7 2.2 %collective-permute-start.33 = (bf16[4,656,128]{2,1,0:T(8,128)(2,1)S(1)}, bf16[4,656,128]{2,1,0:T(8,128)(2,1)S(1)}, u32[]{:S(2)}, u32[]{:S(2)}) collective-permute-start(bf16[4,656,128]{2,1,0:T(8,128)(2,1)S(1)} %stack.1.pieces), channel_id=1, source_target_pairs={{0,4},{4,0},{8,12},{12,8},{16,20},{20,16},{24,28},{28,24},{1,5},{5... | collective-permute-start | bytes 2015240 | tf_op jit(solution)/shard_map/ppermute | solution.py:412

commit v2 on v1

--- a/solution.py
+++ b/solution.py
@@ -387,8 +387,9 @@
                     pieces[q, first + inner : first + inner + size].astype(F32) * scale
                 )
                 row += size
-            if tap % 3 == 2:
-                taps = pl.ds(tap - 2, 3)
+            some = (end - begin) // 3
+            if (tap + 1 - begin) % some == 0:
+                taps = pl.ds(tap + 1 - some, some)
                 copy = pltpu.make_async_copy(
                     held.at[taps], out.at[taps, pl.ds(side * part, part)], sem.at[len(copies)]
                 )
@@ -521,6 +522,7 @@
         [pltpu.VMEM((2, chips * deep_rows, width), F32)],
         flops=2 * dx * dy * dz * 27 * width * filters,
     )
+    deep_first, terms[-1] = lax.optimization_barrier((deep_first, terms[-1]))
     cuts = ((0, 5), (5, 9))
     steps = [3 * (end - begin) * (cin // 2) // chips for begin, end in cuts]
     flops = 2 * (nx + 4) * rows * 18 * cin * 2 * width
@@ -550,6 +552,7 @@
     )
     sums = core_sums("core_sum", mine, theirs)
     grad, sums[0] = lax.optimization_barrier((grad, sums[0]))
+    first = backward(paired(sums, "space", 2))
     size = (chips, steps[1] + deep_rows, width)
     theirs = call(
         functools.partial(early_grad_rest_body, False, cuts[1]),
@@ -568,10 +571,9 @@
         [helds[1]],
         flops=flops,
     )
-    sums = [sums, core_sums("core_sum_rest", mine, theirs)]
-    first = backward(paired(sums[0], "space", 2))
-    *sums[1], first = lax.optimization_barrier((*sums[1], first))
-    second = backward(paired(sums[1], "space", 2))
+    sums = core_sums("core_sum_rest", mine, theirs)
+    *sums, first = lax.optimization_barrier((*sums, first))
+    second = backward(paired(sums, "space", 2))
     (early,) = call(
         functools.partial(chip_sum_body, chips), "chip_sum", [struct((steps[0], width))], first
     )
@@ -613,7 +615,7 @@
     scratch = [
         pltpu.VMEM((27, cin // 2, width), F32),
         pltpu.VMEM((27, filters // 2, width), F32),
-        DMA((18,)),
+        DMA((9,)),
     ]
     results = call(
         functools.partial(finish_body, True, *scales),

time: 76.3 us -> 75.6 us (level)
    ppermute x27, waiting for transfers between devices: 11.4 us -> 10.3 us  [paired(): lax.ppermute(values[j], axis, [(i, i ^ step * j) for i in range(count)])]
  transfers between devices with their start and end apart: 34 -> 34, of which waited for: 14 -> 12; matrix products, arithmetic and copies ran while one was open for 0% -> 0% of each run, Pallas kernels for 12% -> 12%
where the time goes in v2:
time: 75.6 us; the launch traced here: 75.4 us
  starting transfers between devices  44.6 us (59%)
  waiting for transfers between devices  15.1 us (20%)
  Pallas kernels  14.1 us (19%)
  between operations  0.84 us (1%)
  local copies, waits for them, and re-layouts  0.76 us (1%)
    ppermute x27, starting transfers between devices, paired(): lax.ppermute(values[j], axis, [(i, i ^ step * j) for i in range(count)])  36.1 us
    pallas_call x20, Pallas kernels, call(): pl.pallas_call(body, name=name, out_shape=out_shape, in_specs=[HBM if i i...  14.1 us
    ppermute x27, waiting for transfers between devices, paired(): lax.ppermute(values[j], axis, [(i, i ^ step * j) for i in range(count)])  10.3 us
    ppermute x4, starting transfers between devices, swap(): return lax.ppermute(value, axis, pairs + [(b, a) for a, b in pairs])  8.18 us
    ppermute x4, waiting for transfers between devices, swap(): return lax.ppermute(value, axis, pairs + [(b, a) for a, b in pairs])  3.24 us
    ppermute x3, waiting for transfers between devices, exchange(): lax.ppermute(value, axis, [(i, i ^ step) for i in range(lax.axis_size(axi...  1.6 us
  transfers between devices with their start and end apart: 34, of which 12 were waited for; matrix products, arithmetic and copies ran while one was open for 0% of the time, Pallas kernels for 12%

profile of v2, /device:TPU:0, one launch (start us, length us, event | category | flops | bytes accessed | tf_op | source)
XLA Modules:
  0.0 75.4 jit_solution(17404911798245020921)
XLA Ops:
  0.6 0.7 fusion
  1.4 3.1 %collective-permute-start = (bf16[4,2,16,128]{3,2,1,0:T(8,128)(2,1)S(1)}, bf16[4,2,16,128]{3,2,1,0:T(8,128)(2,1)S(1)}, u32[]{:S(2)}, u32[]{:S(2)}) collective-permute-start(bf16[4,2,16,128]{3,2,1,0:T(8,128)(2,1)S(1)} %edges.1), channel_id=1, source_target_pairs={{0,1},{2,3},{1,0},{3,2},{4,5},{6,7},{5,4},{7,6},{8,9},{10,11},{9,8... | collective-permute-start | bytes 98312 | tf_op jit(solution)/shard_map/ppermute | solution.py:423
  4.5 2.5 %collective-permute-start.1 = (bf16[4,2,16,128]{3,2,1,0:T(8,128)(2,1)S(1)}, bf16[4,2,16,128]{3,2,1,0:T(8,128)(2,1)S(1)}, u32[]{:S(2)}, u32[]{:S(2)}) collective-permute-start(bf16[4,2,16,128]{3,2,1,0:T(8,128)(2,1)S(1)} %edges.1), channel_id=1, source_target_pairs={{1,2},{3,0},{2,1},{0,3},{5,6},{7,4},{6,5},{4,7},{9,10},{11,8},{10,... | collective-permute-start | bytes 98312 | tf_op jit(solution)/shard_map/ppermute | solution.py:423
  7.0 3.2 %collective-permute-done.1.yodd = bf16[4,2,16,128]{3,2,1,0:T(8,128)(2,1)S(1)} collective-permute-done((bf16[4,2,16,128]{3,2,1,0:T(8,128)(2,1)S(1)}, bf16[4,2,16,128]{3,2,1,0:T(8,128)(2,1)S(1)}, u32[]{:S(2)}, u32[]{:S(2)}) %collective-permute-start.1) | collective-permute-done | bytes 32800 | tf_op jit(solution)/shard_map/ppermute | solution.py:423
  10.4 2.5 %collective-permute-start.3 = (bf16[3,18,16,128]{3,2,1,0:T(8,128)(2,1)S(1)}, bf16[3,18,16,128]{3,2,1,0:T(8,128)(2,1)S(1)}, u32[]{:S(2)}, u32[]{:S(2)}) collective-permute-start(bf16[3,18,16,128]{3,2,1,0:T(8,128)(2,1)S(1)} %get-tuple-element.82), channel_id=1, source_target_pairs={{4,8},{12,16},{20,24},{28,0},{8,4},{16,12},{24,20},{0,28},{5,9},{1... | collective-permute-start | bytes 663560 | tf_op jit(solution)/shard_map/ppermute | solution.py:423
  12.9 2.2 %early_near.1 = (bf16[3,7,128,512]{3,2,1,0:T(8,128)(2,1)S(1)}, f32[4,128,256]{2,1,0:T(8,128)S(1)}, bf16[2,64,128]{2,1,0:T(8,128)(2,1)S(1)}, bf16[9,512,256]{2,1,0:T(8,128)(2,1)S(1)}) custom-call(bf16[4,16,16,128]{3,2,1,0:T(8,128)(2,1)S(1)} %get-tuple-element.78.center, bf16[4,2,16,128]{3,2,1,0:T(8,128)(2,1)S(1)} %get-tuple-element.79.sides, ...), custom_call_target="tpu_custom_call" | custom-call | flops 1207959552 | bytes 1048576 | tf_op jit(solution)/shard_map/early_near/pallas_call | solution.py:23
  15.1 2.5 %collective-permute-start.7 = (bf16[2,64,128]{2,1,0:T(8,128)(2,1)S(1)}, bf16[2,64,128]{2,1,0:T(8,128)(2,1)S(1)}, u32[]{:S(2)}, u32[]{:S(2)}) collective-permute-start(bf16[2,64,128]{2,1,0:T(8,128)(2,1)S(1)} %get-tuple-element.92.refs_4_), channel_id=1, source_target_pairs={{0,3},{1,2},{2,1},{3,0},{4,7},{5,6},{6,5},{7,4},{8,11},{9,10},{10,... | collective-permute-start | bytes 98312 | tf_op jit(solution)/shard_map/ppermute | solution.py:406
  17.7 1.9 %collective-permute-start.9 = (bf16[2,64,128]{2,1,0:T(8,128)(2,1)S(1)}, bf16[2,64,128]{2,1,0:T(8,128)(2,1)S(1)}, u32[]{:S(2)}, u32[]{:S(2)}) collective-permute-start(bf16[2,64,128]{2,1,0:T(8,128)(2,1)S(1)} %get-tuple-element.92.refs_4_), channel_id=1, source_target_pairs={{0,1},{1,0},{2,3},{3,2},{4,5},{5,4},{6,7},{7,6},{8,9},{9,8},{10,11... | collective-permute-start | bytes 98312 | tf_op jit(solution)/shard_map/ppermute | solution.py:406
  19.6 1.9 %early_far.1 = (bf16[3,3,128,512]{3,2,1,0:T(8,128)(2,1)S(1)}, f32[4,128,256]{2,1,0:T(8,128)S(1)}, bf16[2,64,128]{2,1,0:T(8,128)(2,1)S(1)}) custom-call(bf16[3,7,128,512]{3,2,1,0:T(8,128)(2,1)S(1)} %get-tuple-element.86.windows, bf16[3,18,16,128]{3,2,1,0:T(8,128)(2,1)S(1)} %collective-permute-done.3.far, bf16[9,512,256]{2,1,0:T(8,128)(2,1)S(1)} %get-tuple-element.83.wide), custom_call_target="tpu_custom_call" | custom-call | flops 1207959552 | bytes 1048576 | tf_op jit(solution)/shard_map/early_far/pallas_call | solution.py:23
  21.5 2.5 %collective-permute-start.4 = (bf16[2,64,128]{2,1,0:T(8,128)(2,1)S(1)}, bf16[2,64,128]{2,1,0:T(8,128)(2,1)S(1)}, u32[]{:S(2)}, u32[]{:S(2)}) collective-permute-start(bf16[2,64,128]{2,1,0:T(8,128)(2,1)S(1)} %get-tuple-element.88.refs_0_), channel_id=1, source_target_pairs={{0,3},{1,2},{2,1},{3,0},{4,7},{5,6},{6,5},{7,4},{8,11},{9,10},{10,... | collective-permute-start | bytes 98312 | tf_op jit(solution)/shard_map/ppermute | solution.py:406
  24.1 1.9 %collective-permute-start.6 = (bf16[2,64,128]{2,1,0:T(8,128)(2,1)S(1)}, bf16[2,64,128]{2,1,0:T(8,128)(2,1)S(1)}, u32[]{:S(2)}, u32[]{:S(2)}) collective-permute-start(bf16[2,64,128]{2,1,0:T(8,128)(2,1)S(1)} %get-tuple-element.88.refs_0_), channel_id=1, source_target_pairs={{0,1},{1,0},{2,3},{3,2},{4,5},{5,4},{6,7},{7,6},{8,9},{9,8},{10,11... | collective-permute-start | bytes 98312 | tf_op jit(solution)/shard_map/ppermute | solution.py:406
  26.0 1.1 %turn_windows.1.refs_6_.refs_1_ = bf16[3,2,256,1280]{3,2,1,0:T(8,128)(2,1)S(1)} custom-call(bf16[3,7,128,512]{3,2,1,0:T(8,128)(2,1)S(1)} %get-tuple-element.86.windows, bf16[3,3,128,512]{3,2,1,0:T(8,128)(2,1)S(1)} %get-tuple-element.87.far_windows), custom_call_target="tpu_custom_call" | custom-call | flops 1073741824 | bytes 1048576 | tf_op jit(solution)/shard_map/turn_windows/pallas_call | solution.py:23
  27.3 1.6 %collective-permute-done.5.refs_2_ = bf16[2,64,128]{2,1,0:T(8,128)(2,1)S(1)} collective-permute-done((bf16[2,64,128]{2,1,0:T(8,128)(2,1)S(1)}, bf16[2,64,128]{2,1,0:T(8,128)(2,1)S(1)}, u32[]{:S(2)}, u32[]{:S(2)}) %collective-permute-start.5) | collective-permute-done | bytes 32800 | tf_op jit(solution)/shard_map/ppermute | solution.py:406
  28.9 2.1 %deep_conv.1 = (bf16[2,32,8,64]{3,2,1,0:T(8,128)(2,1)}, bf16[2,256,64]{2,1,0:T(8,128)(2,1)S(1)}, bf16[3,4,256,384]{3,2,1,0:T(8,128)(2,1)S(1)}, f32[4,64,128]{2,1...) custom-call(bf16[2,64,128]{2,1,0:T(8,128)(2,1)S(1)} %get-tuple-eleme, ...), custom_call_target="tpu_custom_call" | custom-call | flops 452984832 | bytes 1048576 | tf_op jit(solution)/shard_map/deep_conv/pallas_call | solution.py:23
  31.0 1.9 %collective-permute-start.10 = (bf16[4,64,128]{2,1,0:T(8,128)(2,1)S(1)}, bf16[4,64,128]{2,1,0:T(8,128)(2,1)S(1)}, u32[]{:S(2)}, u32[]{:S(2)}) collective-permute-start(bf16[4,64,128]{2,1,0:T(8,128)(2,1)S(1)} %get-tuple-element.101), channel_id=1, source_target_pairs={{0,3},{1,2},{2,1},{3,0},{4,7},{5,6},{6,5},{7,4},{8,11},{9,10},{10,... | collective-permute-start | bytes 196616 | tf_op jit(solution)/shard_map/ppermute | solution.py:406
  32.9 0.7 collective-permute-start.11
  33.6 1.9 %collective-permute-start.12 = (bf16[4,64,128]{2,1,0:T(8,128)(2,1)S(1)}, bf16[4,64,128]{2,1,0:T(8,128)(2,1)S(1)}, u32[]{:S(2)}, u32[]{:S(2)}) collective-permute-start(bf16[4,64,128]{2,1,0:T(8,128)(2,1)S(1)} %get-tuple-element.104), channel_id=1, source_target_pairs={{0,1},{1,0},{2,3},{3,2},{4,5},{5,4},{6,7},{7,6},{8,9},{9,8},{10,11... | collective-permute-start | bytes 196616 | tf_op jit(solution)/shard_map/ppermute | solution.py:406
  35.5 0.7 deep_grad.1
  36.2 0.9 %collective-permute-done.10.refs_1_ = bf16[4,64,128]{2,1,0:T(8,128)(2,1)S(1)} collective-permute-done((bf16[4,64,128]{2,1,0:T(8,128)(2,1)S(1)}, bf16[4,64,128]{2,1,0:T(8,128)(2,1)S(1)}, u32[]{:S(2)}, u32[]{:S(2)}) %collective-permute-start.10) | collective-permute-done | bytes 65568 | tf_op jit(solution)/shard_map/ppermute | solution.py:406
  37.2 1.6 %collective-permute-done.11.refs_2_ = bf16[4,64,128]{2,1,0:T(8,128)(2,1)S(1)} collective-permute-done((bf16[4,64,128]{2,1,0:T(8,128)(2,1)S(1)}, bf16[4,64,128]{2,1,0:T(8,128)(2,1)S(1)}, u32[]{:S(2)}, u32[]{:S(2)}) %collective-permute-start.11) | collective-permute-done | bytes 65568 | tf_op jit(solution)/shard_map/ppermute | solution.py:406
  38.8 1.0 %early_grad.1 = (bf16[4,240,128]{2,1,0:T(8,128)(2,1)S(1)}, bf16[8,128,256]{2,1,0:T(8,128)(2,1)S(1)}) custom-call(f32[4,64,128]{2,1,0:T(8,128)S(1)} %get-tuple-element.97.refs_0_, bf16[4,64,128]{2,1,0:T(8,128)(2,1)S(1)} %collective-permute-done.10.refs_1_, bf16[4,64,128]{2,1,0:T(8,128)(2,1)S(1)} %collective-permute-done.11.refs_2_, ...), custom_call_target="tpu_custom_call" | custom-call | flops 1207959552 | bytes 1048576 | tf_op jit(solution)/shard_map/early_grad/pallas_call | solution.py:23
  39.9 0.8 %early_grad_own.1.mine = f32[4,240,128]{2,1,0:T(8,128)S(1)} custom-call(bf16[8,128,256]{2,1,0:T(8,128)(2,1)S(1)} %get-tuple-element.111.refs_0_, bf16[3,2,256,1280]{3,2,1,0:T(8,128)(2,1)S(1)} %turn_windows.1.refs_6_.refs_1_), custom_call_target="tpu_custom_call" | custom-call | flops 1207959552 | bytes 1048576 | tf_op jit(solution)/shard_map/early_grad_own/pallas_call | solution.py:23
  40.7 0.6 collective-permute-done.13.other
  41.5 0.7 early_grad_rest.1
  42.4 1.7 %collective-permute-start.15 = (bf16[240,128]{1,0:T(8,128)(2,1)S(1)}, bf16[240,128]{1,0:T(8,128)(2,1)S(1)}, u32[]{:S(2)}, u32[]{:S(2)}) collective-permute-start(bf16[240,128]{1,0:T(8,128)(2,1)S(1)} %get-tuple-element.119), channel_id=1, source_target_pairs={{0,24},{4,28},{8,16},{12,20},{16,8},{20,12},{24,0},{28,4},{1,25},{... | collective-permute-start | bytes 184328 | tf_op jit(solution)/shard_map/ppermute | solution.py:406
  44.1 1.0 %collective-permute-start.16 = (bf16[240,128]{1,0:T(8,128)(2,1)S(1)}, bf16[240,128]{1,0:T(8,128)(2,1)S(1)}, u32[]{:S(2)}, u32[]{:S(2)}) collective-permute-start(bf16[240,128]{1,0:T(8,128)(2,1)S(1)} %get-tuple-element.120), channel_id=1, source_target_pairs={{0,16},{4,20},{8,24},{12,28},{16,0},{20,4},{24,8},{28,12},{1,17},{... | collective-permute-start | bytes 184328 | tf_op jit(solution)/shard_map/ppermute | solution.py:406
  45.0 0.8 %collective-permute-start.17 = (bf16[240,128]{1,0:T(8,128)(2,1)S(1)}, bf16[240,128]{1,0:T(8,128)(2,1)S(1)}, u32[]{:S(2)}, u32[]{:S(2)}) collective-permute-start(bf16[240,128]{1,0:T(8,128)(2,1)S(1)} %get-tuple-element.121), channel_id=1, source_target_pairs={{0,8},{4,12},{8,0},{12,4},{16,24},{20,28},{24,16},{28,20},{1,9},{5... | collective-permute-start | bytes 184328 | tf_op jit(solution)/shard_map/ppermute | solution.py:406
  45.9 0.7 early_grad_rest_own.1.mine
  46.7 0.9 %collective-permute-done.15.refs_1_ = bf16[240,128]{1,0:T(8,128)(2,1)S(1)} collective-permute-done((bf16[240,128]{1,0:T(8,128)(2,1)S(1)}, bf16[240,128]{1,0:T(8,128)(2,1)S(1)}, u32[]{:S(2)}, u32[]{:S(2)}) %collective-permute-start.15) | collective-permute-done | bytes 61472 | tf_op jit(solution)/shard_map/ppermute | solution.py:406
  47.6 1.2 %collective-permute-done.16.refs_2_ = bf16[240,128]{1,0:T(8,128)(2,1)S(1)} collective-permute-done((bf16[240,128]{1,0:T(8,128)(2,1)S(1)}, bf16[240,128]{1,0:T(8,128)(2,1)S(1)}, u32[]{:S(2)}, u32[]{:S(2)}) %collective-permute-start.16) | collective-permute-done | bytes 61472 | tf_op jit(solution)/shard_map/ppermute | solution.py:406
  48.9 0.4 collective-permute-done.17.refs_3_
  49.3 1.3 %collective-permute-start.18 = (bf16[416,128]{1,0:T(8,128)(2,1)S(1)}, bf16[416,128]{1,0:T(8,128)(2,1)S(1)}, u32[]{:S(2)}, u32[]{:S(2)}) collective-permute-start(bf16[416,128]{1,0:T(8,128)(2,1)S(1)} %get-tuple-element.123), channel_id=1, source_target_pairs={{0,24},{4,28},{8,16},{12,20},{16,8},{20,12},{24,0},{28,4},{1,25},{... | collective-permute-start | bytes 319496 | tf_op jit(solution)/shard_map/ppermute | solution.py:406
  50.6 1.0 %collective-permute-start.19 = (bf16[416,128]{1,0:T(8,128)(2,1)S(1)}, bf16[416,128]{1,0:T(8,128)(2,1)S(1)}, u32[]{:S(2)}, u32[]{:S(2)}) collective-permute-start(bf16[416,128]{1,0:T(8,128)(2,1)S(1)} %get-tuple-element.124), channel_id=1, source_target_pairs={{0,16},{4,20},{8,24},{12,28},{16,0},{20,4},{24,8},{28,12},{1,17},{... | collective-permute-start | bytes 319496 | tf_op jit(solution)/shard_map/ppermute | solution.py:406
  51.6 1.2 %collective-permute-start.20 = (bf16[416,128]{1,0:T(8,128)(2,1)S(1)}, bf16[416,128]{1,0:T(8,128)(2,1)S(1)}, u32[]{:S(2)}, u32[]{:S(2)}) collective-permute-start(bf16[416,128]{1,0:T(8,128)(2,1)S(1)} %get-tuple-element.125), channel_id=1, source_target_pairs={{0,8},{4,12},{8,0},{12,4},{16,24},{20,28},{24,16},{28,20},{1,9},{5... | collective-permute-start | bytes 319496 | tf_op jit(solution)/shard_map/ppermute | solution.py:406
  52.8 2.7 %collective-permute-start.21 = (bf16[240,128]{1,0:T(8,128)(2,1)S(1)}, bf16[240,128]{1,0:T(8,128)(2,1)S(1)}, u32[]{:S(2)}, u32[]{:S(2)}) collective-permute-start(bf16[240,128]{1,0:T(8,128)(2,1)S(1)} %chip_sum.1.refs_0_), channel_id=1, source_target_pairs={{0,3},{1,2},{2,1},{3,0},{4,7},{5,6},{6,5},{7,4},{8,11},{9,10},{10,... | collective-permute-start | bytes 184328 | tf_op jit(solution)/shard_map/ppermute | solution.py:406
  55.7 1.5 %collective-permute-start.23 = (bf16[240,128]{1,0:T(8,128)(2,1)S(1)}, bf16[240,128]{1,0:T(8,128)(2,1)S(1)}, u32[]{:S(2)}, u32[]{:S(2)}) collective-permute-start(bf16[240,128]{1,0:T(8,128)(2,1)S(1)} %chip_sum.1.refs_0_), channel_id=1, source_target_pairs={{0,1},{1,0},{2,3},{3,2},{4,5},{5,4},{6,7},{7,6},{8,9},{9,8},{10,11... | collective-permute-start | bytes 184328 | tf_op jit(solution)/shard_map/ppermute | solution.py:406
  57.3 2.7 %collective-permute-start.24 = (bf16[192,128]{1,0:T(8,128)(2,1)S(1)}, bf16[192,128]{1,0:T(8,128)(2,1)S(1)}, u32[]{:S(2)}, u32[]{:S(2)}) collective-permute-start(bf16[192,128]{1,0:T(8,128)(2,1)S(1)} %get-tuple-element.143.refs_0_), channel_id=1, source_target_pairs={{0,3},{1,2},{2,1},{3,0},{4,7},{5,6},{6,5},{7,4},{8,11},{9,10},{10,... | collective-permute-start | bytes 147464 | tf_op jit(solution)/shard_map/ppermute | solution.py:406
  60.0 1.7 %collective-permute-start.26 = (bf16[192,128]{1,0:T(8,128)(2,1)S(1)}, bf16[192,128]{1,0:T(8,128)(2,1)S(1)}, u32[]{:S(2)}, u32[]{:S(2)}) collective-permute-start(bf16[192,128]{1,0:T(8,128)(2,1)S(1)} %get-tuple-element.143.refs_0_), channel_id=1, source_target_pairs={{0,1},{1,0},{2,3},{3,2},{4,5},{5,4},{6,7},{7,6},{8,9},{9,8},{10,11... | collective-permute-start | bytes 147464 | tf_op jit(solution)/shard_map/ppermute | solution.py:406
  61.8 1.0 %collective-permute-start.27 = (bf16[464,128]{1,0:T(8,128)(2,1)S(1)}, bf16[464,128]{1,0:T(8,128)(2,1)S(1)}, u32[]{:S(2)}, u32[]{:S(2)}) collective-permute-start(bf16[464,128]{1,0:T(8,128)(2,1)S(1)} %filt_sum.1.refs_0_), channel_id=1, source_target_pairs={{0,8},{4,12},{8,0},{12,4},{16,24},{20,28},{24,16},{28,20},{1,9},{5... | collective-permute-start | bytes 356360 | tf_op jit(solution)/shard_map/ppermute | solution.py:406
  62.8 1.1 %collective-permute-start.28 = (bf16[464,128]{1,0:T(8,128)(2,1)S(1)}, bf16[464,128]{1,0:T(8,128)(2,1)S(1)}, u32[]{:S(2)}, u32[]{:S(2)}) collective-permute-start(bf16[464,128]{1,0:T(8,128)(2,1)S(1)} %filt_sum.1.refs_0_), channel_id=1, source_target_pairs={{0,16},{4,20},{8,24},{12,28},{16,0},{20,4},{24,8},{28,12},{1,17},{... | collective-permute-start | bytes 356360 | tf_op jit(solution)/shard_map/ppermute | solution.py:406
  63.8 1.5 %collective-permute-start.29 = (bf16[464,128]{1,0:T(8,128)(2,1)S(1)}, bf16[464,128]{1,0:T(8,128)(2,1)S(1)}, u32[]{:S(2)}, u32[]{:S(2)}) collective-permute-start(bf16[464,128]{1,0:T(8,128)(2,1)S(1)} %filt_sum.1.refs_0_), channel_id=1, source_target_pairs={{0,24},{4,28},{8,16},{12,20},{16,8},{20,12},{24,0},{28,4},{1,25},{... | collective-permute-start | bytes 356360 | tf_op jit(solution)/shard_map/ppermute | solution.py:406
  65.4 1.1 %collective-permute-start.31 = (bf16[192,128]{1,0:T(8,128)(2,1)S(1)}, bf16[192,128]{1,0:T(8,128)(2,1)S(1)}, u32[]{:S(2)}, u32[]{:S(2)}) collective-permute-start(bf16[192,128]{1,0:T(8,128)(2,1)S(1)} %filt_sum_rest.1.refs_4_), channel_id=1, source_target_pairs={{0,16},{4,20},{8,24},{12,28},{16,0},{20,4},{24,8},{28,12},{1,17},{... | collective-permute-start | bytes 147464 | tf_op jit(solution)/shard_map/ppermute | solution.py:406
  66.5 1.3 %collective-permute-start.32 = (bf16[192,128]{1,0:T(8,128)(2,1)S(1)}, bf16[192,128]{1,0:T(8,128)(2,1)S(1)}, u32[]{:S(2)}, u32[]{:S(2)}) collective-permute-start(bf16[192,128]{1,0:T(8,128)(2,1)S(1)} %filt_sum_rest.1.refs_4_), channel_id=1, source_target_pairs={{0,24},{4,28},{8,16},{12,20},{16,8},{20,12},{24,0},{28,4},{1,25},{... | collective-permute-start | bytes 147464 | tf_op jit(solution)/shard_map/ppermute | solution.py:406
  67.9 1.1 %collective-permute-start.30 = (bf16[192,128]{1,0:T(8,128)(2,1)S(1)}, bf16[192,128]{1,0:T(8,128)(2,1)S(1)}, u32[]{:S(2)}, u32[]{:S(2)}) collective-permute-start(bf16[192,128]{1,0:T(8,128)(2,1)S(1)} %filt_sum_rest.1.refs_4_), channel_id=1, source_target_pairs={{0,8},{4,12},{8,0},{12,4},{16,24},{20,28},{24,16},{28,20},{1,9},{5... | collective-permute-start | bytes 147464 | tf_op jit(solution)/shard_map/ppermute | solution.py:406
  69.0 3.0 %collective-permute-done.31.refs_6_ = bf16[192,128]{1,0:T(8,128)(2,1)S(1)} collective-permute-done((bf16[192,128]{1,0:T(8,128)(2,1)S(1)}, bf16[192,128]{1,0:T(8,128)(2,1)S(1)}, u32[]{:S(2)}, u32[]{:S(2)}) %collective-permute-start.31) | collective-permute-done | bytes 49184 | tf_op jit(solution)/shard_map/ppermute | solution.py:406
  72.2 1.1 %finish_own.1 = (f32[27,128,128]{2,1,0:T(8,128)}, f32[27,64,128]{2,1,0:T(8,128)}) custom-call(bf16[4,656,128]{2,1,0:T(8,128)(2,1)S(1)} %stack.1.pieces), custom_call_target="tpu_custom_call" | custom-call | bytes 1048576 | tf_op jit(solution)/shard_map/finish_own/pallas_call | solution.py:23
  73.3 1.0 %collective-permute-done.33.pieces = bf16[4,656,128]{2,1,0:T(8,128)(2,1)S(1)} collective-permute-done((bf16[4,656,128]{2,1,0:T(8,128)(2,1)S(1)}, bf16[4,656,128]{2,1,0:T(8,128)(2,1)S(1)}, u32[]{:S(2)}, u32[]{:S(2)}) %collective-permute-start.33) | collective-permute-done | bytes 671776 | tf_op jit(solution)/shard_map/ppermute | solution.py:413
  74.3 1.1 %finish_other.1 = (f32[27,128,128]{2,1,0:T(8,128)}, f32[27,64,128]{2,1,0:T(8,128)}) custom-call(bf16[4,656,128]{2,1,0:T(8,128)(2,1)S(1)} %collective-permute-done.33.pieces, f32[27,128,128]{2,1,0:T(8,128)} %get-tuple-element.149.refs_0_, f32[27,64,128]{2,1,0:T(8,128)} %get-tuple-element.150.refs_1_), custom_call_target="tpu_custom_call", output_to_operand_aliasing={{0}: (1, {}), {1}: (2, {})} | custom-call | bytes 1048576 | tf_op jit(solution)/shard_map/finish_other/pallas_call | solution.py:23
  (50 shorter events, 1.4 us)
Async XLA Ops:
  1.4 8.8 %copy-start = (bf16[4,16,16,128]{3,2,1,0:T(8,128)(2,1)S(1)}, bf16[4,16,16,128]{3,2,1,0:T(8,128)(2,1)}, u32[]{:S(2)}) copy-start(bf16[4,16,16,128]{3,2,1,0:T(8,128)(2,1)} %center.1) | copy-start | bytes 786436
  1.4 11.5 %copy-start.1 = (bf16[27,128,128]{2,1,0:T(8,128)(2,1)S(1)}, bf16[27,128,128]{2,1,0:T(8,128)(2,1)}, u32[]{:S(2)}) copy-start(bf16[27,128,128]{2,1,0:T(8,128)(2,1)} %w.1) | copy-start | bytes 2654212
  1.4 5.6 %collective-permute-start = (bf16[4,2,16,128]{3,2,1,0:T(8,128)(2,1)S(1)}, bf16[4,2,16,128]{3,2,1,0:T(8,128)(2,1)S(1)}, u32[]{:S(2)}, u32[]{:S(2)}) collective-permute-start(bf16[4,2,16,128]{3,2,1,0:T(8,128)(2,1)S(1)} %edges.1), channel_id=1, source_target_pairs={{0,1},{2,3},{1,0},{3,2},{4,5},{6,7},{5,4},{7,6},{8,9},{10,11},{9,8... | collective-permute-start | bytes 98312 | tf_op jit(solution)/shard_map/ppermute | solution.py:423
  4.5 5.7 %collective-permute-start.1 = (bf16[4,2,16,128]{3,2,1,0:T(8,128)(2,1)S(1)}, bf16[4,2,16,128]{3,2,1,0:T(8,128)(2,1)S(1)}, u32[]{:S(2)}, u32[]{:S(2)}) collective-permute-start(bf16[4,2,16,128]{3,2,1,0:T(8,128)(2,1)S(1)} %edges.1), channel_id=1, source_target_pairs={{1,2},{3,0},{2,1},{0,3},{5,6},{7,4},{6,5},{4,7},{9,10},{11,8},{10,... | collective-permute-start | bytes 98312 | tf_op jit(solution)/shard_map/ppermute | solution.py:423
  10.3 2.6 %collective-permute-start.2 = (bf16[3,18,16,128]{3,2,1,0:T(8,128)(2,1)S(1)}, bf16[3,18,16,128]{3,2,1,0:T(8,128)(2,1)S(1)}, u32[]{:S(2)}, u32[]{:S(2)}) collective-permute-start(bf16[3,18,16,128]{3,2,1,0:T(8,128)(2,1)S(1)} %get-tuple-element.80), channel_id=1, source_target_pairs={{0,4},{8,12},{16,20},{24,28},{4,0},{12,8},{20,16},{28,24},{1,5},{9... | collective-permute-start | bytes 663560 | tf_op jit(solution)/shard_map/ppermute | solution.py:423
  10.4 9.2 %collective-permute-start.3 = (bf16[3,18,16,128]{3,2,1,0:T(8,128)(2,1)S(1)}, bf16[3,18,16,128]{3,2,1,0:T(8,128)(2,1)S(1)}, u32[]{:S(2)}, u32[]{:S(2)}) collective-permute-start(bf16[3,18,16,128]{3,2,1,0:T(8,128)(2,1)S(1)} %get-tuple-element.82), channel_id=1, source_target_pairs={{4,8},{12,16},{20,24},{28,0},{8,4},{16,12},{24,20},{0,28},{5,9},{1... | collective-permute-start | bytes 663560 | tf_op jit(solution)/shard_map/ppermute | solution.py:423
  15.1 9.0 %collective-permute-start.7 = (bf16[2,64,128]{2,1,0:T(8,128)(2,1)S(1)}, bf16[2,64,128]{2,1,0:T(8,128)(2,1)S(1)}, u32[]{:S(2)}, u32[]{:S(2)}) collective-permute-start(bf16[2,64,128]{2,1,0:T(8,128)(2,1)S(1)} %get-tuple-element.92.refs_4_), channel_id=1, source_target_pairs={{0,3},{1,2},{2,1},{3,0},{4,7},{5,6},{6,5},{7,4},{8,11},{9,10},{10,... | collective-permute-start | bytes 98312 | tf_op jit(solution)/shard_map/ppermute | solution.py:406
  17.7 8.3 %collective-permute-start.8 = (bf16[2,64,128]{2,1,0:T(8,128)(2,1)S(1)}, bf16[2,64,128]{2,1,0:T(8,128)(2,1)S(1)}, u32[]{:S(2)}, u32[]{:S(2)}) collective-permute-start(bf16[2,64,128]{2,1,0:T(8,128)(2,1)S(1)} %get-tuple-element.92.refs_4_), channel_id=1, source_target_pairs={{0,2},{1,3},{2,0},{3,1},{4,6},{5,7},{6,4},{7,5},{8,10},{9,11},{10,... | collective-permute-start | bytes 98312 | tf_op jit(solution)/shard_map/ppermute | solution.py:406
  17.7 8.3 %collective-permute-start.9 = (bf16[2,64,128]{2,1,0:T(8,128)(2,1)S(1)}, bf16[2,64,128]{2,1,0:T(8,128)(2,1)S(1)}, u32[]{:S(2)}, u32[]{:S(2)}) collective-permute-start(bf16[2,64,128]{2,1,0:T(8,128)(2,1)S(1)} %get-tuple-element.92.refs_4_), channel_id=1, source_target_pairs={{0,1},{1,0},{2,3},{3,2},{4,5},{5,4},{6,7},{7,6},{8,9},{9,8},{10,11... | collective-permute-start | bytes 98312 | tf_op jit(solution)/shard_map/ppermute | solution.py:406
  21.5 5.8 %collective-permute-start.4 = (bf16[2,64,128]{2,1,0:T(8,128)(2,1)S(1)}, bf16[2,64,128]{2,1,0:T(8,128)(2,1)S(1)}, u32[]{:S(2)}, u32[]{:S(2)}) collective-permute-start(bf16[2,64,128]{2,1,0:T(8,128)(2,1)S(1)} %get-tuple-element.88.refs_0_), channel_id=1, source_target_pairs={{0,3},{1,2},{2,1},{3,0},{4,7},{5,6},{6,5},{7,4},{8,11},{9,10},{10,... | collective-permute-start | bytes 98312 | tf_op jit(solution)/shard_map/ppermute | solution.py:406
  24.1 4.8 %collective-permute-start.5 = (bf16[2,64,128]{2,1,0:T(8,128)(2,1)S(1)}, bf16[2,64,128]{2,1,0:T(8,128)(2,1)S(1)}, u32[]{:S(2)}, u32[]{:S(2)}) collective-permute-start(bf16[2,64,128]{2,1,0:T(8,128)(2,1)S(1)} %get-tuple-element.88.refs_0_), channel_id=1, source_target_pairs={{0,2},{1,3},{2,0},{3,1},{4,6},{5,7},{6,4},{7,5},{8,10},{9,11},{10,... | collective-permute-start | bytes 98312 | tf_op jit(solution)/shard_map/ppermute | solution.py:406
  24.1 4.8 %collective-permute-start.6 = (bf16[2,64,128]{2,1,0:T(8,128)(2,1)S(1)}, bf16[2,64,128]{2,1,0:T(8,128)(2,1)S(1)}, u32[]{:S(2)}, u32[]{:S(2)}) collective-permute-start(bf16[2,64,128]{2,1,0:T(8,128)(2,1)S(1)} %get-tuple-element.88.refs_0_), channel_id=1, source_target_pairs={{0,1},{1,0},{2,3},{3,2},{4,5},{5,4},{6,7},{7,6},{8,9},{9,8},{10,11... | collective-permute-start | bytes 98312 | tf_op jit(solution)/shard_map/ppermute | solution.py:406
  26.0 2.9 %copy-start.2 = (bf16[27,128,64]{1,2,0:T(8,128)(2,1)S(1)}, bf16[27,128,64]{1,2,0:T(8,128)(2,1)}, u32[]{:S(2)}) copy-start(bf16[27,128,64]{1,2,0:T(8,128)(2,1)} %param.6) | copy-start | bytes 1327108
  26.0 2.9 %copy-start.3 = (bf16[2,32,8,64]{3,2,1,0:T(8,128)(2,1)S(1)}, bf16[2,32,8,64]{3,2,1,0:T(8,128)(2,1)}, u32[]{:S(2)}) copy-start(bf16[2,32,8,64]{3,2,1,0:T(8,128)(2,1)} %refs_9_.1) | copy-start | bytes 196612
  31.0 6.1 %collective-permute-start.10 = (bf16[4,64,128]{2,1,0:T(8,128)(2,1)S(1)}, bf16[4,64,128]{2,1,0:T(8,128)(2,1)S(1)}, u32[]{:S(2)}, u32[]{:S(2)}) collective-permute-start(bf16[4,64,128]{2,1,0:T(8,128)(2,1)S(1)} %get-tuple-element.101), channel_id=1, source_target_pairs={{0,3},{1,2},{2,1},{3,0},{4,7},{5,6},{6,5},{7,4},{8,11},{9,10},{10,... | collective-permute-start | bytes 196616 | tf_op jit(solution)/shard_map/ppermute | solution.py:406
  32.9 5.9 %collective-permute-start.11 = (bf16[4,64,128]{2,1,0:T(8,128)(2,1)S(1)}, bf16[4,64,128]{2,1,0:T(8,128)(2,1)S(1)}, u32[]{:S(2)}, u32[]{:S(2)}) collective-permute-start(bf16[4,64,128]{2,1,0:T(8,128)(2,1)S(1)} %get-tuple-element.103), channel_id=1, source_target_pairs={{0,2},{1,3},{2,0},{3,1},{4,6},{5,7},{6,4},{7,5},{8,10},{9,11},{10,... | collective-permute-start | bytes 196616 | tf_op jit(solution)/shard_map/ppermute | solution.py:406
  33.6 5.2 %collective-permute-start.12 = (bf16[4,64,128]{2,1,0:T(8,128)(2,1)S(1)}, bf16[4,64,128]{2,1,0:T(8,128)(2,1)S(1)}, u32[]{:S(2)}, u32[]{:S(2)}) collective-permute-start(bf16[4,64,128]{2,1,0:T(8,128)(2,1)S(1)} %get-tuple-element.104), channel_id=1, source_target_pairs={{0,1},{1,0},{2,3},{3,2},{4,5},{5,4},{6,7},{7,6},{8,9},{9,8},{10,11... | collective-permute-start | bytes 196616 | tf_op jit(solution)/shard_map/ppermute | solution.py:406
  39.8 1.6 %collective-permute-start.13 = (bf16[4,240,128]{2,1,0:T(8,128)(2,1)S(1)}, bf16[4,240,128]{2,1,0:T(8,128)(2,1)S(1)}, u32[]{:S(2)}, u32[]{:S(2)}) collective-permute-start(bf16[4,240,128]{2,1,0:T(8,128)(2,1)S(1)} %get-tuple-element.109), channel_id=1, source_target_pairs={{0,4},{4,0},{8,12},{12,8},{16,20},{20,16},{24,28},{28,24},{1,5},{5... | collective-permute-start | bytes 737288 | tf_op jit(solution)/shard_map/ppermute | solution.py:413
  42.2 4.4 %collective-permute-start.14 = (bf16[4,416,128]{2,1,0:T(8,128)(2,1)S(1)}, bf16[4,416,128]{2,1,0:T(8,128)(2,1)S(1)}, u32[]{:S(2)}, u32[]{:S(2)}) collective-permute-start(bf16[4,416,128]{2,1,0:T(8,128)(2,1)S(1)} %early_grad_rest.1), channel_id=1, source_target_pairs={{0,4},{4,0},{8,12},{12,8},{16,20},{20,16},{24,28},{28,24},{1,5},{5... | collective-permute-start | bytes 1277960 | tf_op jit(solution)/shard_map/ppermute | solution.py:413
  42.4 5.3 %collective-permute-start.15 = (bf16[240,128]{1,0:T(8,128)(2,1)S(1)}, bf16[240,128]{1,0:T(8,128)(2,1)S(1)}, u32[]{:S(2)}, u32[]{:S(2)}) collective-permute-start(bf16[240,128]{1,0:T(8,128)(2,1)S(1)} %get-tuple-element.119), channel_id=1, source_target_pairs={{0,24},{4,28},{8,16},{12,20},{16,8},{20,12},{24,0},{28,4},{1,25},{... | collective-permute-start | bytes 184328 | tf_op jit(solution)/shard_map/ppermute | solution.py:406
  44.1 4.8 %collective-permute-start.16 = (bf16[240,128]{1,0:T(8,128)(2,1)S(1)}, bf16[240,128]{1,0:T(8,128)(2,1)S(1)}, u32[]{:S(2)}, u32[]{:S(2)}) collective-permute-start(bf16[240,128]{1,0:T(8,128)(2,1)S(1)} %get-tuple-element.120), channel_id=1, source_target_pairs={{0,16},{4,20},{8,24},{12,28},{16,0},{20,4},{24,8},{28,12},{1,17},{... | collective-permute-start | bytes 184328 | tf_op jit(solution)/shard_map/ppermute | solution.py:406
  45.0 4.2 %collective-permute-start.17 = (bf16[240,128]{1,0:T(8,128)(2,1)S(1)}, bf16[240,128]{1,0:T(8,128)(2,1)S(1)}, u32[]{:S(2)}, u32[]{:S(2)}) collective-permute-start(bf16[240,128]{1,0:T(8,128)(2,1)S(1)} %get-tuple-element.121), channel_id=1, source_target_pairs={{0,8},{4,12},{8,0},{12,4},{16,24},{20,28},{24,16},{28,20},{1,9},{5... | collective-permute-start | bytes 184328 | tf_op jit(solution)/shard_map/ppermute | solution.py:406
  49.3 6.5 %collective-permute-start.18 = (bf16[416,128]{1,0:T(8,128)(2,1)S(1)}, bf16[416,128]{1,0:T(8,128)(2,1)S(1)}, u32[]{:S(2)}, u32[]{:S(2)}) collective-permute-start(bf16[416,128]{1,0:T(8,128)(2,1)S(1)} %get-tuple-element.123), channel_id=1, source_target_pairs={{0,24},{4,28},{8,16},{12,20},{16,8},{20,12},{24,0},{28,4},{1,25},{... | collective-permute-start | bytes 319496 | tf_op jit(solution)/shard_map/ppermute | solution.py:406
  50.6 6.6 %collective-permute-start.19 = (bf16[416,128]{1,0:T(8,128)(2,1)S(1)}, bf16[416,128]{1,0:T(8,128)(2,1)S(1)}, u32[]{:S(2)}, u32[]{:S(2)}) collective-permute-start(bf16[416,128]{1,0:T(8,128)(2,1)S(1)} %get-tuple-element.124), channel_id=1, source_target_pairs={{0,16},{4,20},{8,24},{12,28},{16,0},{20,4},{24,8},{28,12},{1,17},{... | collective-permute-start | bytes 319496 | tf_op jit(solution)/shard_map/ppermute | solution.py:406
  51.6 5.7 %collective-permute-start.20 = (bf16[416,128]{1,0:T(8,128)(2,1)S(1)}, bf16[416,128]{1,0:T(8,128)(2,1)S(1)}, u32[]{:S(2)}, u32[]{:S(2)}) collective-permute-start(bf16[416,128]{1,0:T(8,128)(2,1)S(1)} %get-tuple-element.125), channel_id=1, source_target_pairs={{0,8},{4,12},{8,0},{12,4},{16,24},{20,28},{24,16},{28,20},{1,9},{5... | collective-permute-start | bytes 319496 | tf_op jit(solution)/shard_map/ppermute | solution.py:406
  52.8 7.2 %collective-permute-start.21 = (bf16[240,128]{1,0:T(8,128)(2,1)S(1)}, bf16[240,128]{1,0:T(8,128)(2,1)S(1)}, u32[]{:S(2)}, u32[]{:S(2)}) collective-permute-start(bf16[240,128]{1,0:T(8,128)(2,1)S(1)} %chip_sum.1.refs_0_), channel_id=1, source_target_pairs={{0,3},{1,2},{2,1},{3,0},{4,7},{5,6},{6,5},{7,4},{8,11},{9,10},{10,... | collective-permute-start | bytes 184328 | tf_op jit(solution)/shard_map/ppermute | solution.py:406
  55.5 6.3 %collective-permute-start.22 = (bf16[240,128]{1,0:T(8,128)(2,1)S(1)}, bf16[240,128]{1,0:T(8,128)(2,1)S(1)}, u32[]{:S(2)}, u32[]{:S(2)}) collective-permute-start(bf16[240,128]{1,0:T(8,128)(2,1)S(1)} %chip_sum.1.refs_0_), channel_id=1, source_target_pairs={{0,2},{1,3},{2,0},{3,1},{4,6},{5,7},{6,4},{7,5},{8,10},{9,11},{10,... | collective-permute-start | bytes 184328 | tf_op jit(solution)/shard_map/ppermute | solution.py:406
  55.7 6.0 %collective-permute-start.23 = (bf16[240,128]{1,0:T(8,128)(2,1)S(1)}, bf16[240,128]{1,0:T(8,128)(2,1)S(1)}, u32[]{:S(2)}, u32[]{:S(2)}) collective-permute-start(bf16[240,128]{1,0:T(8,128)(2,1)S(1)} %chip_sum.1.refs_0_), channel_id=1, source_target_pairs={{0,1},{1,0},{2,3},{3,2},{4,5},{5,4},{6,7},{7,6},{8,9},{9,8},{10,11... | collective-permute-start | bytes 184328 | tf_op jit(solution)/shard_map/ppermute | solution.py:406
  57.3 6.5 %collective-permute-start.24 = (bf16[192,128]{1,0:T(8,128)(2,1)S(1)}, bf16[192,128]{1,0:T(8,128)(2,1)S(1)}, u32[]{:S(2)}, u32[]{:S(2)}) collective-permute-start(bf16[192,128]{1,0:T(8,128)(2,1)S(1)} %get-tuple-element.143.refs_0_), channel_id=1, source_target_pairs={{0,3},{1,2},{2,1},{3,0},{4,7},{5,6},{6,5},{7,4},{8,11},{9,10},{10,... | collective-permute-start | bytes 147464 | tf_op jit(solution)/shard_map/ppermute | solution.py:406
  60.0 5.4 %collective-permute-start.25 = (bf16[192,128]{1,0:T(8,128)(2,1)S(1)}, bf16[192,128]{1,0:T(8,128)(2,1)S(1)}, u32[]{:S(2)}, u32[]{:S(2)}) collective-permute-start(bf16[192,128]{1,0:T(8,128)(2,1)S(1)} %get-tuple-element.143.refs_0_), channel_id=1, source_target_pairs={{0,2},{1,3},{2,0},{3,1},{4,6},{5,7},{6,4},{7,5},{8,10},{9,11},{10,... | collective-permute-start | bytes 147464 | tf_op jit(solution)/shard_map/ppermute | solution.py:406
  60.0 5.3 %collective-permute-start.26 = (bf16[192,128]{1,0:T(8,128)(2,1)S(1)}, bf16[192,128]{1,0:T(8,128)(2,1)S(1)}, u32[]{:S(2)}, u32[]{:S(2)}) collective-permute-start(bf16[192,128]{1,0:T(8,128)(2,1)S(1)} %get-tuple-element.143.refs_0_), channel_id=1, source_target_pairs={{0,1},{1,0},{2,3},{3,2},{4,5},{5,4},{6,7},{7,6},{8,9},{9,8},{10,11... | collective-permute-start | bytes 147464 | tf_op jit(solution)/shard_map/ppermute | solution.py:406
  61.8 6.1 %collective-permute-start.27 = (bf16[464,128]{1,0:T(8,128)(2,1)S(1)}, bf16[464,128]{1,0:T(8,128)(2,1)S(1)}, u32[]{:S(2)}, u32[]{:S(2)}) collective-permute-start(bf16[464,128]{1,0:T(8,128)(2,1)S(1)} %filt_sum.1.refs_0_), channel_id=1, source_target_pairs={{0,8},{4,12},{8,0},{12,4},{16,24},{20,28},{24,16},{28,20},{1,9},{5... | collective-permute-start | bytes 356360 | tf_op jit(solution)/shard_map/ppermute | solution.py:406
  62.8 9.2 %collective-permute-start.28 = (bf16[464,128]{1,0:T(8,128)(2,1)S(1)}, bf16[464,128]{1,0:T(8,128)(2,1)S(1)}, u32[]{:S(2)}, u32[]{:S(2)}) collective-permute-start(bf16[464,128]{1,0:T(8,128)(2,1)S(1)} %filt_sum.1.refs_0_), channel_id=1, source_target_pairs={{0,16},{4,20},{8,24},{12,28},{16,0},{20,4},{24,8},{28,12},{1,17},{... | collective-permute-start | bytes 356360 | tf_op jit(solution)/shard_map/ppermute | solution.py:406
  63.8 8.2 %collective-permute-start.29 = (bf16[464,128]{1,0:T(8,128)(2,1)S(1)}, bf16[464,128]{1,0:T(8,128)(2,1)S(1)}, u32[]{:S(2)}, u32[]{:S(2)}) collective-permute-start(bf16[464,128]{1,0:T(8,128)(2,1)S(1)} %filt_sum.1.refs_0_), channel_id=1, source_target_pairs={{0,24},{4,28},{8,16},{12,20},{16,8},{20,12},{24,0},{28,4},{1,25},{... | collective-permute-start | bytes 356360 | tf_op jit(solution)/shard_map/ppermute | solution.py:406
  65.4 6.6 %collective-permute-start.31 = (bf16[192,128]{1,0:T(8,128)(2,1)S(1)}, bf16[192,128]{1,0:T(8,128)(2,1)S(1)}, u32[]{:S(2)}, u32[]{:S(2)}) collective-permute-start(bf16[192,128]{1,0:T(8,128)(2,1)S(1)} %filt_sum_rest.1.refs_4_), channel_id=1, source_target_pairs={{0,16},{4,20},{8,24},{12,28},{16,0},{20,4},{24,8},{28,12},{1,17},{... | collective-permute-start | bytes 147464 | tf_op jit(solution)/shard_map/ppermute | solution.py:406
  66.5 5.5 %collective-permute-start.32 = (bf16[192,128]{1,0:T(8,128)(2,1)S(1)}, bf16[192,128]{1,0:T(8,128)(2,1)S(1)}, u32[]{:S(2)}, u32[]{:S(2)}) collective-permute-start(bf16[192,128]{1,0:T(8,128)(2,1)S(1)} %filt_sum_rest.1.refs_4_), channel_id=1, source_target_pairs={{0,24},{4,28},{8,16},{12,20},{16,8},{20,12},{24,0},{28,4},{1,25},{... | collective-permute-start | bytes 147464 | tf_op jit(solution)/shard_map/ppermute | solution.py:406
  67.9 4.1 %collective-permute-start.30 = (bf16[192,128]{1,0:T(8,128)(2,1)S(1)}, bf16[192,128]{1,0:T(8,128)(2,1)S(1)}, u32[]{:S(2)}, u32[]{:S(2)}) collective-permute-start(bf16[192,128]{1,0:T(8,128)(2,1)S(1)} %filt_sum_rest.1.refs_4_), channel_id=1, source_target_pairs={{0,8},{4,12},{8,0},{12,4},{16,24},{20,28},{24,16},{28,20},{1,9},{5... | collective-permute-start | bytes 147464 | tf_op jit(solution)/shard_map/ppermute | solution.py:406
  72.1 2.2 %collective-permute-start.33 = (bf16[4,656,128]{2,1,0:T(8,128)(2,1)S(1)}, bf16[4,656,128]{2,1,0:T(8,128)(2,1)S(1)}, u32[]{:S(2)}, u32[]{:S(2)}) collective-permute-start(bf16[4,656,128]{2,1,0:T(8,128)(2,1)S(1)} %stack.1.pieces), channel_id=1, source_target_pairs={{0,4},{4,0},{8,12},{12,8},{16,20},{20,16},{24,28},{28,24},{1,5},{5... | collective-permute-start | bytes 2015240 | tf_op jit(solution)/shard_map/ppermute | solution.py:413

commit v3 on v2

--- a/solution.py
+++ b/solution.py
@@ -92,13 +92,12 @@
     field[:, :, 8 + nz : 16 + nz] = jnp.zeros((count, wide_y, 8, cin), F32)
 
 
-def early_rows_of(windows, start, wide, ny, keep):
-    rows = windows.shape[2]
+def early_rows_of(row_of, rows, wide, ny, keep):
     cout = wide.shape[2] // 2
     acc = jnp.zeros((2 * rows, 2 * cout), F32)
     for ab in range(9):
         a, b = ab // 3, ab % 3
-        left = windows[b, pl.ds(start + a, 2)].reshape(2 * rows, windows.shape[3])
+        left = jnp.concatenate([row_of(b, a), row_of(b, a + 1)], axis=0)
         acc = acc + jnp.dot(left, wide[ab], preferred_element_type=F32)
     sig = sigmoid(acc)
     slope = (sig * (1.0 + acc * (1.0 - sig)) * keep).reshape(2, rows, 2 * cout)
@@ -131,27 +130,44 @@
     field[pl.ds((1 - odd) * nx, 3), :, cells] = near[...].astype(F32)
     fill_windows(field, windows)
     for chunk in range(nx // 2):
-        slope, pool = early_rows_of(windows, 1 - odd + 2 * chunk, wide, ny, 0.125)
+        start = 1 - odd + 2 * chunk
+        slope, pool = early_rows_of(
+            lambda b, i: windows[b, start + i], windows.shape[2], wide, ny, 0.125
+        )
         sg[2 * chunk : 2 * chunk + 2] = slope
         pooled[chunk] = pool
 
 
-def far_body(windows, far, wide, far_windows, sg, pooled, field, held):
+def far_body(windows, far, wide, far_windows, sg, pooled, field):
     _, wide_y, nz, _ = far.shape
+    rows = windows.shape[2]
     odd = lax.rem(lax.axis_index("space"), 2)
     clear_ends(field, nz)
     inside = jnp.where(has_both("space"), 1.0, 0.0).astype(F32)
     field[:, :, 8 : 8 + nz] = far[...].astype(F32) * inside
     fill_windows(field, far_windows)
-    for b in range(3):
-        held[b, pl.ds(3 * odd, 3)] = far_windows[b]
-        held[b, pl.ds(3 - 3 * odd, 3)] = windows[b, pl.ds(4 * odd, 3)]
-    first = jnp.where(odd == 0, inside, 1.0)
-    second = jnp.where(odd == 1, inside, 1.0)
-    for chunk, flag in enumerate((first, second)):
-        slope, pool = early_rows_of(held, 2 * chunk, wide, wide_y - 2, 0.125 * flag)
-        sg[2 * chunk : 2 * chunk + 2] = slope
-        pooled[chunk] = pool
+
+    def rows_for(parity):
+        for chunk in range(2):
+
+            def row_of(b, i):
+                spot = 2 * chunk + i
+                if (spot < 3) == (parity == 0):
+                    return far_windows[b, spot % 3]
+                return windows[b, spot % 3 + 4 * parity]
+
+            keep = 0.125 * inside if chunk == parity else 0.125
+            slope, pool = early_rows_of(row_of, rows, wide, wide_y - 2, keep)
+            sg[2 * chunk : 2 * chunk + 2] = slope
+            pooled[chunk] = pool
+
+    @pl.when(odd == 0)
+    def _():
+        rows_for(0)
+
+    @pl.when(odd == 1)
+    def _():
+        rows_for(1)
 
 
 def transpose_body(windows, far_windows, turned):
@@ -213,19 +229,19 @@
                 )
     slopes[:, 0:1] = jnp.zeros((nx, 1, nz, filters), F32)
     slopes[:, ny + 1 :] = jnp.zeros((nx, 1, nz, filters), F32)
-    for x in range(nx):
-        acc = jnp.zeros((rows, filters), F32)
-        for ab in range(9):
-            a, b = ab // 3, ab % 3
-            acc = acc + lax.dot_general(
-                windows[b, x + a], wide[ab], (((1,), (1,)), ((), ())), preferred_element_type=F32
-            )
-        sig = sigmoid(acc)
-        block_out[x] = (acc * sig).reshape(ny, nz, filters).astype(BF16)
-        slope = sig * (1.0 + acc * (1.0 - sig))
-        value = (cot[x].astype(F32).reshape(rows, filters) * slope).astype(BF16)
-        grad[x] = value
-        slopes[x, 1 : ny + 1] = value.astype(F32).reshape(ny, nz, filters)
+    acc = jnp.zeros((nx * rows, filters), F32)
+    for ab in range(9):
+        a, b = ab // 3, ab % 3
+        left = windows[b, a : a + nx].reshape(nx * rows, 3 * width)
+        acc = acc + lax.dot_general(
+            left, wide[ab], (((1,), (1,)), ((), ())), preferred_element_type=F32
+        )
+    sig = sigmoid(acc)
+    block_out[...] = (acc * sig).reshape(nx, ny, nz, filters).astype(BF16)
+    slope = sig * (1.0 + acc * (1.0 - sig))
+    value = (cot[...].astype(F32).reshape(nx * rows, filters) * slope).astype(BF16)
+    grad[...] = value.reshape(nx, rows, filters)
+    slopes[:, 1 : ny + 1] = value.astype(F32).reshape(nx, ny, nz, filters)
     for x in range(nx):
         plane = slopes[x]
         plane = jnp.concatenate([roll_z(plane, -1), plane, roll_z(plane, 1)], axis=2)
@@ -233,13 +249,15 @@
             turned[b, x] = (
                 plane[2 - b : 2 - b + ny].reshape(rows, 3 * filters).astype(BF16)
             )
+    shares = []
+    for a in range(3):
+        total = jnp.zeros((nx * rows, width), F32)
+        for b in range(3):
+            left = turned[b].reshape(nx * rows, 3 * filters)
+            total = total + jnp.dot(left, wt[3 * a + b], preferred_element_type=F32)
+        shares.append(total.reshape(nx, ny, nz, width))
     for r in range(nx + 2):
-        total = jnp.zeros((rows, width), F32)
-        for ab in range(9):
-            a, b = ab // 3, ab % 3
-            if 0 <= r - a < nx:
-                total = total + jnp.dot(turned[b, r - a], wt[ab], preferred_element_type=F32)
-        terms[r] = total.reshape(ny, nz, width)
+        terms[r] = sum(shares[a][r - a] for a in range(3) if 0 <= r - a < nx)
     for j in range(parts_n):
         spot = lax.bitwise_xor(mine, j) * py
         value = terms[:, pl.ds(spot, py)]
@@ -472,7 +490,6 @@
         (windows, far, wide),
         [
             pltpu.VMEM((3, ny + 2, nz + 16, cin), F32),
-            pltpu.VMEM((3, 6, rows, 4 * cin), BF16),
         ],
         flops=2 * nx * rows * 36 * cin * 2 * width,
     )

time: 75.6 us -> 77 us (1.019)
  Pallas kernels: 14.1 us -> 15.3 us
    pallas_call x20, Pallas kernels: 14.1 us -> 15.3 us  [call(): pl.pallas_call(body, name=name, out_shape=out_shape, in_specs=[HBM if i i...]
  transfers between devices with their start and end apart: 34 -> 34, of which waited for: 12 -> 15; matrix products, arithmetic and copies ran while one was open for 0% -> 0% of each run, Pallas kernels for 12% -> 12%
where the time goes in v3:
time: 77 us; the launch traced here: 76.9 us
  starting transfers between devices  44.3 us (58%)
  waiting for transfers between devices  15.5 us (20%)
  Pallas kernels  15.3 us (20%)
  between operations  0.99 us (1%)
    ppermute x27, starting transfers between devices, paired(): lax.ppermute(values[j], axis, [(i, i ^ step * j) for i in range(count)])  35.7 us
    pallas_call x20, Pallas kernels, call(): pl.pallas_call(body, name=name, out_shape=out_shape, in_specs=[HBM if i i...  15.3 us
    ppermute x27, waiting for transfers between devices, paired(): lax.ppermute(values[j], axis, [(i, i ^ step * j) for i in range(count)])  10.7 us
    ppermute x4, starting transfers between devices, swap(): return lax.ppermute(value, axis, pairs + [(b, a) for a, b in pairs])  8.18 us
    ppermute x4, waiting for transfers between devices, swap(): return lax.ppermute(value, axis, pairs + [(b, a) for a, b in pairs])  3.24 us
    ppermute x3, waiting for transfers between devices, exchange(): lax.ppermute(value, axis, [(i, i ^ step) for i in range(lax.axis_size(axi...  1.6 us
  transfers between devices with their start and end apart: 34, of which 15 were waited for; matrix products, arithmetic and copies ran while one was open for 0% of the time, Pallas kernels for 12%

profile of v3, /device:TPU:0, one launch (start us, length us, event | category | flops | bytes accessed | tf_op | source)
XLA Modules:
  0.0 76.9 jit_solution(18127058424582413727)
XLA Ops:
  0.6 0.7 fusion
  1.4 3.1 %collective-permute-start = (bf16[4,2,16,128]{3,2,1,0:T(8,128)(2,1)S(1)}, bf16[4,2,16,128]{3,2,1,0:T(8,128)(2,1)S(1)}, u32[]{:S(2)}, u32[]{:S(2)}) collective-permute-start(bf16[4,2,16,128]{3,2,1,0:T(8,128)(2,1)S(1)} %edges.1), channel_id=1, source_target_pairs={{0,1},{2,3},{1,0},{3,2},{4,5},{6,7},{5,4},{7,6},{8,9},{10,11},{9,8... | collective-permute-start | bytes 98312 | tf_op jit(solution)/shard_map/ppermute | solution.py:441
  4.5 2.5 %collective-permute-start.1 = (bf16[4,2,16,128]{3,2,1,0:T(8,128)(2,1)S(1)}, bf16[4,2,16,128]{3,2,1,0:T(8,128)(2,1)S(1)}, u32[]{:S(2)}, u32[]{:S(2)}) collective-permute-start(bf16[4,2,16,128]{3,2,1,0:T(8,128)(2,1)S(1)} %edges.1), channel_id=1, source_target_pairs={{1,2},{3,0},{2,1},{0,3},{5,6},{7,4},{6,5},{4,7},{9,10},{11,8},{10,... | collective-permute-start | bytes 98312 | tf_op jit(solution)/shard_map/ppermute | solution.py:441
  7.0 3.2 %collective-permute-done.1.yodd = bf16[4,2,16,128]{3,2,1,0:T(8,128)(2,1)S(1)} collective-permute-done((bf16[4,2,16,128]{3,2,1,0:T(8,128)(2,1)S(1)}, bf16[4,2,16,128]{3,2,1,0:T(8,128)(2,1)S(1)}, u32[]{:S(2)}, u32[]{:S(2)}) %collective-permute-start.1) | collective-permute-done | bytes 32800 | tf_op jit(solution)/shard_map/ppermute | solution.py:441
  10.4 2.5 %collective-permute-start.3 = (bf16[3,18,16,128]{3,2,1,0:T(8,128)(2,1)S(1)}, bf16[3,18,16,128]{3,2,1,0:T(8,128)(2,1)S(1)}, u32[]{:S(2)}, u32[]{:S(2)}) collective-permute-start(bf16[3,18,16,128]{3,2,1,0:T(8,128)(2,1)S(1)} %get-tuple-element.82), channel_id=1, source_target_pairs={{4,8},{12,16},{20,24},{28,0},{8,4},{16,12},{24,20},{0,28},{5,9},{1... | collective-permute-start | bytes 663560 | tf_op jit(solution)/shard_map/ppermute | solution.py:441
  12.9 2.2 %early_near.1 = (bf16[3,7,128,512]{3,2,1,0:T(8,128)(2,1)S(1)}, f32[4,128,256]{2,1,0:T(8,128)S(1)}, bf16[2,64,128]{2,1,0:T(8,128)(2,1)S(1)}, bf16[9,512,256]{2,1,0:T(8,128)(2,1)S(1)}) custom-call(bf16[4,16,16,128]{3,2,1,0:T(8,128)(2,1)S(1)} %get-tuple-element.78.center, bf16[4,2,16,128]{3,2,1,0:T(8,128)(2,1)S(1)} %get-tuple-element.79.sides, ...), custom_call_target="tpu_custom_call" | custom-call | flops 1207959552 | bytes 1048576 | tf_op jit(solution)/shard_map/early_near/pallas_call | solution.py:23
  15.1 2.5 %collective-permute-start.7 = (bf16[2,64,128]{2,1,0:T(8,128)(2,1)S(1)}, bf16[2,64,128]{2,1,0:T(8,128)(2,1)S(1)}, u32[]{:S(2)}, u32[]{:S(2)}) collective-permute-start(bf16[2,64,128]{2,1,0:T(8,128)(2,1)S(1)} %get-tuple-element.92.refs_4_), channel_id=1, source_target_pairs={{0,3},{1,2},{2,1},{3,0},{4,7},{5,6},{6,5},{7,4},{8,11},{9,10},{10,... | collective-permute-start | bytes 98312 | tf_op jit(solution)/shard_map/ppermute | solution.py:424
  17.7 1.9 %collective-permute-start.9 = (bf16[2,64,128]{2,1,0:T(8,128)(2,1)S(1)}, bf16[2,64,128]{2,1,0:T(8,128)(2,1)S(1)}, u32[]{:S(2)}, u32[]{:S(2)}) collective-permute-start(bf16[2,64,128]{2,1,0:T(8,128)(2,1)S(1)} %get-tuple-element.92.refs_4_), channel_id=1, source_target_pairs={{0,1},{1,0},{2,3},{3,2},{4,5},{5,4},{6,7},{7,6},{8,9},{9,8},{10,11... | collective-permute-start | bytes 98312 | tf_op jit(solution)/shard_map/ppermute | solution.py:424
  19.6 2.0 %early_far.1 = (bf16[3,3,128,512]{3,2,1,0:T(8,128)(2,1)S(1)}, f32[4,128,256]{2,1,0:T(8,128)S(1)}, bf16[2,64,128]{2,1,0:T(8,128)(2,1)S(1)}) custom-call(bf16[3,7,128,512]{3,2,1,0:T(8,128)(2,1)S(1)} %get-tuple-element.86.windows, bf16[3,18,16,128]{3,2,1,0:T(8,128)(2,1)S(1)} %collective-permute-done.3.far, bf16[9,512,256]{2,1,0:T(8,128)(2,1)S(1)} %get-tuple-element.83.wide), custom_call_target="tpu_custom_call" | custom-call | flops 1207959552 | bytes 1048576 | tf_op jit(solution)/shard_map/early_far/pallas_call | solution.py:23
  21.6 2.5 %collective-permute-start.4 = (bf16[2,64,128]{2,1,0:T(8,128)(2,1)S(1)}, bf16[2,64,128]{2,1,0:T(8,128)(2,1)S(1)}, u32[]{:S(2)}, u32[]{:S(2)}) collective-permute-start(bf16[2,64,128]{2,1,0:T(8,128)(2,1)S(1)} %get-tuple-element.88.refs_0_), channel_id=1, source_target_pairs={{0,3},{1,2},{2,1},{3,0},{4,7},{5,6},{6,5},{7,4},{8,11},{9,10},{10,... | collective-permute-start | bytes 98312 | tf_op jit(solution)/shard_map/ppermute | solution.py:424
  24.1 1.9 %collective-permute-start.6 = (bf16[2,64,128]{2,1,0:T(8,128)(2,1)S(1)}, bf16[2,64,128]{2,1,0:T(8,128)(2,1)S(1)}, u32[]{:S(2)}, u32[]{:S(2)}) collective-permute-start(bf16[2,64,128]{2,1,0:T(8,128)(2,1)S(1)} %get-tuple-element.88.refs_0_), channel_id=1, source_target_pairs={{0,1},{1,0},{2,3},{3,2},{4,5},{5,4},{6,7},{7,6},{8,9},{9,8},{10,11... | collective-permute-start | bytes 98312 | tf_op jit(solution)/shard_map/ppermute | solution.py:424
  26.1 1.1 %turn_windows.1.refs_6_.refs_1_ = bf16[3,2,256,1280]{3,2,1,0:T(8,128)(2,1)S(1)} custom-call(bf16[3,7,128,512]{3,2,1,0:T(8,128)(2,1)S(1)} %get-tuple-element.86.windows, bf16[3,3,128,512]{3,2,1,0:T(8,128)(2,1)S(1)} %get-tuple-element.87.far_windows), custom_call_target="tpu_custom_call" | custom-call | flops 1073741824 | bytes 1048576 | tf_op jit(solution)/shard_map/turn_windows/pallas_call | solution.py:23
  27.4 1.6 %collective-permute-done.5.refs_2_ = bf16[2,64,128]{2,1,0:T(8,128)(2,1)S(1)} collective-permute-done((bf16[2,64,128]{2,1,0:T(8,128)(2,1)S(1)}, bf16[2,64,128]{2,1,0:T(8,128)(2,1)S(1)}, u32[]{:S(2)}, u32[]{:S(2)}) %collective-permute-start.5) | collective-permute-done | bytes 32800 | tf_op jit(solution)/shard_map/ppermute | solution.py:424
  29.0 3.3 %deep_conv.1 = (bf16[2,32,8,64]{3,2,1,0:T(8,128)(2,1)}, bf16[2,256,64]{2,1,0:T(8,128)(2,1)S(1)}, bf16[3,4,256,384]{3,2,1,0:T(8,128)(2,1)S(1)}, f32[4,64,128]{2,1...) custom-call(bf16[2,64,128]{2,1,0:T(8,128)(2,1)S(1)} %get-tuple-eleme, ...), custom_call_target="tpu_custom_call" | custom-call | flops 452984832 | bytes 1048576 | tf_op jit(solution)/shard_map/deep_conv/pallas_call | solution.py:23
  32.2 1.9 %collective-permute-start.10 = (bf16[4,64,128]{2,1,0:T(8,128)(2,1)S(1)}, bf16[4,64,128]{2,1,0:T(8,128)(2,1)S(1)}, u32[]{:S(2)}, u32[]{:S(2)}) collective-permute-start(bf16[4,64,128]{2,1,0:T(8,128)(2,1)S(1)} %get-tuple-element.101), channel_id=1, source_target_pairs={{0,3},{1,2},{2,1},{3,0},{4,7},{5,6},{6,5},{7,4},{8,11},{9,10},{10,... | collective-permute-start | bytes 196616 | tf_op jit(solution)/shard_map/ppermute | solution.py:424
  34.1 0.7 collective-permute-start.11
  34.8 1.9 %collective-permute-start.12 = (bf16[4,64,128]{2,1,0:T(8,128)(2,1)S(1)}, bf16[4,64,128]{2,1,0:T(8,128)(2,1)S(1)}, u32[]{:S(2)}, u32[]{:S(2)}) collective-permute-start(bf16[4,64,128]{2,1,0:T(8,128)(2,1)S(1)} %get-tuple-element.104), channel_id=1, source_target_pairs={{0,1},{1,0},{2,3},{3,2},{4,5},{5,4},{6,7},{7,6},{8,9},{9,8},{10,11... | collective-permute-start | bytes 196616 | tf_op jit(solution)/shard_map/ppermute | solution.py:424
  36.7 0.7 deep_grad.1
  37.4 0.9 %collective-permute-done.10.refs_1_ = bf16[4,64,128]{2,1,0:T(8,128)(2,1)S(1)} collective-permute-done((bf16[4,64,128]{2,1,0:T(8,128)(2,1)S(1)}, bf16[4,64,128]{2,1,0:T(8,128)(2,1)S(1)}, u32[]{:S(2)}, u32[]{:S(2)}) %collective-permute-start.10) | collective-permute-done | bytes 65568 | tf_op jit(solution)/shard_map/ppermute | solution.py:424
  38.4 1.6 %collective-permute-done.11.refs_2_ = bf16[4,64,128]{2,1,0:T(8,128)(2,1)S(1)} collective-permute-done((bf16[4,64,128]{2,1,0:T(8,128)(2,1)S(1)}, bf16[4,64,128]{2,1,0:T(8,128)(2,1)S(1)}, u32[]{:S(2)}, u32[]{:S(2)}) %collective-permute-start.11) | collective-permute-done | bytes 65568 | tf_op jit(solution)/shard_map/ppermute | solution.py:424
  40.0 1.0 %early_grad.1 = (bf16[4,240,128]{2,1,0:T(8,128)(2,1)S(1)}, bf16[8,128,256]{2,1,0:T(8,128)(2,1)S(1)}) custom-call(f32[4,64,128]{2,1,0:T(8,128)S(1)} %get-tuple-element.97.refs_0_, bf16[4,64,128]{2,1,0:T(8,128)(2,1)S(1)} %collective-permute-done.10.refs_1_, bf16[4,64,128]{2,1,0:T(8,128)(2,1)S(1)} %collective-permute-done.11.refs_2_, ...), custom_call_target="tpu_custom_call" | custom-call | flops 1207959552 | bytes 1048576 | tf_op jit(solution)/shard_map/early_grad/pallas_call | solution.py:23
  41.1 0.8 %early_grad_own.1.mine = f32[4,240,128]{2,1,0:T(8,128)S(1)} custom-call(bf16[8,128,256]{2,1,0:T(8,128)(2,1)S(1)} %get-tuple-element.111.refs_0_, bf16[3,2,256,1280]{3,2,1,0:T(8,128)(2,1)S(1)} %turn_windows.1.refs_6_.refs_1_), custom_call_target="tpu_custom_call" | custom-call | flops 1207959552 | bytes 1048576 | tf_op jit(solution)/shard_map/early_grad_own/pallas_call | solution.py:23
  42.0 0.6 collective-permute-done.13.other
  42.7 0.7 early_grad_rest.1
  43.6 1.4 %collective-permute-start.15 = (bf16[240,128]{1,0:T(8,128)(2,1)S(1)}, bf16[240,128]{1,0:T(8,128)(2,1)S(1)}, u32[]{:S(2)}, u32[]{:S(2)}) collective-permute-start(bf16[240,128]{1,0:T(8,128)(2,1)S(1)} %get-tuple-element.119), channel_id=1, source_target_pairs={{0,24},{4,28},{8,16},{12,20},{16,8},{20,12},{24,0},{28,4},{1,25},{... | collective-permute-start | bytes 184328 | tf_op jit(solution)/shard_map/ppermute | solution.py:424
  45.0 1.3 %collective-permute-start.16 = (bf16[240,128]{1,0:T(8,128)(2,1)S(1)}, bf16[240,128]{1,0:T(8,128)(2,1)S(1)}, u32[]{:S(2)}, u32[]{:S(2)}) collective-permute-start(bf16[240,128]{1,0:T(8,128)(2,1)S(1)} %get-tuple-element.120), channel_id=1, source_target_pairs={{0,16},{4,20},{8,24},{12,28},{16,0},{20,4},{24,8},{28,12},{1,17},{... | collective-permute-start | bytes 184328 | tf_op jit(solution)/shard_map/ppermute | solution.py:424
  46.3 0.8 %collective-permute-start.17 = (bf16[240,128]{1,0:T(8,128)(2,1)S(1)}, bf16[240,128]{1,0:T(8,128)(2,1)S(1)}, u32[]{:S(2)}, u32[]{:S(2)}) collective-permute-start(bf16[240,128]{1,0:T(8,128)(2,1)S(1)} %get-tuple-element.121), channel_id=1, source_target_pairs={{0,8},{4,12},{8,0},{12,4},{16,24},{20,28},{24,16},{28,20},{1,9},{5... | collective-permute-start | bytes 184328 | tf_op jit(solution)/shard_map/ppermute | solution.py:424
  47.1 0.7 early_grad_rest_own.1.mine
  47.9 1.0 %collective-permute-done.15.refs_1_ = bf16[240,128]{1,0:T(8,128)(2,1)S(1)} collective-permute-done((bf16[240,128]{1,0:T(8,128)(2,1)S(1)}, bf16[240,128]{1,0:T(8,128)(2,1)S(1)}, u32[]{:S(2)}, u32[]{:S(2)}) %collective-permute-start.15) | collective-permute-done | bytes 61472 | tf_op jit(solution)/shard_map/ppermute | solution.py:424
  48.9 1.2 %collective-permute-done.16.refs_2_ = bf16[240,128]{1,0:T(8,128)(2,1)S(1)} collective-permute-done((bf16[240,128]{1,0:T(8,128)(2,1)S(1)}, bf16[240,128]{1,0:T(8,128)(2,1)S(1)}, u32[]{:S(2)}, u32[]{:S(2)}) %collective-permute-start.16) | collective-permute-done | bytes 61472 | tf_op jit(solution)/shard_map/ppermute | solution.py:424
  50.5 1.3 %collective-permute-start.18 = (bf16[416,128]{1,0:T(8,128)(2,1)S(1)}, bf16[416,128]{1,0:T(8,128)(2,1)S(1)}, u32[]{:S(2)}, u32[]{:S(2)}) collective-permute-start(bf16[416,128]{1,0:T(8,128)(2,1)S(1)} %get-tuple-element.123), channel_id=1, source_target_pairs={{0,24},{4,28},{8,16},{12,20},{16,8},{20,12},{24,0},{28,4},{1,25},{... | collective-permute-start | bytes 319496 | tf_op jit(solution)/shard_map/ppermute | solution.py:424
  51.8 1.0 %collective-permute-start.19 = (bf16[416,128]{1,0:T(8,128)(2,1)S(1)}, bf16[416,128]{1,0:T(8,128)(2,1)S(1)}, u32[]{:S(2)}, u32[]{:S(2)}) collective-permute-start(bf16[416,128]{1,0:T(8,128)(2,1)S(1)} %get-tuple-element.124), channel_id=1, source_target_pairs={{0,16},{4,20},{8,24},{12,28},{16,0},{20,4},{24,8},{28,12},{1,17},{... | collective-permute-start | bytes 319496 | tf_op jit(solution)/shard_map/ppermute | solution.py:424
  52.8 1.2 %collective-permute-start.20 = (bf16[416,128]{1,0:T(8,128)(2,1)S(1)}, bf16[416,128]{1,0:T(8,128)(2,1)S(1)}, u32[]{:S(2)}, u32[]{:S(2)}) collective-permute-start(bf16[416,128]{1,0:T(8,128)(2,1)S(1)} %get-tuple-element.125), channel_id=1, source_target_pairs={{0,8},{4,12},{8,0},{12,4},{16,24},{20,28},{24,16},{28,20},{1,9},{5... | collective-permute-start | bytes 319496 | tf_op jit(solution)/shard_map/ppermute | solution.py:424
  54.0 2.7 %collective-permute-start.21 = (bf16[240,128]{1,0:T(8,128)(2,1)S(1)}, bf16[240,128]{1,0:T(8,128)(2,1)S(1)}, u32[]{:S(2)}, u32[]{:S(2)}) collective-permute-start(bf16[240,128]{1,0:T(8,128)(2,1)S(1)} %chip_sum.1.refs_0_), channel_id=1, source_target_pairs={{0,3},{1,2},{2,1},{3,0},{4,7},{5,6},{6,5},{7,4},{8,11},{9,10},{10,... | collective-permute-start | bytes 184328 | tf_op jit(solution)/shard_map/ppermute | solution.py:424
  57.2 1.3 %collective-permute-start.23 = (bf16[240,128]{1,0:T(8,128)(2,1)S(1)}, bf16[240,128]{1,0:T(8,128)(2,1)S(1)}, u32[]{:S(2)}, u32[]{:S(2)}) collective-permute-start(bf16[240,128]{1,0:T(8,128)(2,1)S(1)} %chip_sum.1.refs_0_), channel_id=1, source_target_pairs={{0,1},{1,0},{2,3},{3,2},{4,5},{5,4},{6,7},{7,6},{8,9},{9,8},{10,11... | collective-permute-start | bytes 184328 | tf_op jit(solution)/shard_map/ppermute | solution.py:424
  58.5 2.7 %collective-permute-start.24 = (bf16[192,128]{1,0:T(8,128)(2,1)S(1)}, bf16[192,128]{1,0:T(8,128)(2,1)S(1)}, u32[]{:S(2)}, u32[]{:S(2)}) collective-permute-start(bf16[192,128]{1,0:T(8,128)(2,1)S(1)} %get-tuple-element.143.refs_0_), channel_id=1, source_target_pairs={{0,3},{1,2},{2,1},{3,0},{4,7},{5,6},{6,5},{7,4},{8,11},{9,10},{10,... | collective-permute-start | bytes 147464 | tf_op jit(solution)/shard_map/ppermute | solution.py:424
  61.2 1.7 %collective-permute-start.26 = (bf16[192,128]{1,0:T(8,128)(2,1)S(1)}, bf16[192,128]{1,0:T(8,128)(2,1)S(1)}, u32[]{:S(2)}, u32[]{:S(2)}) collective-permute-start(bf16[192,128]{1,0:T(8,128)(2,1)S(1)} %get-tuple-element.143.refs_0_), channel_id=1, source_target_pairs={{0,1},{1,0},{2,3},{3,2},{4,5},{5,4},{6,7},{7,6},{8,9},{9,8},{10,11... | collective-permute-start | bytes 147464 | tf_op jit(solution)/shard_map/ppermute | solution.py:424
  63.2 0.8 %collective-permute-start.27 = (bf16[464,128]{1,0:T(8,128)(2,1)S(1)}, bf16[464,128]{1,0:T(8,128)(2,1)S(1)}, u32[]{:S(2)}, u32[]{:S(2)}) collective-permute-start(bf16[464,128]{1,0:T(8,128)(2,1)S(1)} %filt_sum.1.refs_0_), channel_id=1, source_target_pairs={{0,8},{4,12},{8,0},{12,4},{16,24},{20,28},{24,16},{28,20},{1,9},{5... | collective-permute-start | bytes 356360 | tf_op jit(solution)/shard_map/ppermute | solution.py:424
  64.0 1.0 %collective-permute-start.28 = (bf16[464,128]{1,0:T(8,128)(2,1)S(1)}, bf16[464,128]{1,0:T(8,128)(2,1)S(1)}, u32[]{:S(2)}, u32[]{:S(2)}) collective-permute-start(bf16[464,128]{1,0:T(8,128)(2,1)S(1)} %filt_sum.1.refs_0_), channel_id=1, source_target_pairs={{0,16},{4,20},{8,24},{12,28},{16,0},{20,4},{24,8},{28,12},{1,17},{... | collective-permute-start | bytes 356360 | tf_op jit(solution)/shard_map/ppermute | solution.py:424
  65.0 1.8 %collective-permute-start.29 = (bf16[464,128]{1,0:T(8,128)(2,1)S(1)}, bf16[464,128]{1,0:T(8,128)(2,1)S(1)}, u32[]{:S(2)}, u32[]{:S(2)}) collective-permute-start(bf16[464,128]{1,0:T(8,128)(2,1)S(1)} %filt_sum.1.refs_0_), channel_id=1, source_target_pairs={{0,24},{4,28},{8,16},{12,20},{16,8},{20,12},{24,0},{28,4},{1,25},{... | collective-permute-start | bytes 356360 | tf_op jit(solution)/shard_map/ppermute | solution.py:424
  66.8 0.7 collective-permute-start.31
  67.5 1.6 %collective-permute-start.32 = (bf16[192,128]{1,0:T(8,128)(2,1)S(1)}, bf16[192,128]{1,0:T(8,128)(2,1)S(1)}, u32[]{:S(2)}, u32[]{:S(2)}) collective-permute-start(bf16[192,128]{1,0:T(8,128)(2,1)S(1)} %filt_sum_rest.1.refs_4_), channel_id=1, source_target_pairs={{0,24},{4,28},{8,16},{12,20},{16,8},{20,12},{24,0},{28,4},{1,25},{... | collective-permute-start | bytes 147464 | tf_op jit(solution)/shard_map/ppermute | solution.py:424
  69.2 1.1 %collective-permute-start.30 = (bf16[192,128]{1,0:T(8,128)(2,1)S(1)}, bf16[192,128]{1,0:T(8,128)(2,1)S(1)}, u32[]{:S(2)}, u32[]{:S(2)}) collective-permute-start(bf16[192,128]{1,0:T(8,128)(2,1)S(1)} %filt_sum_rest.1.refs_4_), channel_id=1, source_target_pairs={{0,8},{4,12},{8,0},{12,4},{16,24},{20,28},{24,16},{28,20},{1,9},{5... | collective-permute-start | bytes 147464 | tf_op jit(solution)/shard_map/ppermute | solution.py:424
  70.3 2.5 %collective-permute-done.31.refs_6_ = bf16[192,128]{1,0:T(8,128)(2,1)S(1)} collective-permute-done((bf16[192,128]{1,0:T(8,128)(2,1)S(1)}, bf16[192,128]{1,0:T(8,128)(2,1)S(1)}, u32[]{:S(2)}, u32[]{:S(2)}) %collective-permute-start.31) | collective-permute-done | bytes 49184 | tf_op jit(solution)/shard_map/ppermute | solution.py:424
  72.8 0.5 collective-permute-done.30.refs_5_
  73.5 1.1 %finish_own.1 = (f32[27,128,128]{2,1,0:T(8,128)}, f32[27,64,128]{2,1,0:T(8,128)}) custom-call(bf16[4,656,128]{2,1,0:T(8,128)(2,1)S(1)} %stack.1.pieces), custom_call_target="tpu_custom_call" | custom-call | bytes 1048576 | tf_op jit(solution)/shard_map/finish_own/pallas_call | solution.py:23
  74.6 1.0 %collective-permute-done.33.pieces = bf16[4,656,128]{2,1,0:T(8,128)(2,1)S(1)} collective-permute-done((bf16[4,656,128]{2,1,0:T(8,128)(2,1)S(1)}, bf16[4,656,128]{2,1,0:T(8,128)(2,1)S(1)}, u32[]{:S(2)}, u32[]{:S(2)}) %collective-permute-start.33) | collective-permute-done | bytes 671776 | tf_op jit(solution)/shard_map/ppermute | solution.py:431
  75.6 1.1 %finish_other.1 = (f32[27,128,128]{2,1,0:T(8,128)}, f32[27,64,128]{2,1,0:T(8,128)}) custom-call(bf16[4,656,128]{2,1,0:T(8,128)(2,1)S(1)} %collective-permute-done.33.pieces, f32[27,128,128]{2,1,0:T(8,128)} %get-tuple-element.149.refs_0_, f32[27,64,128]{2,1,0:T(8,128)} %get-tuple-element.150.refs_1_), custom_call_target="tpu_custom_call", output_to_operand_aliasing={{0}: (1, {}), {1}: (2, {})} | custom-call | bytes 1048576 | tf_op jit(solution)/shard_map/finish_other/pallas_call | solution.py:23
  (50 shorter events, 2.3 us)
Async XLA Ops:
  1.4 8.8 %copy-start = (bf16[4,16,16,128]{3,2,1,0:T(8,128)(2,1)S(1)}, bf16[4,16,16,128]{3,2,1,0:T(8,128)(2,1)}, u32[]{:S(2)}) copy-start(bf16[4,16,16,128]{3,2,1,0:T(8,128)(2,1)} %center.1) | copy-start | bytes 786436
  1.4 11.5 %copy-start.1 = (bf16[27,128,128]{2,1,0:T(8,128)(2,1)S(1)}, bf16[27,128,128]{2,1,0:T(8,128)(2,1)}, u32[]{:S(2)}) copy-start(bf16[27,128,128]{2,1,0:T(8,128)(2,1)} %w.1) | copy-start | bytes 2654212
  1.4 5.6 %collective-permute-start = (bf16[4,2,16,128]{3,2,1,0:T(8,128)(2,1)S(1)}, bf16[4,2,16,128]{3,2,1,0:T(8,128)(2,1)S(1)}, u32[]{:S(2)}, u32[]{:S(2)}) collective-permute-start(bf16[4,2,16,128]{3,2,1,0:T(8,128)(2,1)S(1)} %edges.1), channel_id=1, source_target_pairs={{0,1},{2,3},{1,0},{3,2},{4,5},{6,7},{5,4},{7,6},{8,9},{10,11},{9,8... | collective-permute-start | bytes 98312 | tf_op jit(solution)/shard_map/ppermute | solution.py:441
  4.5 5.7 %collective-permute-start.1 = (bf16[4,2,16,128]{3,2,1,0:T(8,128)(2,1)S(1)}, bf16[4,2,16,128]{3,2,1,0:T(8,128)(2,1)S(1)}, u32[]{:S(2)}, u32[]{:S(2)}) collective-permute-start(bf16[4,2,16,128]{3,2,1,0:T(8,128)(2,1)S(1)} %edges.1), channel_id=1, source_target_pairs={{1,2},{3,0},{2,1},{0,3},{5,6},{7,4},{6,5},{4,7},{9,10},{11,8},{10,... | collective-permute-start | bytes 98312 | tf_op jit(solution)/shard_map/ppermute | solution.py:441
  10.3 2.6 %collective-permute-start.2 = (bf16[3,18,16,128]{3,2,1,0:T(8,128)(2,1)S(1)}, bf16[3,18,16,128]{3,2,1,0:T(8,128)(2,1)S(1)}, u32[]{:S(2)}, u32[]{:S(2)}) collective-permute-start(bf16[3,18,16,128]{3,2,1,0:T(8,128)(2,1)S(1)} %get-tuple-element.80), channel_id=1, source_target_pairs={{0,4},{8,12},{16,20},{24,28},{4,0},{12,8},{20,16},{28,24},{1,5},{9... | collective-permute-start | bytes 663560 | tf_op jit(solution)/shard_map/ppermute | solution.py:441
  10.4 9.2 %collective-permute-start.3 = (bf16[3,18,16,128]{3,2,1,0:T(8,128)(2,1)S(1)}, bf16[3,18,16,128]{3,2,1,0:T(8,128)(2,1)S(1)}, u32[]{:S(2)}, u32[]{:S(2)}) collective-permute-start(bf16[3,18,16,128]{3,2,1,0:T(8,128)(2,1)S(1)} %get-tuple-element.82), channel_id=1, source_target_pairs={{4,8},{12,16},{20,24},{28,0},{8,4},{16,12},{24,20},{0,28},{5,9},{1... | collective-permute-start | bytes 663560 | tf_op jit(solution)/shard_map/ppermute | solution.py:441
  15.1 9.0 %collective-permute-start.7 = (bf16[2,64,128]{2,1,0:T(8,128)(2,1)S(1)}, bf16[2,64,128]{2,1,0:T(8,128)(2,1)S(1)}, u32[]{:S(2)}, u32[]{:S(2)}) collective-permute-start(bf16[2,64,128]{2,1,0:T(8,128)(2,1)S(1)} %get-tuple-element.92.refs_4_), channel_id=1, source_target_pairs={{0,3},{1,2},{2,1},{3,0},{4,7},{5,6},{6,5},{7,4},{8,11},{9,10},{10,... | collective-permute-start | bytes 98312 | tf_op jit(solution)/shard_map/ppermute | solution.py:424
  17.7 8.4 %collective-permute-start.8 = (bf16[2,64,128]{2,1,0:T(8,128)(2,1)S(1)}, bf16[2,64,128]{2,1,0:T(8,128)(2,1)S(1)}, u32[]{:S(2)}, u32[]{:S(2)}) collective-permute-start(bf16[2,64,128]{2,1,0:T(8,128)(2,1)S(1)} %get-tuple-element.92.refs_4_), channel_id=1, source_target_pairs={{0,2},{1,3},{2,0},{3,1},{4,6},{5,7},{6,4},{7,5},{8,10},{9,11},{10,... | collective-permute-start | bytes 98312 | tf_op jit(solution)/shard_map/ppermute | solution.py:424
  17.7 8.4 %collective-permute-start.9 = (bf16[2,64,128]{2,1,0:T(8,128)(2,1)S(1)}, bf16[2,64,128]{2,1,0:T(8,128)(2,1)S(1)}, u32[]{:S(2)}, u32[]{:S(2)}) collective-permute-start(bf16[2,64,128]{2,1,0:T(8,128)(2,1)S(1)} %get-tuple-element.92.refs_4_), channel_id=1, source_target_pairs={{0,1},{1,0},{2,3},{3,2},{4,5},{5,4},{6,7},{7,6},{8,9},{9,8},{10,11... | collective-permute-start | bytes 98312 | tf_op jit(solution)/shard_map/ppermute | solution.py:424
  21.6 5.8 %collective-permute-start.4 = (bf16[2,64,128]{2,1,0:T(8,128)(2,1)S(1)}, bf16[2,64,128]{2,1,0:T(8,128)(2,1)S(1)}, u32[]{:S(2)}, u32[]{:S(2)}) collective-permute-start(bf16[2,64,128]{2,1,0:T(8,128)(2,1)S(1)} %get-tuple-element.88.refs_0_), channel_id=1, source_target_pairs={{0,3},{1,2},{2,1},{3,0},{4,7},{5,6},{6,5},{7,4},{8,11},{9,10},{10,... | collective-permute-start | bytes 98312 | tf_op jit(solution)/shard_map/ppermute | solution.py:424
  24.1 4.8 %collective-permute-start.5 = (bf16[2,64,128]{2,1,0:T(8,128)(2,1)S(1)}, bf16[2,64,128]{2,1,0:T(8,128)(2,1)S(1)}, u32[]{:S(2)}, u32[]{:S(2)}) collective-permute-start(bf16[2,64,128]{2,1,0:T(8,128)(2,1)S(1)} %get-tuple-element.88.refs_0_), channel_id=1, source_target_pairs={{0,2},{1,3},{2,0},{3,1},{4,6},{5,7},{6,4},{7,5},{8,10},{9,11},{10,... | collective-permute-start | bytes 98312 | tf_op jit(solution)/shard_map/ppermute | solution.py:424
  24.1 4.8 %collective-permute-start.6 = (bf16[2,64,128]{2,1,0:T(8,128)(2,1)S(1)}, bf16[2,64,128]{2,1,0:T(8,128)(2,1)S(1)}, u32[]{:S(2)}, u32[]{:S(2)}) collective-permute-start(bf16[2,64,128]{2,1,0:T(8,128)(2,1)S(1)} %get-tuple-element.88.refs_0_), channel_id=1, source_target_pairs={{0,1},{1,0},{2,3},{3,2},{4,5},{5,4},{6,7},{7,6},{8,9},{9,8},{10,11... | collective-permute-start | bytes 98312 | tf_op jit(solution)/shard_map/ppermute | solution.py:424
  26.1 2.9 %copy-start.2 = (bf16[27,128,64]{1,2,0:T(8,128)(2,1)S(1)}, bf16[27,128,64]{1,2,0:T(8,128)(2,1)}, u32[]{:S(2)}) copy-start(bf16[27,128,64]{1,2,0:T(8,128)(2,1)} %param.6) | copy-start | bytes 1327108
  26.1 2.9 %copy-start.3 = (bf16[2,32,8,64]{3,2,1,0:T(8,128)(2,1)S(1)}, bf16[2,32,8,64]{3,2,1,0:T(8,128)(2,1)}, u32[]{:S(2)}) copy-start(bf16[2,32,8,64]{3,2,1,0:T(8,128)(2,1)} %refs_9_.1) | copy-start | bytes 196612
  32.2 6.1 %collective-permute-start.10 = (bf16[4,64,128]{2,1,0:T(8,128)(2,1)S(1)}, bf16[4,64,128]{2,1,0:T(8,128)(2,1)S(1)}, u32[]{:S(2)}, u32[]{:S(2)}) collective-permute-start(bf16[4,64,128]{2,1,0:T(8,128)(2,1)S(1)} %get-tuple-element.101), channel_id=1, source_target_pairs={{0,3},{1,2},{2,1},{3,0},{4,7},{5,6},{6,5},{7,4},{8,11},{9,10},{10,... | collective-permute-start | bytes 196616 | tf_op jit(solution)/shard_map/ppermute | solution.py:424
  34.1 5.9 %collective-permute-start.11 = (bf16[4,64,128]{2,1,0:T(8,128)(2,1)S(1)}, bf16[4,64,128]{2,1,0:T(8,128)(2,1)S(1)}, u32[]{:S(2)}, u32[]{:S(2)}) collective-permute-start(bf16[4,64,128]{2,1,0:T(8,128)(2,1)S(1)} %get-tuple-element.103), channel_id=1, source_target_pairs={{0,2},{1,3},{2,0},{3,1},{4,6},{5,7},{6,4},{7,5},{8,10},{9,11},{10,... | collective-permute-start | bytes 196616 | tf_op jit(solution)/shard_map/ppermute | solution.py:424
  34.8 5.2 %collective-permute-start.12 = (bf16[4,64,128]{2,1,0:T(8,128)(2,1)S(1)}, bf16[4,64,128]{2,1,0:T(8,128)(2,1)S(1)}, u32[]{:S(2)}, u32[]{:S(2)}) collective-permute-start(bf16[4,64,128]{2,1,0:T(8,128)(2,1)S(1)} %get-tuple-element.104), channel_id=1, source_target_pairs={{0,1},{1,0},{2,3},{3,2},{4,5},{5,4},{6,7},{7,6},{8,9},{9,8},{10,11... | collective-permute-start | bytes 196616 | tf_op jit(solution)/shard_map/ppermute | solution.py:424
  41.0 1.6 %collective-permute-start.13 = (bf16[4,240,128]{2,1,0:T(8,128)(2,1)S(1)}, bf16[4,240,128]{2,1,0:T(8,128)(2,1)S(1)}, u32[]{:S(2)}, u32[]{:S(2)}) collective-permute-start(bf16[4,240,128]{2,1,0:T(8,128)(2,1)S(1)} %get-tuple-element.109), channel_id=1, source_target_pairs={{0,4},{4,0},{8,12},{12,8},{16,20},{20,16},{24,28},{28,24},{1,5},{5... | collective-permute-start | bytes 737288 | tf_op jit(solution)/shard_map/ppermute | solution.py:431
  43.4 4.4 %collective-permute-start.14 = (bf16[4,416,128]{2,1,0:T(8,128)(2,1)S(1)}, bf16[4,416,128]{2,1,0:T(8,128)(2,1)S(1)}, u32[]{:S(2)}, u32[]{:S(2)}) collective-permute-start(bf16[4,416,128]{2,1,0:T(8,128)(2,1)S(1)} %early_grad_rest.1), channel_id=1, source_target_pairs={{0,4},{4,0},{8,12},{12,8},{16,20},{20,16},{24,28},{28,24},{1,5},{5... | collective-permute-start | bytes 1277960 | tf_op jit(solution)/shard_map/ppermute | solution.py:431
  43.6 5.3 %collective-permute-start.15 = (bf16[240,128]{1,0:T(8,128)(2,1)S(1)}, bf16[240,128]{1,0:T(8,128)(2,1)S(1)}, u32[]{:S(2)}, u32[]{:S(2)}) collective-permute-start(bf16[240,128]{1,0:T(8,128)(2,1)S(1)} %get-tuple-element.119), channel_id=1, source_target_pairs={{0,24},{4,28},{8,16},{12,20},{16,8},{20,12},{24,0},{28,4},{1,25},{... | collective-permute-start | bytes 184328 | tf_op jit(solution)/shard_map/ppermute | solution.py:424
  45.0 5.1 %collective-permute-start.16 = (bf16[240,128]{1,0:T(8,128)(2,1)S(1)}, bf16[240,128]{1,0:T(8,128)(2,1)S(1)}, u32[]{:S(2)}, u32[]{:S(2)}) collective-permute-start(bf16[240,128]{1,0:T(8,128)(2,1)S(1)} %get-tuple-element.120), channel_id=1, source_target_pairs={{0,16},{4,20},{8,24},{12,28},{16,0},{20,4},{24,8},{28,12},{1,17},{... | collective-permute-start | bytes 184328 | tf_op jit(solution)/shard_map/ppermute | solution.py:424
  46.3 4.2 %collective-permute-start.17 = (bf16[240,128]{1,0:T(8,128)(2,1)S(1)}, bf16[240,128]{1,0:T(8,128)(2,1)S(1)}, u32[]{:S(2)}, u32[]{:S(2)}) collective-permute-start(bf16[240,128]{1,0:T(8,128)(2,1)S(1)} %get-tuple-element.121), channel_id=1, source_target_pairs={{0,8},{4,12},{8,0},{12,4},{16,24},{20,28},{24,16},{28,20},{1,9},{5... | collective-permute-start | bytes 184328 | tf_op jit(solution)/shard_map/ppermute | solution.py:424
  50.5 6.7 %collective-permute-start.18 = (bf16[416,128]{1,0:T(8,128)(2,1)S(1)}, bf16[416,128]{1,0:T(8,128)(2,1)S(1)}, u32[]{:S(2)}, u32[]{:S(2)}) collective-permute-start(bf16[416,128]{1,0:T(8,128)(2,1)S(1)} %get-tuple-element.123), channel_id=1, source_target_pairs={{0,24},{4,28},{8,16},{12,20},{16,8},{20,12},{24,0},{28,4},{1,25},{... | collective-permute-start | bytes 319496 | tf_op jit(solution)/shard_map/ppermute | solution.py:424
  51.8 6.7 %collective-permute-start.19 = (bf16[416,128]{1,0:T(8,128)(2,1)S(1)}, bf16[416,128]{1,0:T(8,128)(2,1)S(1)}, u32[]{:S(2)}, u32[]{:S(2)}) collective-permute-start(bf16[416,128]{1,0:T(8,128)(2,1)S(1)} %get-tuple-element.124), channel_id=1, source_target_pairs={{0,16},{4,20},{8,24},{12,28},{16,0},{20,4},{24,8},{28,12},{1,17},{... | collective-permute-start | bytes 319496 | tf_op jit(solution)/shard_map/ppermute | solution.py:424
  52.8 5.7 %collective-permute-start.20 = (bf16[416,128]{1,0:T(8,128)(2,1)S(1)}, bf16[416,128]{1,0:T(8,128)(2,1)S(1)}, u32[]{:S(2)}, u32[]{:S(2)}) collective-permute-start(bf16[416,128]{1,0:T(8,128)(2,1)S(1)} %get-tuple-element.125), channel_id=1, source_target_pairs={{0,8},{4,12},{8,0},{12,4},{16,24},{20,28},{24,16},{28,20},{1,9},{5... | collective-permute-start | bytes 319496 | tf_op jit(solution)/shard_map/ppermute | solution.py:424
  54.0 7.2 %collective-permute-start.21 = (bf16[240,128]{1,0:T(8,128)(2,1)S(1)}, bf16[240,128]{1,0:T(8,128)(2,1)S(1)}, u32[]{:S(2)}, u32[]{:S(2)}) collective-permute-start(bf16[240,128]{1,0:T(8,128)(2,1)S(1)} %chip_sum.1.refs_0_), channel_id=1, source_target_pairs={{0,3},{1,2},{2,1},{3,0},{4,7},{5,6},{6,5},{7,4},{8,11},{9,10},{10,... | collective-permute-start | bytes 184328 | tf_op jit(solution)/shard_map/ppermute | solution.py:424
  56.7 6.4 %collective-permute-start.22 = (bf16[240,128]{1,0:T(8,128)(2,1)S(1)}, bf16[240,128]{1,0:T(8,128)(2,1)S(1)}, u32[]{:S(2)}, u32[]{:S(2)}) collective-permute-start(bf16[240,128]{1,0:T(8,128)(2,1)S(1)} %chip_sum.1.refs_0_), channel_id=1, source_target_pairs={{0,2},{1,3},{2,0},{3,1},{4,6},{5,7},{6,4},{7,5},{8,10},{9,11},{10,... | collective-permute-start | bytes 184328 | tf_op jit(solution)/shard_map/ppermute | solution.py:424
  57.2 6.0 %collective-permute-start.23 = (bf16[240,128]{1,0:T(8,128)(2,1)S(1)}, bf16[240,128]{1,0:T(8,128)(2,1)S(1)}, u32[]{:S(2)}, u32[]{:S(2)}) collective-permute-start(bf16[240,128]{1,0:T(8,128)(2,1)S(1)} %chip_sum.1.refs_0_), channel_id=1, source_target_pairs={{0,1},{1,0},{2,3},{3,2},{4,5},{5,4},{6,7},{7,6},{8,9},{9,8},{10,11... | collective-permute-start | bytes 184328 | tf_op jit(solution)/shard_map/ppermute | solution.py:424
  58.5 6.5 %collective-permute-start.24 = (bf16[192,128]{1,0:T(8,128)(2,1)S(1)}, bf16[192,128]{1,0:T(8,128)(2,1)S(1)}, u32[]{:S(2)}, u32[]{:S(2)}) collective-permute-start(bf16[192,128]{1,0:T(8,128)(2,1)S(1)} %get-tuple-element.143.refs_0_), channel_id=1, source_target_pairs={{0,3},{1,2},{2,1},{3,0},{4,7},{5,6},{6,5},{7,4},{8,11},{9,10},{10,... | collective-permute-start | bytes 147464 | tf_op jit(solution)/shard_map/ppermute | solution.py:424
  61.2 5.5 %collective-permute-start.25 = (bf16[192,128]{1,0:T(8,128)(2,1)S(1)}, bf16[192,128]{1,0:T(8,128)(2,1)S(1)}, u32[]{:S(2)}, u32[]{:S(2)}) collective-permute-start(bf16[192,128]{1,0:T(8,128)(2,1)S(1)} %get-tuple-element.143.refs_0_), channel_id=1, source_target_pairs={{0,2},{1,3},{2,0},{3,1},{4,6},{5,7},{6,4},{7,5},{8,10},{9,11},{10,... | collective-permute-start | bytes 147464 | tf_op jit(solution)/shard_map/ppermute | solution.py:424
  61.2 5.5 %collective-permute-start.26 = (bf16[192,128]{1,0:T(8,128)(2,1)S(1)}, bf16[192,128]{1,0:T(8,128)(2,1)S(1)}, u32[]{:S(2)}, u32[]{:S(2)}) collective-permute-start(bf16[192,128]{1,0:T(8,128)(2,1)S(1)} %get-tuple-element.143.refs_0_), channel_id=1, source_target_pairs={{0,1},{1,0},{2,3},{3,2},{4,5},{5,4},{6,7},{7,6},{8,9},{9,8},{10,11... | collective-permute-start | bytes 147464 | tf_op jit(solution)/shard_map/ppermute | solution.py:424
  63.2 6.0 %collective-permute-start.27 = (bf16[464,128]{1,0:T(8,128)(2,1)S(1)}, bf16[464,128]{1,0:T(8,128)(2,1)S(1)}, u32[]{:S(2)}, u32[]{:S(2)}) collective-permute-start(bf16[464,128]{1,0:T(8,128)(2,1)S(1)} %filt_sum.1.refs_0_), channel_id=1, source_target_pairs={{0,8},{4,12},{8,0},{12,4},{16,24},{20,28},{24,16},{28,20},{1,9},{5... | collective-permute-start | bytes 356360 | tf_op jit(solution)/shard_map/ppermute | solution.py:424
  64.0 8.8 %collective-permute-start.28 = (bf16[464,128]{1,0:T(8,128)(2,1)S(1)}, bf16[464,128]{1,0:T(8,128)(2,1)S(1)}, u32[]{:S(2)}, u32[]{:S(2)}) collective-permute-start(bf16[464,128]{1,0:T(8,128)(2,1)S(1)} %filt_sum.1.refs_0_), channel_id=1, source_target_pairs={{0,16},{4,20},{8,24},{12,28},{16,0},{20,4},{24,8},{28,12},{1,17},{... | collective-permute-start | bytes 356360 | tf_op jit(solution)/shard_map/ppermute | solution.py:424
  65.0 7.9 %collective-permute-start.29 = (bf16[464,128]{1,0:T(8,128)(2,1)S(1)}, bf16[464,128]{1,0:T(8,128)(2,1)S(1)}, u32[]{:S(2)}, u32[]{:S(2)}) collective-permute-start(bf16[464,128]{1,0:T(8,128)(2,1)S(1)} %filt_sum.1.refs_0_), channel_id=1, source_target_pairs={{0,24},{4,28},{8,16},{12,20},{16,8},{20,12},{24,0},{28,4},{1,25},{... | collective-permute-start | bytes 356360 | tf_op jit(solution)/shard_map/ppermute | solution.py:424
  66.8 6.1 %collective-permute-start.31 = (bf16[192,128]{1,0:T(8,128)(2,1)S(1)}, bf16[192,128]{1,0:T(8,128)(2,1)S(1)}, u32[]{:S(2)}, u32[]{:S(2)}) collective-permute-start(bf16[192,128]{1,0:T(8,128)(2,1)S(1)} %filt_sum_rest.1.refs_4_), channel_id=1, source_target_pairs={{0,16},{4,20},{8,24},{12,28},{16,0},{20,4},{24,8},{28,12},{1,17},{... | collective-permute-start | bytes 147464 | tf_op jit(solution)/shard_map/ppermute | solution.py:424
  67.5 5.3 %collective-permute-start.32 = (bf16[192,128]{1,0:T(8,128)(2,1)S(1)}, bf16[192,128]{1,0:T(8,128)(2,1)S(1)}, u32[]{:S(2)}, u32[]{:S(2)}) collective-permute-start(bf16[192,128]{1,0:T(8,128)(2,1)S(1)} %filt_sum_rest.1.refs_4_), channel_id=1, source_target_pairs={{0,24},{4,28},{8,16},{12,20},{16,8},{20,12},{24,0},{28,4},{1,25},{... | collective-permute-start | bytes 147464 | tf_op jit(solution)/shard_map/ppermute | solution.py:424
  69.2 4.1 %collective-permute-start.30 = (bf16[192,128]{1,0:T(8,128)(2,1)S(1)}, bf16[192,128]{1,0:T(8,128)(2,1)S(1)}, u32[]{:S(2)}, u32[]{:S(2)}) collective-permute-start(bf16[192,128]{1,0:T(8,128)(2,1)S(1)} %filt_sum_rest.1.refs_4_), channel_id=1, source_target_pairs={{0,8},{4,12},{8,0},{12,4},{16,24},{20,28},{24,16},{28,20},{1,9},{5... | collective-permute-start | bytes 147464 | tf_op jit(solution)/shard_map/ppermute | solution.py:424
  73.4 2.2 %collective-permute-start.33 = (bf16[4,656,128]{2,1,0:T(8,128)(2,1)S(1)}, bf16[4,656,128]{2,1,0:T(8,128)(2,1)S(1)}, u32[]{:S(2)}, u32[]{:S(2)}) collective-permute-start(bf16[4,656,128]{2,1,0:T(8,128)(2,1)S(1)} %stack.1.pieces), channel_id=1, source_target_pairs={{0,4},{4,0},{8,12},{12,8},{16,20},{20,16},{24,28},{28,24},{1,5},{5... | collective-permute-start | bytes 2015240 | tf_op jit(solution)/shard_map/ppermute | solution.py:431

commit v4 on v2

--- a/solution.py
+++ b/solution.py
@@ -95,19 +95,21 @@
 def early_rows_of(windows, start, wide, ny, keep):
     rows = windows.shape[2]
     cout = wide.shape[2] // 2
-    acc = jnp.zeros((2 * rows, 2 * cout), F32)
-    for ab in range(9):
-        a, b = ab // 3, ab % 3
-        left = windows[b, pl.ds(start + a, 2)].reshape(2 * rows, windows.shape[3])
-        acc = acc + jnp.dot(left, wide[ab], preferred_element_type=F32)
-    sig = sigmoid(acc)
-    slope = (sig * (1.0 + acc * (1.0 - sig)) * keep).reshape(2, rows, 2 * cout)
-    act = acc * sig
-    act = act[:rows] + act[rows:]
-    act = act[:, :cout] + act[:, cout:]
-    act = act.reshape(ny // 2, 2, rows // ny, cout)
+    slopes, acts = [], []
+    for row in range(2):
+        acc = jnp.zeros((rows, 2 * cout), F32)
+        for ab in range(9):
+            a, b = ab // 3, ab % 3
+            acc = acc + jnp.dot(
+                windows[b, start + a + row], wide[ab], preferred_element_type=F32
+            )
+        sig = sigmoid(acc)
+        slopes.append(sig * (1.0 + acc * (1.0 - sig)) * keep)
+        act = acc * sig
+        acts.append(act[:, :cout] + act[:, cout:])
+    act = (acts[0] + acts[1]).reshape(ny // 2, 2, rows // ny, cout)
     act = (act[:, 0] + act[:, 1]) * keep
-    return slope, act.reshape(rows // 2, cout).astype(BF16)
+    return slopes, act.reshape(rows // 2, cout).astype(BF16)
 
 
 def near_body(center, sides, near, w, windows, sg, pooled, wide, field):
@@ -132,7 +134,8 @@
     fill_windows(field, windows)
     for chunk in range(nx // 2):
         slope, pool = early_rows_of(windows, 1 - odd + 2 * chunk, wide, ny, 0.125)
-        sg[2 * chunk : 2 * chunk + 2] = slope
+        for row in range(2):
+            sg[2 * chunk + row] = slope[row]
         pooled[chunk] = pool
 
 
@@ -150,7 +153,8 @@
     second = jnp.where(odd == 1, inside, 1.0)
     for chunk, flag in enumerate((first, second)):
         slope, pool = early_rows_of(held, 2 * chunk, wide, wide_y - 2, 0.125 * flag)
-        sg[2 * chunk : 2 * chunk + 2] = slope
+        for row in range(2):
+            sg[2 * chunk + row] = slope[row]
         pooled[chunk] = pool
 
 

time: 75.6 us -> 75.7 us (level)
  transfers between devices with their start and end apart: 34 -> 34, of which waited for: 12 -> 14; matrix products, arithmetic and copies ran while one was open for 0% -> 0% of each run, Pallas kernels for 12% -> 12%
where the time goes in v4:
time: 75.7 us; the launch traced here: 75.5 us
  starting transfers between devices  44.3 us (59%)
  waiting for transfers between devices  15.4 us (20%)
  Pallas kernels  14.2 us (19%)
  between operations  0.83 us (1%)
  local copies, waits for them, and re-layouts  0.76 us (1%)
    ppermute x27, starting transfers between devices, paired(): lax.ppermute(values[j], axis, [(i, i ^ step * j) for i in range(count)])  35.8 us
    pallas_call x20, Pallas kernels, call(): pl.pallas_call(body, name=name, out_shape=out_shape, in_specs=[HBM if i i...  14.2 us
    ppermute x27, waiting for transfers between devices, paired(): lax.ppermute(values[j], axis, [(i, i ^ step * j) for i in range(count)])  10.5 us
    ppermute x4, starting transfers between devices, swap(): return lax.ppermute(value, axis, pairs + [(b, a) for a, b in pairs])  8.18 us
    ppermute x4, waiting for transfers between devices, swap(): return lax.ppermute(value, axis, pairs + [(b, a) for a, b in pairs])  3.24 us
    ppermute x3, waiting for transfers between devices, exchange(): lax.ppermute(value, axis, [(i, i ^ step) for i in range(lax.axis_size(axi...  1.6 us
  transfers between devices with their start and end apart: 34, of which 14 were waited for; matrix products, arithmetic and copies ran while one was open for 0% of the time, Pallas kernels for 12%

profile of v4, /device:TPU:0, one launch (start us, length us, event | category | flops | bytes accessed | tf_op | source)
XLA Modules:
  0.0 75.5 jit_solution(992869342054677188)
XLA Ops:
  0.6 0.7 fusion
  1.4 3.1 %collective-permute-start = (bf16[4,2,16,128]{3,2,1,0:T(8,128)(2,1)S(1)}, bf16[4,2,16,128]{3,2,1,0:T(8,128)(2,1)S(1)}, u32[]{:S(2)}, u32[]{:S(2)}) collective-permute-start(bf16[4,2,16,128]{3,2,1,0:T(8,128)(2,1)S(1)} %edges.1), channel_id=1, source_target_pairs={{0,1},{2,3},{1,0},{3,2},{4,5},{6,7},{5,4},{7,6},{8,9},{10,11},{9,8... | collective-permute-start | bytes 98312 | tf_op jit(solution)/shard_map/ppermute | solution.py:427
  4.5 2.5 %collective-permute-start.1 = (bf16[4,2,16,128]{3,2,1,0:T(8,128)(2,1)S(1)}, bf16[4,2,16,128]{3,2,1,0:T(8,128)(2,1)S(1)}, u32[]{:S(2)}, u32[]{:S(2)}) collective-permute-start(bf16[4,2,16,128]{3,2,1,0:T(8,128)(2,1)S(1)} %edges.1), channel_id=1, source_target_pairs={{1,2},{3,0},{2,1},{0,3},{5,6},{7,4},{6,5},{4,7},{9,10},{11,8},{10,... | collective-permute-start | bytes 98312 | tf_op jit(solution)/shard_map/ppermute | solution.py:427
  7.0 3.2 %collective-permute-done.1.yodd = bf16[4,2,16,128]{3,2,1,0:T(8,128)(2,1)S(1)} collective-permute-done((bf16[4,2,16,128]{3,2,1,0:T(8,128)(2,1)S(1)}, bf16[4,2,16,128]{3,2,1,0:T(8,128)(2,1)S(1)}, u32[]{:S(2)}, u32[]{:S(2)}) %collective-permute-start.1) | collective-permute-done | bytes 32800 | tf_op jit(solution)/shard_map/ppermute | solution.py:427
  10.4 2.5 %collective-permute-start.3 = (bf16[3,18,16,128]{3,2,1,0:T(8,128)(2,1)S(1)}, bf16[3,18,16,128]{3,2,1,0:T(8,128)(2,1)S(1)}, u32[]{:S(2)}, u32[]{:S(2)}) collective-permute-start(bf16[3,18,16,128]{3,2,1,0:T(8,128)(2,1)S(1)} %get-tuple-element.82), channel_id=1, source_target_pairs={{4,8},{12,16},{20,24},{28,0},{8,4},{16,12},{24,20},{0,28},{5,9},{1... | collective-permute-start | bytes 663560 | tf_op jit(solution)/shard_map/ppermute | solution.py:427
  12.9 2.3 %early_near.1 = (bf16[3,7,128,512]{3,2,1,0:T(8,128)(2,1)S(1)}, f32[4,128,256]{2,1,0:T(8,128)S(1)}, bf16[2,64,128]{2,1,0:T(8,128)(2,1)S(1)}, bf16[9,512,256]{2,1,0:T(8,128)(2,1)S(1)}) custom-call(bf16[4,16,16,128]{3,2,1,0:T(8,128)(2,1)S(1)} %get-tuple-element.78.center, bf16[4,2,16,128]{3,2,1,0:T(8,128)(2,1)S(1)} %get-tuple-element.79.sides, ...), custom_call_target="tpu_custom_call" | custom-call | flops 1207959552 | bytes 1048576 | tf_op jit(solution)/shard_map/early_near/pallas_call | solution.py:23
  15.2 2.5 %collective-permute-start.7 = (bf16[2,64,128]{2,1,0:T(8,128)(2,1)S(1)}, bf16[2,64,128]{2,1,0:T(8,128)(2,1)S(1)}, u32[]{:S(2)}, u32[]{:S(2)}) collective-permute-start(bf16[2,64,128]{2,1,0:T(8,128)(2,1)S(1)} %get-tuple-element.92.refs_4_), channel_id=1, source_target_pairs={{0,3},{1,2},{2,1},{3,0},{4,7},{5,6},{6,5},{7,4},{8,11},{9,10},{10,... | collective-permute-start | bytes 98312 | tf_op jit(solution)/shard_map/ppermute | solution.py:410
  17.7 1.9 %collective-permute-start.9 = (bf16[2,64,128]{2,1,0:T(8,128)(2,1)S(1)}, bf16[2,64,128]{2,1,0:T(8,128)(2,1)S(1)}, u32[]{:S(2)}, u32[]{:S(2)}) collective-permute-start(bf16[2,64,128]{2,1,0:T(8,128)(2,1)S(1)} %get-tuple-element.92.refs_4_), channel_id=1, source_target_pairs={{0,1},{1,0},{2,3},{3,2},{4,5},{5,4},{6,7},{7,6},{8,9},{9,8},{10,11... | collective-permute-start | bytes 98312 | tf_op jit(solution)/shard_map/ppermute | solution.py:410
  19.7 2.0 %early_far.1 = (bf16[3,3,128,512]{3,2,1,0:T(8,128)(2,1)S(1)}, f32[4,128,256]{2,1,0:T(8,128)S(1)}, bf16[2,64,128]{2,1,0:T(8,128)(2,1)S(1)}) custom-call(bf16[3,7,128,512]{3,2,1,0:T(8,128)(2,1)S(1)} %get-tuple-element.86.windows, bf16[3,18,16,128]{3,2,1,0:T(8,128)(2,1)S(1)} %collective-permute-done.3.far, bf16[9,512,256]{2,1,0:T(8,128)(2,1)S(1)} %get-tuple-element.83.wide), custom_call_target="tpu_custom_call" | custom-call | flops 1207959552 | bytes 1048576 | tf_op jit(solution)/shard_map/early_far/pallas_call | solution.py:23
  21.7 2.5 %collective-permute-start.4 = (bf16[2,64,128]{2,1,0:T(8,128)(2,1)S(1)}, bf16[2,64,128]{2,1,0:T(8,128)(2,1)S(1)}, u32[]{:S(2)}, u32[]{:S(2)}) collective-permute-start(bf16[2,64,128]{2,1,0:T(8,128)(2,1)S(1)} %get-tuple-element.88.refs_0_), channel_id=1, source_target_pairs={{0,3},{1,2},{2,1},{3,0},{4,7},{5,6},{6,5},{7,4},{8,11},{9,10},{10,... | collective-permute-start | bytes 98312 | tf_op jit(solution)/shard_map/ppermute | solution.py:410
  24.2 1.9 %collective-permute-start.6 = (bf16[2,64,128]{2,1,0:T(8,128)(2,1)S(1)}, bf16[2,64,128]{2,1,0:T(8,128)(2,1)S(1)}, u32[]{:S(2)}, u32[]{:S(2)}) collective-permute-start(bf16[2,64,128]{2,1,0:T(8,128)(2,1)S(1)} %get-tuple-element.88.refs_0_), channel_id=1, source_target_pairs={{0,1},{1,0},{2,3},{3,2},{4,5},{5,4},{6,7},{7,6},{8,9},{9,8},{10,11... | collective-permute-start | bytes 98312 | tf_op jit(solution)/shard_map/ppermute | solution.py:410
  26.2 1.1 %turn_windows.1.refs_6_.refs_1_ = bf16[3,2,256,1280]{3,2,1,0:T(8,128)(2,1)S(1)} custom-call(bf16[3,7,128,512]{3,2,1,0:T(8,128)(2,1)S(1)} %get-tuple-element.86.windows, bf16[3,3,128,512]{3,2,1,0:T(8,128)(2,1)S(1)} %get-tuple-element.87.far_windows), custom_call_target="tpu_custom_call" | custom-call | flops 1073741824 | bytes 1048576 | tf_op jit(solution)/shard_map/turn_windows/pallas_call | solution.py:23
  27.5 1.6 %collective-permute-done.5.refs_2_ = bf16[2,64,128]{2,1,0:T(8,128)(2,1)S(1)} collective-permute-done((bf16[2,64,128]{2,1,0:T(8,128)(2,1)S(1)}, bf16[2,64,128]{2,1,0:T(8,128)(2,1)S(1)}, u32[]{:S(2)}, u32[]{:S(2)}) %collective-permute-start.5) | collective-permute-done | bytes 32800 | tf_op jit(solution)/shard_map/ppermute | solution.py:410
  29.0 2.1 %deep_conv.1 = (bf16[2,32,8,64]{3,2,1,0:T(8,128)(2,1)}, bf16[2,256,64]{2,1,0:T(8,128)(2,1)S(1)}, bf16[3,4,256,384]{3,2,1,0:T(8,128)(2,1)S(1)}, f32[4,64,128]{2,1...) custom-call(bf16[2,64,128]{2,1,0:T(8,128)(2,1)S(1)} %get-tuple-eleme, ...), custom_call_target="tpu_custom_call" | custom-call | flops 452984832 | bytes 1048576 | tf_op jit(solution)/shard_map/deep_conv/pallas_call | solution.py:23
  31.2 1.9 %collective-permute-start.10 = (bf16[4,64,128]{2,1,0:T(8,128)(2,1)S(1)}, bf16[4,64,128]{2,1,0:T(8,128)(2,1)S(1)}, u32[]{:S(2)}, u32[]{:S(2)}) collective-permute-start(bf16[4,64,128]{2,1,0:T(8,128)(2,1)S(1)} %get-tuple-element.101), channel_id=1, source_target_pairs={{0,3},{1,2},{2,1},{3,0},{4,7},{5,6},{6,5},{7,4},{8,11},{9,10},{10,... | collective-permute-start | bytes 196616 | tf_op jit(solution)/shard_map/ppermute | solution.py:410
  33.0 0.7 collective-permute-start.11
  33.7 1.9 %collective-permute-start.12 = (bf16[4,64,128]{2,1,0:T(8,128)(2,1)S(1)}, bf16[4,64,128]{2,1,0:T(8,128)(2,1)S(1)}, u32[]{:S(2)}, u32[]{:S(2)}) collective-permute-start(bf16[4,64,128]{2,1,0:T(8,128)(2,1)S(1)} %get-tuple-element.104), channel_id=1, source_target_pairs={{0,1},{1,0},{2,3},{3,2},{4,5},{5,4},{6,7},{7,6},{8,9},{9,8},{10,11... | collective-permute-start | bytes 196616 | tf_op jit(solution)/shard_map/ppermute | solution.py:410
  35.6 0.7 deep_grad.1
  36.4 0.9 %collective-permute-done.10.refs_1_ = bf16[4,64,128]{2,1,0:T(8,128)(2,1)S(1)} collective-permute-done((bf16[4,64,128]{2,1,0:T(8,128)(2,1)S(1)}, bf16[4,64,128]{2,1,0:T(8,128)(2,1)S(1)}, u32[]{:S(2)}, u32[]{:S(2)}) %collective-permute-start.10) | collective-permute-done | bytes 65568 | tf_op jit(solution)/shard_map/ppermute | solution.py:410
  37.3 1.6 %collective-permute-done.11.refs_2_ = bf16[4,64,128]{2,1,0:T(8,128)(2,1)S(1)} collective-permute-done((bf16[4,64,128]{2,1,0:T(8,128)(2,1)S(1)}, bf16[4,64,128]{2,1,0:T(8,128)(2,1)S(1)}, u32[]{:S(2)}, u32[]{:S(2)}) %collective-permute-start.11) | collective-permute-done | bytes 65568 | tf_op jit(solution)/shard_map/ppermute | solution.py:410
  38.9 1.0 %early_grad.1 = (bf16[4,240,128]{2,1,0:T(8,128)(2,1)S(1)}, bf16[8,128,256]{2,1,0:T(8,128)(2,1)S(1)}) custom-call(f32[4,64,128]{2,1,0:T(8,128)S(1)} %get-tuple-element.97.refs_0_, bf16[4,64,128]{2,1,0:T(8,128)(2,1)S(1)} %collective-permute-done.10.refs_1_, bf16[4,64,128]{2,1,0:T(8,128)(2,1)S(1)} %collective-permute-done.11.refs_2_, ...), custom_call_target="tpu_custom_call" | custom-call | flops 1207959552 | bytes 1048576 | tf_op jit(solution)/shard_map/early_grad/pallas_call | solution.py:23
  40.0 0.8 %early_grad_own.1.mine = f32[4,240,128]{2,1,0:T(8,128)S(1)} custom-call(bf16[8,128,256]{2,1,0:T(8,128)(2,1)S(1)} %get-tuple-element.111.refs_0_, bf16[3,2,256,1280]{3,2,1,0:T(8,128)(2,1)S(1)} %turn_windows.1.refs_6_.refs_1_), custom_call_target="tpu_custom_call" | custom-call | flops 1207959552 | bytes 1048576 | tf_op jit(solution)/shard_map/early_grad_own/pallas_call | solution.py:23
  40.9 0.6 collective-permute-done.13.other
  41.6 0.7 early_grad_rest.1
  42.5 1.4 %collective-permute-start.15 = (bf16[240,128]{1,0:T(8,128)(2,1)S(1)}, bf16[240,128]{1,0:T(8,128)(2,1)S(1)}, u32[]{:S(2)}, u32[]{:S(2)}) collective-permute-start(bf16[240,128]{1,0:T(8,128)(2,1)S(1)} %get-tuple-element.119), channel_id=1, source_target_pairs={{0,24},{4,28},{8,16},{12,20},{16,8},{20,12},{24,0},{28,4},{1,25},{... | collective-permute-start | bytes 184328 | tf_op jit(solution)/shard_map/ppermute | solution.py:410
  43.9 1.2 %collective-permute-start.16 = (bf16[240,128]{1,0:T(8,128)(2,1)S(1)}, bf16[240,128]{1,0:T(8,128)(2,1)S(1)}, u32[]{:S(2)}, u32[]{:S(2)}) collective-permute-start(bf16[240,128]{1,0:T(8,128)(2,1)S(1)} %get-tuple-element.120), channel_id=1, source_target_pairs={{0,16},{4,20},{8,24},{12,28},{16,0},{20,4},{24,8},{28,12},{1,17},{... | collective-permute-start | bytes 184328 | tf_op jit(solution)/shard_map/ppermute | solution.py:410
  45.1 0.9 %collective-permute-start.17 = (bf16[240,128]{1,0:T(8,128)(2,1)S(1)}, bf16[240,128]{1,0:T(8,128)(2,1)S(1)}, u32[]{:S(2)}, u32[]{:S(2)}) collective-permute-start(bf16[240,128]{1,0:T(8,128)(2,1)S(1)} %get-tuple-element.121), channel_id=1, source_target_pairs={{0,8},{4,12},{8,0},{12,4},{16,24},{20,28},{24,16},{28,20},{1,9},{5... | collective-permute-start | bytes 184328 | tf_op jit(solution)/shard_map/ppermute | solution.py:410
  46.0 0.7 early_grad_rest_own.1.mine
  46.8 1.0 %collective-permute-done.15.refs_1_ = bf16[240,128]{1,0:T(8,128)(2,1)S(1)} collective-permute-done((bf16[240,128]{1,0:T(8,128)(2,1)S(1)}, bf16[240,128]{1,0:T(8,128)(2,1)S(1)}, u32[]{:S(2)}, u32[]{:S(2)}) %collective-permute-start.15) | collective-permute-done | bytes 61472 | tf_op jit(solution)/shard_map/ppermute | solution.py:410
  47.8 1.2 %collective-permute-done.16.refs_2_ = bf16[240,128]{1,0:T(8,128)(2,1)S(1)} collective-permute-done((bf16[240,128]{1,0:T(8,128)(2,1)S(1)}, bf16[240,128]{1,0:T(8,128)(2,1)S(1)}, u32[]{:S(2)}, u32[]{:S(2)}) %collective-permute-start.16) | collective-permute-done | bytes 61472 | tf_op jit(solution)/shard_map/ppermute | solution.py:410
  49.3 1.3 %collective-permute-start.18 = (bf16[416,128]{1,0:T(8,128)(2,1)S(1)}, bf16[416,128]{1,0:T(8,128)(2,1)S(1)}, u32[]{:S(2)}, u32[]{:S(2)}) collective-permute-start(bf16[416,128]{1,0:T(8,128)(2,1)S(1)} %get-tuple-element.123), channel_id=1, source_target_pairs={{0,24},{4,28},{8,16},{12,20},{16,8},{20,12},{24,0},{28,4},{1,25},{... | collective-permute-start | bytes 319496 | tf_op jit(solution)/shard_map/ppermute | solution.py:410
  50.7 1.0 %collective-permute-start.19 = (bf16[416,128]{1,0:T(8,128)(2,1)S(1)}, bf16[416,128]{1,0:T(8,128)(2,1)S(1)}, u32[]{:S(2)}, u32[]{:S(2)}) collective-permute-start(bf16[416,128]{1,0:T(8,128)(2,1)S(1)} %get-tuple-element.124), channel_id=1, source_target_pairs={{0,16},{4,20},{8,24},{12,28},{16,0},{20,4},{24,8},{28,12},{1,17},{... | collective-permute-start | bytes 319496 | tf_op jit(solution)/shard_map/ppermute | solution.py:410
  51.7 1.1 %collective-permute-start.20 = (bf16[416,128]{1,0:T(8,128)(2,1)S(1)}, bf16[416,128]{1,0:T(8,128)(2,1)S(1)}, u32[]{:S(2)}, u32[]{:S(2)}) collective-permute-start(bf16[416,128]{1,0:T(8,128)(2,1)S(1)} %get-tuple-element.125), channel_id=1, source_target_pairs={{0,8},{4,12},{8,0},{12,4},{16,24},{20,28},{24,16},{28,20},{1,9},{5... | collective-permute-start | bytes 319496 | tf_op jit(solution)/shard_map/ppermute | solution.py:410
  52.9 2.7 %collective-permute-start.21 = (bf16[240,128]{1,0:T(8,128)(2,1)S(1)}, bf16[240,128]{1,0:T(8,128)(2,1)S(1)}, u32[]{:S(2)}, u32[]{:S(2)}) collective-permute-start(bf16[240,128]{1,0:T(8,128)(2,1)S(1)} %chip_sum.1.refs_0_), channel_id=1, source_target_pairs={{0,3},{1,2},{2,1},{3,0},{4,7},{5,6},{6,5},{7,4},{8,11},{9,10},{10,... | collective-permute-start | bytes 184328 | tf_op jit(solution)/shard_map/ppermute | solution.py:410
  55.6 0.4 collective-permute-done.18.refs_1_
  56.0 1.3 %collective-permute-start.23 = (bf16[240,128]{1,0:T(8,128)(2,1)S(1)}, bf16[240,128]{1,0:T(8,128)(2,1)S(1)}, u32[]{:S(2)}, u32[]{:S(2)}) collective-permute-start(bf16[240,128]{1,0:T(8,128)(2,1)S(1)} %chip_sum.1.refs_0_), channel_id=1, source_target_pairs={{0,1},{1,0},{2,3},{3,2},{4,5},{5,4},{6,7},{7,6},{8,9},{9,8},{10,11... | collective-permute-start | bytes 184328 | tf_op jit(solution)/shard_map/ppermute | solution.py:410
  57.4 2.7 %collective-permute-start.24 = (bf16[192,128]{1,0:T(8,128)(2,1)S(1)}, bf16[192,128]{1,0:T(8,128)(2,1)S(1)}, u32[]{:S(2)}, u32[]{:S(2)}) collective-permute-start(bf16[192,128]{1,0:T(8,128)(2,1)S(1)} %get-tuple-element.143.refs_0_), channel_id=1, source_target_pairs={{0,3},{1,2},{2,1},{3,0},{4,7},{5,6},{6,5},{7,4},{8,11},{9,10},{10,... | collective-permute-start | bytes 147464 | tf_op jit(solution)/shard_map/ppermute | solution.py:410
  60.1 1.7 %collective-permute-start.26 = (bf16[192,128]{1,0:T(8,128)(2,1)S(1)}, bf16[192,128]{1,0:T(8,128)(2,1)S(1)}, u32[]{:S(2)}, u32[]{:S(2)}) collective-permute-start(bf16[192,128]{1,0:T(8,128)(2,1)S(1)} %get-tuple-element.143.refs_0_), channel_id=1, source_target_pairs={{0,1},{1,0},{2,3},{3,2},{4,5},{5,4},{6,7},{7,6},{8,9},{9,8},{10,11... | collective-permute-start | bytes 147464 | tf_op jit(solution)/shard_map/ppermute | solution.py:410
  61.9 1.0 %collective-permute-start.27 = (bf16[464,128]{1,0:T(8,128)(2,1)S(1)}, bf16[464,128]{1,0:T(8,128)(2,1)S(1)}, u32[]{:S(2)}, u32[]{:S(2)}) collective-permute-start(bf16[464,128]{1,0:T(8,128)(2,1)S(1)} %filt_sum.1.refs_0_), channel_id=1, source_target_pairs={{0,8},{4,12},{8,0},{12,4},{16,24},{20,28},{24,16},{28,20},{1,9},{5... | collective-permute-start | bytes 356360 | tf_op jit(solution)/shard_map/ppermute | solution.py:410
  62.9 1.0 %collective-permute-start.28 = (bf16[464,128]{1,0:T(8,128)(2,1)S(1)}, bf16[464,128]{1,0:T(8,128)(2,1)S(1)}, u32[]{:S(2)}, u32[]{:S(2)}) collective-permute-start(bf16[464,128]{1,0:T(8,128)(2,1)S(1)} %filt_sum.1.refs_0_), channel_id=1, source_target_pairs={{0,16},{4,20},{8,24},{12,28},{16,0},{20,4},{24,8},{28,12},{1,17},{... | collective-permute-start | bytes 356360 | tf_op jit(solution)/shard_map/ppermute | solution.py:410
  63.9 1.6 %collective-permute-start.29 = (bf16[464,128]{1,0:T(8,128)(2,1)S(1)}, bf16[464,128]{1,0:T(8,128)(2,1)S(1)}, u32[]{:S(2)}, u32[]{:S(2)}) collective-permute-start(bf16[464,128]{1,0:T(8,128)(2,1)S(1)} %filt_sum.1.refs_0_), channel_id=1, source_target_pairs={{0,24},{4,28},{8,16},{12,20},{16,8},{20,12},{24,0},{28,4},{1,25},{... | collective-permute-start | bytes 356360 | tf_op jit(solution)/shard_map/ppermute | solution.py:410
  65.5 0.9 %collective-permute-start.31 = (bf16[192,128]{1,0:T(8,128)(2,1)S(1)}, bf16[192,128]{1,0:T(8,128)(2,1)S(1)}, u32[]{:S(2)}, u32[]{:S(2)}) collective-permute-start(bf16[192,128]{1,0:T(8,128)(2,1)S(1)} %filt_sum_rest.1.refs_4_), channel_id=1, source_target_pairs={{0,16},{4,20},{8,24},{12,28},{16,0},{20,4},{24,8},{28,12},{1,17},{... | collective-permute-start | bytes 147464 | tf_op jit(solution)/shard_map/ppermute | solution.py:410
  66.4 1.5 %collective-permute-start.32 = (bf16[192,128]{1,0:T(8,128)(2,1)S(1)}, bf16[192,128]{1,0:T(8,128)(2,1)S(1)}, u32[]{:S(2)}, u32[]{:S(2)}) collective-permute-start(bf16[192,128]{1,0:T(8,128)(2,1)S(1)} %filt_sum_rest.1.refs_4_), channel_id=1, source_target_pairs={{0,24},{4,28},{8,16},{12,20},{16,8},{20,12},{24,0},{28,4},{1,25},{... | collective-permute-start | bytes 147464 | tf_op jit(solution)/shard_map/ppermute | solution.py:410
  68.0 1.0 %collective-permute-start.30 = (bf16[192,128]{1,0:T(8,128)(2,1)S(1)}, bf16[192,128]{1,0:T(8,128)(2,1)S(1)}, u32[]{:S(2)}, u32[]{:S(2)}) collective-permute-start(bf16[192,128]{1,0:T(8,128)(2,1)S(1)} %filt_sum_rest.1.refs_4_), channel_id=1, source_target_pairs={{0,8},{4,12},{8,0},{12,4},{16,24},{20,28},{24,16},{28,20},{1,9},{5... | collective-permute-start | bytes 147464 | tf_op jit(solution)/shard_map/ppermute | solution.py:410
  69.0 3.0 %collective-permute-done.31.refs_6_ = bf16[192,128]{1,0:T(8,128)(2,1)S(1)} collective-permute-done((bf16[192,128]{1,0:T(8,128)(2,1)S(1)}, bf16[192,128]{1,0:T(8,128)(2,1)S(1)}, u32[]{:S(2)}, u32[]{:S(2)}) %collective-permute-start.31) | collective-permute-done | bytes 49184 | tf_op jit(solution)/shard_map/ppermute | solution.py:410
  72.3 1.1 %finish_own.1 = (f32[27,128,128]{2,1,0:T(8,128)}, f32[27,64,128]{2,1,0:T(8,128)}) custom-call(bf16[4,656,128]{2,1,0:T(8,128)(2,1)S(1)} %stack.1.pieces), custom_call_target="tpu_custom_call" | custom-call | bytes 1048576 | tf_op jit(solution)/shard_map/finish_own/pallas_call | solution.py:23
  73.4 1.0 %collective-permute-done.33.pieces = bf16[4,656,128]{2,1,0:T(8,128)(2,1)S(1)} collective-permute-done((bf16[4,656,128]{2,1,0:T(8,128)(2,1)S(1)}, bf16[4,656,128]{2,1,0:T(8,128)(2,1)S(1)}, u32[]{:S(2)}, u32[]{:S(2)}) %collective-permute-start.33) | collective-permute-done | bytes 671776 | tf_op jit(solution)/shard_map/ppermute | solution.py:417
  74.4 1.1 %finish_other.1 = (f32[27,128,128]{2,1,0:T(8,128)}, f32[27,64,128]{2,1,0:T(8,128)}) custom-call(bf16[4,656,128]{2,1,0:T(8,128)(2,1)S(1)} %collective-permute-done.33.pieces, f32[27,128,128]{2,1,0:T(8,128)} %get-tuple-element.149.refs_0_, f32[27,64,128]{2,1,0:T(8,128)} %get-tuple-element.150.refs_1_), custom_call_target="tpu_custom_call", output_to_operand_aliasing={{0}: (1, {}), {1}: (2, {})} | custom-call | bytes 1048576 | tf_op jit(solution)/shard_map/finish_other/pallas_call | solution.py:23
  (50 shorter events, 1.7 us)
Async XLA Ops:
  1.4 8.8 %copy-start = (bf16[4,16,16,128]{3,2,1,0:T(8,128)(2,1)S(1)}, bf16[4,16,16,128]{3,2,1,0:T(8,128)(2,1)}, u32[]{:S(2)}) copy-start(bf16[4,16,16,128]{3,2,1,0:T(8,128)(2,1)} %center.1) | copy-start | bytes 786436
  1.4 11.5 %copy-start.1 = (bf16[27,128,128]{2,1,0:T(8,128)(2,1)S(1)}, bf16[27,128,128]{2,1,0:T(8,128)(2,1)}, u32[]{:S(2)}) copy-start(bf16[27,128,128]{2,1,0:T(8,128)(2,1)} %w.1) | copy-start | bytes 2654212
  1.4 5.6 %collective-permute-start = (bf16[4,2,16,128]{3,2,1,0:T(8,128)(2,1)S(1)}, bf16[4,2,16,128]{3,2,1,0:T(8,128)(2,1)S(1)}, u32[]{:S(2)}, u32[]{:S(2)}) collective-permute-start(bf16[4,2,16,128]{3,2,1,0:T(8,128)(2,1)S(1)} %edges.1), channel_id=1, source_target_pairs={{0,1},{2,3},{1,0},{3,2},{4,5},{6,7},{5,4},{7,6},{8,9},{10,11},{9,8... | collective-permute-start | bytes 98312 | tf_op jit(solution)/shard_map/ppermute | solution.py:427
  4.5 5.7 %collective-permute-start.1 = (bf16[4,2,16,128]{3,2,1,0:T(8,128)(2,1)S(1)}, bf16[4,2,16,128]{3,2,1,0:T(8,128)(2,1)S(1)}, u32[]{:S(2)}, u32[]{:S(2)}) collective-permute-start(bf16[4,2,16,128]{3,2,1,0:T(8,128)(2,1)S(1)} %edges.1), channel_id=1, source_target_pairs={{1,2},{3,0},{2,1},{0,3},{5,6},{7,4},{6,5},{4,7},{9,10},{11,8},{10,... | collective-permute-start | bytes 98312 | tf_op jit(solution)/shard_map/ppermute | solution.py:427
  10.3 2.6 %collective-permute-start.2 = (bf16[3,18,16,128]{3,2,1,0:T(8,128)(2,1)S(1)}, bf16[3,18,16,128]{3,2,1,0:T(8,128)(2,1)S(1)}, u32[]{:S(2)}, u32[]{:S(2)}) collective-permute-start(bf16[3,18,16,128]{3,2,1,0:T(8,128)(2,1)S(1)} %get-tuple-element.80), channel_id=1, source_target_pairs={{0,4},{8,12},{16,20},{24,28},{4,0},{12,8},{20,16},{28,24},{1,5},{9... | collective-permute-start | bytes 663560 | tf_op jit(solution)/shard_map/ppermute | solution.py:427
  10.4 9.3 %collective-permute-start.3 = (bf16[3,18,16,128]{3,2,1,0:T(8,128)(2,1)S(1)}, bf16[3,18,16,128]{3,2,1,0:T(8,128)(2,1)S(1)}, u32[]{:S(2)}, u32[]{:S(2)}) collective-permute-start(bf16[3,18,16,128]{3,2,1,0:T(8,128)(2,1)S(1)} %get-tuple-element.82), channel_id=1, source_target_pairs={{4,8},{12,16},{20,24},{28,0},{8,4},{16,12},{24,20},{0,28},{5,9},{1... | collective-permute-start | bytes 663560 | tf_op jit(solution)/shard_map/ppermute | solution.py:427
  15.2 9.0 %collective-permute-start.7 = (bf16[2,64,128]{2,1,0:T(8,128)(2,1)S(1)}, bf16[2,64,128]{2,1,0:T(8,128)(2,1)S(1)}, u32[]{:S(2)}, u32[]{:S(2)}) collective-permute-start(bf16[2,64,128]{2,1,0:T(8,128)(2,1)S(1)} %get-tuple-element.92.refs_4_), channel_id=1, source_target_pairs={{0,3},{1,2},{2,1},{3,0},{4,7},{5,6},{6,5},{7,4},{8,11},{9,10},{10,... | collective-permute-start | bytes 98312 | tf_op jit(solution)/shard_map/ppermute | solution.py:410
  17.7 8.4 %collective-permute-start.8 = (bf16[2,64,128]{2,1,0:T(8,128)(2,1)S(1)}, bf16[2,64,128]{2,1,0:T(8,128)(2,1)S(1)}, u32[]{:S(2)}, u32[]{:S(2)}) collective-permute-start(bf16[2,64,128]{2,1,0:T(8,128)(2,1)S(1)} %get-tuple-element.92.refs_4_), channel_id=1, source_target_pairs={{0,2},{1,3},{2,0},{3,1},{4,6},{5,7},{6,4},{7,5},{8,10},{9,11},{10,... | collective-permute-start | bytes 98312 | tf_op jit(solution)/shard_map/ppermute | solution.py:410
  17.7 8.4 %collective-permute-start.9 = (bf16[2,64,128]{2,1,0:T(8,128)(2,1)S(1)}, bf16[2,64,128]{2,1,0:T(8,128)(2,1)S(1)}, u32[]{:S(2)}, u32[]{:S(2)}) collective-permute-start(bf16[2,64,128]{2,1,0:T(8,128)(2,1)S(1)} %get-tuple-element.92.refs_4_), channel_id=1, source_target_pairs={{0,1},{1,0},{2,3},{3,2},{4,5},{5,4},{6,7},{7,6},{8,9},{9,8},{10,11... | collective-permute-start | bytes 98312 | tf_op jit(solution)/shard_map/ppermute | solution.py:410
  21.7 5.8 %collective-permute-start.4 = (bf16[2,64,128]{2,1,0:T(8,128)(2,1)S(1)}, bf16[2,64,128]{2,1,0:T(8,128)(2,1)S(1)}, u32[]{:S(2)}, u32[]{:S(2)}) collective-permute-start(bf16[2,64,128]{2,1,0:T(8,128)(2,1)S(1)} %get-tuple-element.88.refs_0_), channel_id=1, source_target_pairs={{0,3},{1,2},{2,1},{3,0},{4,7},{5,6},{6,5},{7,4},{8,11},{9,10},{10,... | collective-permute-start | bytes 98312 | tf_op jit(solution)/shard_map/ppermute | solution.py:410
  24.2 4.8 %collective-permute-start.5 = (bf16[2,64,128]{2,1,0:T(8,128)(2,1)S(1)}, bf16[2,64,128]{2,1,0:T(8,128)(2,1)S(1)}, u32[]{:S(2)}, u32[]{:S(2)}) collective-permute-start(bf16[2,64,128]{2,1,0:T(8,128)(2,1)S(1)} %get-tuple-element.88.refs_0_), channel_id=1, source_target_pairs={{0,2},{1,3},{2,0},{3,1},{4,6},{5,7},{6,4},{7,5},{8,10},{9,11},{10,... | collective-permute-start | bytes 98312 | tf_op jit(solution)/shard_map/ppermute | solution.py:410
  24.2 4.8 %collective-permute-start.6 = (bf16[2,64,128]{2,1,0:T(8,128)(2,1)S(1)}, bf16[2,64,128]{2,1,0:T(8,128)(2,1)S(1)}, u32[]{:S(2)}, u32[]{:S(2)}) collective-permute-start(bf16[2,64,128]{2,1,0:T(8,128)(2,1)S(1)} %get-tuple-element.88.refs_0_), channel_id=1, source_target_pairs={{0,1},{1,0},{2,3},{3,2},{4,5},{5,4},{6,7},{7,6},{8,9},{9,8},{10,11... | collective-permute-start | bytes 98312 | tf_op jit(solution)/shard_map/ppermute | solution.py:410
  26.1 2.9 %copy-start.2 = (bf16[27,128,64]{1,2,0:T(8,128)(2,1)S(1)}, bf16[27,128,64]{1,2,0:T(8,128)(2,1)}, u32[]{:S(2)}) copy-start(bf16[27,128,64]{1,2,0:T(8,128)(2,1)} %param.6) | copy-start | bytes 1327108
  26.1 2.9 %copy-start.3 = (bf16[2,32,8,64]{3,2,1,0:T(8,128)(2,1)S(1)}, bf16[2,32,8,64]{3,2,1,0:T(8,128)(2,1)}, u32[]{:S(2)}) copy-start(bf16[2,32,8,64]{3,2,1,0:T(8,128)(2,1)} %refs_9_.1) | copy-start | bytes 196612
  31.2 6.1 %collective-permute-start.10 = (bf16[4,64,128]{2,1,0:T(8,128)(2,1)S(1)}, bf16[4,64,128]{2,1,0:T(8,128)(2,1)S(1)}, u32[]{:S(2)}, u32[]{:S(2)}) collective-permute-start(bf16[4,64,128]{2,1,0:T(8,128)(2,1)S(1)} %get-tuple-element.101), channel_id=1, source_target_pairs={{0,3},{1,2},{2,1},{3,0},{4,7},{5,6},{6,5},{7,4},{8,11},{9,10},{10,... | collective-permute-start | bytes 196616 | tf_op jit(solution)/shard_map/ppermute | solution.py:410
  33.0 5.9 %collective-permute-start.11 = (bf16[4,64,128]{2,1,0:T(8,128)(2,1)S(1)}, bf16[4,64,128]{2,1,0:T(8,128)(2,1)S(1)}, u32[]{:S(2)}, u32[]{:S(2)}) collective-permute-start(bf16[4,64,128]{2,1,0:T(8,128)(2,1)S(1)} %get-tuple-element.103), channel_id=1, source_target_pairs={{0,2},{1,3},{2,0},{3,1},{4,6},{5,7},{6,4},{7,5},{8,10},{9,11},{10,... | collective-permute-start | bytes 196616 | tf_op jit(solution)/shard_map/ppermute | solution.py:410
  33.7 5.2 %collective-permute-start.12 = (bf16[4,64,128]{2,1,0:T(8,128)(2,1)S(1)}, bf16[4,64,128]{2,1,0:T(8,128)(2,1)S(1)}, u32[]{:S(2)}, u32[]{:S(2)}) collective-permute-start(bf16[4,64,128]{2,1,0:T(8,128)(2,1)S(1)} %get-tuple-element.104), channel_id=1, source_target_pairs={{0,1},{1,0},{2,3},{3,2},{4,5},{5,4},{6,7},{7,6},{8,9},{9,8},{10,11... | collective-permute-start | bytes 196616 | tf_op jit(solution)/shard_map/ppermute | solution.py:410
  40.0 1.6 %collective-permute-start.13 = (bf16[4,240,128]{2,1,0:T(8,128)(2,1)S(1)}, bf16[4,240,128]{2,1,0:T(8,128)(2,1)S(1)}, u32[]{:S(2)}, u32[]{:S(2)}) collective-permute-start(bf16[4,240,128]{2,1,0:T(8,128)(2,1)S(1)} %get-tuple-element.109), channel_id=1, source_target_pairs={{0,4},{4,0},{8,12},{12,8},{16,20},{20,16},{24,28},{28,24},{1,5},{5... | collective-permute-start | bytes 737288 | tf_op jit(solution)/shard_map/ppermute | solution.py:417
  42.3 4.4 %collective-permute-start.14 = (bf16[4,416,128]{2,1,0:T(8,128)(2,1)S(1)}, bf16[4,416,128]{2,1,0:T(8,128)(2,1)S(1)}, u32[]{:S(2)}, u32[]{:S(2)}) collective-permute-start(bf16[4,416,128]{2,1,0:T(8,128)(2,1)S(1)} %early_grad_rest.1), channel_id=1, source_target_pairs={{0,4},{4,0},{8,12},{12,8},{16,20},{20,16},{24,28},{28,24},{1,5},{5... | collective-permute-start | bytes 1277960 | tf_op jit(solution)/shard_map/ppermute | solution.py:417
  42.5 5.3 %collective-permute-start.15 = (bf16[240,128]{1,0:T(8,128)(2,1)S(1)}, bf16[240,128]{1,0:T(8,128)(2,1)S(1)}, u32[]{:S(2)}, u32[]{:S(2)}) collective-permute-start(bf16[240,128]{1,0:T(8,128)(2,1)S(1)} %get-tuple-element.119), channel_id=1, source_target_pairs={{0,24},{4,28},{8,16},{12,20},{16,8},{20,12},{24,0},{28,4},{1,25},{... | collective-permute-start | bytes 184328 | tf_op jit(solution)/shard_map/ppermute | solution.py:410
  43.9 5.1 %collective-permute-start.16 = (bf16[240,128]{1,0:T(8,128)(2,1)S(1)}, bf16[240,128]{1,0:T(8,128)(2,1)S(1)}, u32[]{:S(2)}, u32[]{:S(2)}) collective-permute-start(bf16[240,128]{1,0:T(8,128)(2,1)S(1)} %get-tuple-element.120), channel_id=1, source_target_pairs={{0,16},{4,20},{8,24},{12,28},{16,0},{20,4},{24,8},{28,12},{1,17},{... | collective-permute-start | bytes 184328 | tf_op jit(solution)/shard_map/ppermute | solution.py:410
  45.1 4.2 %collective-permute-start.17 = (bf16[240,128]{1,0:T(8,128)(2,1)S(1)}, bf16[240,128]{1,0:T(8,128)(2,1)S(1)}, u32[]{:S(2)}, u32[]{:S(2)}) collective-permute-start(bf16[240,128]{1,0:T(8,128)(2,1)S(1)} %get-tuple-element.121), channel_id=1, source_target_pairs={{0,8},{4,12},{8,0},{12,4},{16,24},{20,28},{24,16},{28,20},{1,9},{5... | collective-permute-start | bytes 184328 | tf_op jit(solution)/shard_map/ppermute | solution.py:410
  49.3 6.6 %collective-permute-start.18 = (bf16[416,128]{1,0:T(8,128)(2,1)S(1)}, bf16[416,128]{1,0:T(8,128)(2,1)S(1)}, u32[]{:S(2)}, u32[]{:S(2)}) collective-permute-start(bf16[416,128]{1,0:T(8,128)(2,1)S(1)} %get-tuple-element.123), channel_id=1, source_target_pairs={{0,24},{4,28},{8,16},{12,20},{16,8},{20,12},{24,0},{28,4},{1,25},{... | collective-permute-start | bytes 319496 | tf_op jit(solution)/shard_map/ppermute | solution.py:410
  50.7 6.6 %collective-permute-start.19 = (bf16[416,128]{1,0:T(8,128)(2,1)S(1)}, bf16[416,128]{1,0:T(8,128)(2,1)S(1)}, u32[]{:S(2)}, u32[]{:S(2)}) collective-permute-start(bf16[416,128]{1,0:T(8,128)(2,1)S(1)} %get-tuple-element.124), channel_id=1, source_target_pairs={{0,16},{4,20},{8,24},{12,28},{16,0},{20,4},{24,8},{28,12},{1,17},{... | collective-permute-start | bytes 319496 | tf_op jit(solution)/shard_map/ppermute | solution.py:410
  51.7 5.6 %collective-permute-start.20 = (bf16[416,128]{1,0:T(8,128)(2,1)S(1)}, bf16[416,128]{1,0:T(8,128)(2,1)S(1)}, u32[]{:S(2)}, u32[]{:S(2)}) collective-permute-start(bf16[416,128]{1,0:T(8,128)(2,1)S(1)} %get-tuple-element.125), channel_id=1, source_target_pairs={{0,8},{4,12},{8,0},{12,4},{16,24},{20,28},{24,16},{28,20},{1,9},{5... | collective-permute-start | bytes 319496 | tf_op jit(solution)/shard_map/ppermute | solution.py:410
  52.9 7.2 %collective-permute-start.21 = (bf16[240,128]{1,0:T(8,128)(2,1)S(1)}, bf16[240,128]{1,0:T(8,128)(2,1)S(1)}, u32[]{:S(2)}, u32[]{:S(2)}) collective-permute-start(bf16[240,128]{1,0:T(8,128)(2,1)S(1)} %chip_sum.1.refs_0_), channel_id=1, source_target_pairs={{0,3},{1,2},{2,1},{3,0},{4,7},{5,6},{6,5},{7,4},{8,11},{9,10},{10,... | collective-permute-start | bytes 184328 | tf_op jit(solution)/shard_map/ppermute | solution.py:410
  55.6 6.3 %collective-permute-start.22 = (bf16[240,128]{1,0:T(8,128)(2,1)S(1)}, bf16[240,128]{1,0:T(8,128)(2,1)S(1)}, u32[]{:S(2)}, u32[]{:S(2)}) collective-permute-start(bf16[240,128]{1,0:T(8,128)(2,1)S(1)} %chip_sum.1.refs_0_), channel_id=1, source_target_pairs={{0,2},{1,3},{2,0},{3,1},{4,6},{5,7},{6,4},{7,5},{8,10},{9,11},{10,... | collective-permute-start | bytes 184328 | tf_op jit(solution)/shard_map/ppermute | solution.py:410
  56.0 5.9 %collective-permute-start.23 = (bf16[240,128]{1,0:T(8,128)(2,1)S(1)}, bf16[240,128]{1,0:T(8,128)(2,1)S(1)}, u32[]{:S(2)}, u32[]{:S(2)}) collective-permute-start(bf16[240,128]{1,0:T(8,128)(2,1)S(1)} %chip_sum.1.refs_0_), channel_id=1, source_target_pairs={{0,1},{1,0},{2,3},{3,2},{4,5},{5,4},{6,7},{7,6},{8,9},{9,8},{10,11... | collective-permute-start | bytes 184328 | tf_op jit(solution)/shard_map/ppermute | solution.py:410
  57.4 6.5 %collective-permute-start.24 = (bf16[192,128]{1,0:T(8,128)(2,1)S(1)}, bf16[192,128]{1,0:T(8,128)(2,1)S(1)}, u32[]{:S(2)}, u32[]{:S(2)}) collective-permute-start(bf16[192,128]{1,0:T(8,128)(2,1)S(1)} %get-tuple-element.143.refs_0_), channel_id=1, source_target_pairs={{0,3},{1,2},{2,1},{3,0},{4,7},{5,6},{6,5},{7,4},{8,11},{9,10},{10,... | collective-permute-start | bytes 147464 | tf_op jit(solution)/shard_map/ppermute | solution.py:410
  60.1 5.4 %collective-permute-start.25 = (bf16[192,128]{1,0:T(8,128)(2,1)S(1)}, bf16[192,128]{1,0:T(8,128)(2,1)S(1)}, u32[]{:S(2)}, u32[]{:S(2)}) collective-permute-start(bf16[192,128]{1,0:T(8,128)(2,1)S(1)} %get-tuple-element.143.refs_0_), channel_id=1, source_target_pairs={{0,2},{1,3},{2,0},{3,1},{4,6},{5,7},{6,4},{7,5},{8,10},{9,11},{10,... | collective-permute-start | bytes 147464 | tf_op jit(solution)/shard_map/ppermute | solution.py:410
  60.1 5.4 %collective-permute-start.26 = (bf16[192,128]{1,0:T(8,128)(2,1)S(1)}, bf16[192,128]{1,0:T(8,128)(2,1)S(1)}, u32[]{:S(2)}, u32[]{:S(2)}) collective-permute-start(bf16[192,128]{1,0:T(8,128)(2,1)S(1)} %get-tuple-element.143.refs_0_), channel_id=1, source_target_pairs={{0,1},{1,0},{2,3},{3,2},{4,5},{5,4},{6,7},{7,6},{8,9},{9,8},{10,11... | collective-permute-start | bytes 147464 | tf_op jit(solution)/shard_map/ppermute | solution.py:410
  61.9 6.2 %collective-permute-start.27 = (bf16[464,128]{1,0:T(8,128)(2,1)S(1)}, bf16[464,128]{1,0:T(8,128)(2,1)S(1)}, u32[]{:S(2)}, u32[]{:S(2)}) collective-permute-start(bf16[464,128]{1,0:T(8,128)(2,1)S(1)} %filt_sum.1.refs_0_), channel_id=1, source_target_pairs={{0,8},{4,12},{8,0},{12,4},{16,24},{20,28},{24,16},{28,20},{1,9},{5... | collective-permute-start | bytes 356360 | tf_op jit(solution)/shard_map/ppermute | solution.py:410
  62.9 9.2 %collective-permute-start.28 = (bf16[464,128]{1,0:T(8,128)(2,1)S(1)}, bf16[464,128]{1,0:T(8,128)(2,1)S(1)}, u32[]{:S(2)}, u32[]{:S(2)}) collective-permute-start(bf16[464,128]{1,0:T(8,128)(2,1)S(1)} %filt_sum.1.refs_0_), channel_id=1, source_target_pairs={{0,16},{4,20},{8,24},{12,28},{16,0},{20,4},{24,8},{28,12},{1,17},{... | collective-permute-start | bytes 356360 | tf_op jit(solution)/shard_map/ppermute | solution.py:410
  63.9 8.2 %collective-permute-start.29 = (bf16[464,128]{1,0:T(8,128)(2,1)S(1)}, bf16[464,128]{1,0:T(8,128)(2,1)S(1)}, u32[]{:S(2)}, u32[]{:S(2)}) collective-permute-start(bf16[464,128]{1,0:T(8,128)(2,1)S(1)} %filt_sum.1.refs_0_), channel_id=1, source_target_pairs={{0,24},{4,28},{8,16},{12,20},{16,8},{20,12},{24,0},{28,4},{1,25},{... | collective-permute-start | bytes 356360 | tf_op jit(solution)/shard_map/ppermute | solution.py:410
  65.5 6.6 %collective-permute-start.31 = (bf16[192,128]{1,0:T(8,128)(2,1)S(1)}, bf16[192,128]{1,0:T(8,128)(2,1)S(1)}, u32[]{:S(2)}, u32[]{:S(2)}) collective-permute-start(bf16[192,128]{1,0:T(8,128)(2,1)S(1)} %filt_sum_rest.1.refs_4_), channel_id=1, source_target_pairs={{0,16},{4,20},{8,24},{12,28},{16,0},{20,4},{24,8},{28,12},{1,17},{... | collective-permute-start | bytes 147464 | tf_op jit(solution)/shard_map/ppermute | solution.py:410
  66.4 5.7 %collective-permute-start.32 = (bf16[192,128]{1,0:T(8,128)(2,1)S(1)}, bf16[192,128]{1,0:T(8,128)(2,1)S(1)}, u32[]{:S(2)}, u32[]{:S(2)}) collective-permute-start(bf16[192,128]{1,0:T(8,128)(2,1)S(1)} %filt_sum_rest.1.refs_4_), channel_id=1, source_target_pairs={{0,24},{4,28},{8,16},{12,20},{16,8},{20,12},{24,0},{28,4},{1,25},{... | collective-permute-start | bytes 147464 | tf_op jit(solution)/shard_map/ppermute | solution.py:410
  68.0 4.1 %collective-permute-start.30 = (bf16[192,128]{1,0:T(8,128)(2,1)S(1)}, bf16[192,128]{1,0:T(8,128)(2,1)S(1)}, u32[]{:S(2)}, u32[]{:S(2)}) collective-permute-start(bf16[192,128]{1,0:T(8,128)(2,1)S(1)} %filt_sum_rest.1.refs_4_), channel_id=1, source_target_pairs={{0,8},{4,12},{8,0},{12,4},{16,24},{20,28},{24,16},{28,20},{1,9},{5... | collective-permute-start | bytes 147464 | tf_op jit(solution)/shard_map/ppermute | solution.py:410
  72.2 2.2 %collective-permute-start.33 = (bf16[4,656,128]{2,1,0:T(8,128)(2,1)S(1)}, bf16[4,656,128]{2,1,0:T(8,128)(2,1)S(1)}, u32[]{:S(2)}, u32[]{:S(2)}) collective-permute-start(bf16[4,656,128]{2,1,0:T(8,128)(2,1)S(1)} %stack.1.pieces), channel_id=1, source_target_pairs={{0,4},{4,0},{8,12},{12,8},{16,20},{20,16},{24,28},{28,24},{1,5},{5... | collective-permute-start | bytes 2015240 | tf_op jit(solution)/shard_map/ppermute | solution.py:417

commit v5 on v2

--- a/solution.py
+++ b/solution.py
@@ -523,7 +523,7 @@
         flops=2 * dx * dy * dz * 27 * width * filters,
     )
     deep_first, terms[-1] = lax.optimization_barrier((deep_first, terms[-1]))
-    cuts = ((0, 5), (5, 9))
+    cuts = ((0, 4), (4, 9))
     steps = [3 * (end - begin) * (cin // 2) // chips for begin, end in cuts]
     flops = 2 * (nx + 4) * rows * 18 * cin * 2 * width
     helds = [pltpu.VMEM((step * chips, width), F32) for step in steps]

time: 75.6 us -> 75.8 us (level)
  waiting for transfers between devices: 15.1 us -> 16 us
    ppermute x27, waiting for transfers between devices: 10.3 us -> 11.1 us  [paired(): lax.ppermute(values[j], axis, [(i, i ^ step * j) for i in range(count)])]
  transfers between devices with their start and end apart: 34 -> 34, of which waited for: 12 -> 16; matrix products, arithmetic and copies ran while one was open for 0% -> 0% of each run, Pallas kernels for 12% -> 12%
where the time goes in v5:
time: 75.8 us; the launch traced here: 75.7 us
  starting transfers between devices  44.1 us (58%)
  waiting for transfers between devices  16 us (21%)
  Pallas kernels  14 us (18%)
  between operations  0.82 us (1%)
  local copies, waits for them, and re-layouts  0.76 us (1%)
    ppermute x27, starting transfers between devices, paired(): lax.ppermute(values[j], axis, [(i, i ^ step * j) for i in range(count)])  35.5 us
    pallas_call x20, Pallas kernels, call(): pl.pallas_call(body, name=name, out_shape=out_shape, in_specs=[HBM if i i...  14 us
    ppermute x27, waiting for transfers between devices, paired(): lax.ppermute(values[j], axis, [(i, i ^ step * j) for i in range(count)])  11.1 us
    ppermute x4, starting transfers between devices, swap(): return lax.ppermute(value, axis, pairs + [(b, a) for a, b in pairs])  8.18 us
    ppermute x4, waiting for transfers between devices, swap(): return lax.ppermute(value, axis, pairs + [(b, a) for a, b in pairs])  3.24 us
    ppermute x3, waiting for transfers between devices, exchange(): lax.ppermute(value, axis, [(i, i ^ step) for i in range(lax.axis_size(axi...  1.67 us
  transfers between devices with their start and end apart: 34, of which 16 were waited for; matrix products, arithmetic and copies ran while one was open for 0% of the time, Pallas kernels for 12%

profile of v5, /device:TPU:0, one launch (start us, length us, event | category | flops | bytes accessed | tf_op | source)
XLA Modules:
  0.0 75.7 jit_solution(17537182991305550978)
XLA Ops:
  0.6 0.7 fusion
  1.4 3.1 %collective-permute-start = (bf16[4,2,16,128]{3,2,1,0:T(8,128)(2,1)S(1)}, bf16[4,2,16,128]{3,2,1,0:T(8,128)(2,1)S(1)}, u32[]{:S(2)}, u32[]{:S(2)}) collective-permute-start(bf16[4,2,16,128]{3,2,1,0:T(8,128)(2,1)S(1)} %edges.1), channel_id=1, source_target_pairs={{0,1},{2,3},{1,0},{3,2},{4,5},{6,7},{5,4},{7,6},{8,9},{10,11},{9,8... | collective-permute-start | bytes 98312 | tf_op jit(solution)/shard_map/ppermute | solution.py:423
  4.5 2.5 %collective-permute-start.1 = (bf16[4,2,16,128]{3,2,1,0:T(8,128)(2,1)S(1)}, bf16[4,2,16,128]{3,2,1,0:T(8,128)(2,1)S(1)}, u32[]{:S(2)}, u32[]{:S(2)}) collective-permute-start(bf16[4,2,16,128]{3,2,1,0:T(8,128)(2,1)S(1)} %edges.1), channel_id=1, source_target_pairs={{1,2},{3,0},{2,1},{0,3},{5,6},{7,4},{6,5},{4,7},{9,10},{11,8},{10,... | collective-permute-start | bytes 98312 | tf_op jit(solution)/shard_map/ppermute | solution.py:423
  7.0 3.2 %collective-permute-done.1.yodd = bf16[4,2,16,128]{3,2,1,0:T(8,128)(2,1)S(1)} collective-permute-done((bf16[4,2,16,128]{3,2,1,0:T(8,128)(2,1)S(1)}, bf16[4,2,16,128]{3,2,1,0:T(8,128)(2,1)S(1)}, u32[]{:S(2)}, u32[]{:S(2)}) %collective-permute-start.1) | collective-permute-done | bytes 32800 | tf_op jit(solution)/shard_map/ppermute | solution.py:423
  10.4 2.5 %collective-permute-start.3 = (bf16[3,18,16,128]{3,2,1,0:T(8,128)(2,1)S(1)}, bf16[3,18,16,128]{3,2,1,0:T(8,128)(2,1)S(1)}, u32[]{:S(2)}, u32[]{:S(2)}) collective-permute-start(bf16[3,18,16,128]{3,2,1,0:T(8,128)(2,1)S(1)} %get-tuple-element.82), channel_id=1, source_target_pairs={{4,8},{12,16},{20,24},{28,0},{8,4},{16,12},{24,20},{0,28},{5,9},{1... | collective-permute-start | bytes 663560 | tf_op jit(solution)/shard_map/ppermute | solution.py:423
  12.9 2.2 %early_near.1 = (bf16[3,7,128,512]{3,2,1,0:T(8,128)(2,1)S(1)}, f32[4,128,256]{2,1,0:T(8,128)S(1)}, bf16[2,64,128]{2,1,0:T(8,128)(2,1)S(1)}, bf16[9,512,256]{2,1,0:T(8,128)(2,1)S(1)}) custom-call(bf16[4,16,16,128]{3,2,1,0:T(8,128)(2,1)S(1)} %get-tuple-element.78.center, bf16[4,2,16,128]{3,2,1,0:T(8,128)(2,1)S(1)} %get-tuple-element.79.sides, ...), custom_call_target="tpu_custom_call" | custom-call | flops 1207959552 | bytes 1048576 | tf_op jit(solution)/shard_map/early_near/pallas_call | solution.py:23
  15.1 2.5 %collective-permute-start.7 = (bf16[2,64,128]{2,1,0:T(8,128)(2,1)S(1)}, bf16[2,64,128]{2,1,0:T(8,128)(2,1)S(1)}, u32[]{:S(2)}, u32[]{:S(2)}) collective-permute-start(bf16[2,64,128]{2,1,0:T(8,128)(2,1)S(1)} %get-tuple-element.92.refs_4_), channel_id=1, source_target_pairs={{0,3},{1,2},{2,1},{3,0},{4,7},{5,6},{6,5},{7,4},{8,11},{9,10},{10,... | collective-permute-start | bytes 98312 | tf_op jit(solution)/shard_map/ppermute | solution.py:406
  17.7 1.9 %collective-permute-start.9 = (bf16[2,64,128]{2,1,0:T(8,128)(2,1)S(1)}, bf16[2,64,128]{2,1,0:T(8,128)(2,1)S(1)}, u32[]{:S(2)}, u32[]{:S(2)}) collective-permute-start(bf16[2,64,128]{2,1,0:T(8,128)(2,1)S(1)} %get-tuple-element.92.refs_4_), channel_id=1, source_target_pairs={{0,1},{1,0},{2,3},{3,2},{4,5},{5,4},{6,7},{7,6},{8,9},{9,8},{10,11... | collective-permute-start | bytes 98312 | tf_op jit(solution)/shard_map/ppermute | solution.py:406
  19.6 2.0 %early_far.1 = (bf16[3,3,128,512]{3,2,1,0:T(8,128)(2,1)S(1)}, f32[4,128,256]{2,1,0:T(8,128)S(1)}, bf16[2,64,128]{2,1,0:T(8,128)(2,1)S(1)}) custom-call(bf16[3,7,128,512]{3,2,1,0:T(8,128)(2,1)S(1)} %get-tuple-element.86.windows, bf16[3,18,16,128]{3,2,1,0:T(8,128)(2,1)S(1)} %collective-permute-done.3.far, bf16[9,512,256]{2,1,0:T(8,128)(2,1)S(1)} %get-tuple-element.83.wide), custom_call_target="tpu_custom_call" | custom-call | flops 1207959552 | bytes 1048576 | tf_op jit(solution)/shard_map/early_far/pallas_call | solution.py:23
  21.5 2.5 %collective-permute-start.4 = (bf16[2,64,128]{2,1,0:T(8,128)(2,1)S(1)}, bf16[2,64,128]{2,1,0:T(8,128)(2,1)S(1)}, u32[]{:S(2)}, u32[]{:S(2)}) collective-permute-start(bf16[2,64,128]{2,1,0:T(8,128)(2,1)S(1)} %get-tuple-element.88.refs_0_), channel_id=1, source_target_pairs={{0,3},{1,2},{2,1},{3,0},{4,7},{5,6},{6,5},{7,4},{8,11},{9,10},{10,... | collective-permute-start | bytes 98312 | tf_op jit(solution)/shard_map/ppermute | solution.py:406
  24.1 1.9 %collective-permute-start.6 = (bf16[2,64,128]{2,1,0:T(8,128)(2,1)S(1)}, bf16[2,64,128]{2,1,0:T(8,128)(2,1)S(1)}, u32[]{:S(2)}, u32[]{:S(2)}) collective-permute-start(bf16[2,64,128]{2,1,0:T(8,128)(2,1)S(1)} %get-tuple-element.88.refs_0_), channel_id=1, source_target_pairs={{0,1},{1,0},{2,3},{3,2},{4,5},{5,4},{6,7},{7,6},{8,9},{9,8},{10,11... | collective-permute-start | bytes 98312 | tf_op jit(solution)/shard_map/ppermute | solution.py:406
  26.0 1.1 %turn_windows.1.refs_6_.refs_1_ = bf16[3,2,256,1280]{3,2,1,0:T(8,128)(2,1)S(1)} custom-call(bf16[3,7,128,512]{3,2,1,0:T(8,128)(2,1)S(1)} %get-tuple-element.86.windows, bf16[3,3,128,512]{3,2,1,0:T(8,128)(2,1)S(1)} %get-tuple-element.87.far_windows), custom_call_target="tpu_custom_call" | custom-call | flops 1073741824 | bytes 1048576 | tf_op jit(solution)/shard_map/turn_windows/pallas_call | solution.py:23
  27.3 1.6 %collective-permute-done.5.refs_2_ = bf16[2,64,128]{2,1,0:T(8,128)(2,1)S(1)} collective-permute-done((bf16[2,64,128]{2,1,0:T(8,128)(2,1)S(1)}, bf16[2,64,128]{2,1,0:T(8,128)(2,1)S(1)}, u32[]{:S(2)}, u32[]{:S(2)}) %collective-permute-start.5) | collective-permute-done | bytes 32800 | tf_op jit(solution)/shard_map/ppermute | solution.py:406
  28.9 2.1 %deep_conv.1 = (bf16[2,32,8,64]{3,2,1,0:T(8,128)(2,1)}, bf16[2,256,64]{2,1,0:T(8,128)(2,1)S(1)}, bf16[3,4,256,384]{3,2,1,0:T(8,128)(2,1)S(1)}, f32[4,64,128]{2,1...) custom-call(bf16[2,64,128]{2,1,0:T(8,128)(2,1)S(1)} %get-tuple-eleme, ...), custom_call_target="tpu_custom_call" | custom-call | flops 452984832 | bytes 1048576 | tf_op jit(solution)/shard_map/deep_conv/pallas_call | solution.py:23
  31.0 1.9 %collective-permute-start.10 = (bf16[4,64,128]{2,1,0:T(8,128)(2,1)S(1)}, bf16[4,64,128]{2,1,0:T(8,128)(2,1)S(1)}, u32[]{:S(2)}, u32[]{:S(2)}) collective-permute-start(bf16[4,64,128]{2,1,0:T(8,128)(2,1)S(1)} %get-tuple-element.101), channel_id=1, source_target_pairs={{0,3},{1,2},{2,1},{3,0},{4,7},{5,6},{6,5},{7,4},{8,11},{9,10},{10,... | collective-permute-start | bytes 196616 | tf_op jit(solution)/shard_map/ppermute | solution.py:406
  33.6 1.9 %collective-permute-start.12 = (bf16[4,64,128]{2,1,0:T(8,128)(2,1)S(1)}, bf16[4,64,128]{2,1,0:T(8,128)(2,1)S(1)}, u32[]{:S(2)}, u32[]{:S(2)}) collective-permute-start(bf16[4,64,128]{2,1,0:T(8,128)(2,1)S(1)} %get-tuple-element.104), channel_id=1, source_target_pairs={{0,1},{1,0},{2,3},{3,2},{4,5},{5,4},{6,7},{7,6},{8,9},{9,8},{10,11... | collective-permute-start | bytes 196616 | tf_op jit(solution)/shard_map/ppermute | solution.py:406
  35.5 0.7 deep_grad.1
  36.2 0.9 %collective-permute-done.10.refs_1_ = bf16[4,64,128]{2,1,0:T(8,128)(2,1)S(1)} collective-permute-done((bf16[4,64,128]{2,1,0:T(8,128)(2,1)S(1)}, bf16[4,64,128]{2,1,0:T(8,128)(2,1)S(1)}, u32[]{:S(2)}, u32[]{:S(2)}) %collective-permute-start.10) | collective-permute-done | bytes 65568 | tf_op jit(solution)/shard_map/ppermute | solution.py:406
  37.2 1.6 %collective-permute-done.11.refs_2_ = bf16[4,64,128]{2,1,0:T(8,128)(2,1)S(1)} collective-permute-done((bf16[4,64,128]{2,1,0:T(8,128)(2,1)S(1)}, bf16[4,64,128]{2,1,0:T(8,128)(2,1)S(1)}, u32[]{:S(2)}, u32[]{:S(2)}) %collective-permute-start.11) | collective-permute-done | bytes 65568 | tf_op jit(solution)/shard_map/ppermute | solution.py:406
  38.8 0.8 %early_grad.1 = (bf16[4,192,128]{2,1,0:T(8,128)(2,1)S(1)}, bf16[8,128,256]{2,1,0:T(8,128)(2,1)S(1)}) custom-call(f32[4,64,128]{2,1,0:T(8,128)S(1)} %get-tuple-element.97.refs_0_, bf16[4,64,128]{2,1,0:T(8,128)(2,1)S(1)} %collective-permute-done.10.refs_1_, bf16[4,64,128]{2,1,0:T(8,128)(2,1)S(1)} %collective-permute-done.11.refs_2_, ...), custom_call_target="tpu_custom_call" | custom-call | flops 1207959552 | bytes 1048576 | tf_op jit(solution)/shard_map/early_grad/pallas_call | solution.py:23
  39.7 0.7 early_grad_own.1.mine
  40.4 0.7 collective-permute-done.13.other
  41.1 0.8 %early_grad_rest.1 = bf16[4,464,128]{2,1,0:T(8,128)(2,1)S(1)} custom-call(bf16[8,128,256]{2,1,0:T(8,128)(2,1)S(1)} %get-tuple-element.111.refs_0_, bf16[3,2,256,1280]{3,2,1,0:T(8,128)(2,1)S(1)} %turn_windows.1.refs_6_.refs_1_, bf16[4,224,128]{2,1,0:T(8,128)(2,1)S(1)} %get-tuple-element.113.refs_2_), custom_call_target="tpu_custom_call" | custom-call | flops 1207959552 | bytes 1048576 | tf_op jit(solution)/shard_map/early_grad_rest/pallas_call | solution.py:23
  42.2 1.7 %collective-permute-start.15 = (bf16[192,128]{1,0:T(8,128)(2,1)S(1)}, bf16[192,128]{1,0:T(8,128)(2,1)S(1)}, u32[]{:S(2)}, u32[]{:S(2)}) collective-permute-start(bf16[192,128]{1,0:T(8,128)(2,1)S(1)} %get-tuple-element.119), channel_id=1, source_target_pairs={{0,24},{4,28},{8,16},{12,20},{16,8},{20,12},{24,0},{28,4},{1,25},{... | collective-permute-start | bytes 147464 | tf_op jit(solution)/shard_map/ppermute | solution.py:406
  43.9 1.0 %collective-permute-start.16 = (bf16[192,128]{1,0:T(8,128)(2,1)S(1)}, bf16[192,128]{1,0:T(8,128)(2,1)S(1)}, u32[]{:S(2)}, u32[]{:S(2)}) collective-permute-start(bf16[192,128]{1,0:T(8,128)(2,1)S(1)} %get-tuple-element.120), channel_id=1, source_target_pairs={{0,16},{4,20},{8,24},{12,28},{16,0},{20,4},{24,8},{28,12},{1,17},{... | collective-permute-start | bytes 147464 | tf_op jit(solution)/shard_map/ppermute | solution.py:406
  44.9 0.8 %collective-permute-start.17 = (bf16[192,128]{1,0:T(8,128)(2,1)S(1)}, bf16[192,128]{1,0:T(8,128)(2,1)S(1)}, u32[]{:S(2)}, u32[]{:S(2)}) collective-permute-start(bf16[192,128]{1,0:T(8,128)(2,1)S(1)} %get-tuple-element.121), channel_id=1, source_target_pairs={{0,8},{4,12},{8,0},{12,4},{16,24},{20,28},{24,16},{28,20},{1,9},{5... | collective-permute-start | bytes 147464 | tf_op jit(solution)/shard_map/ppermute | solution.py:406
  45.7 0.8 %early_grad_rest_own.1.mine = f32[4,464,128]{2,1,0:T(8,128)S(1)} custom-call(bf16[8,128,256]{2,1,0:T(8,128)(2,1)S(1)} %get-tuple-element.111.refs_0_, bf16[3,2,256,1280]{3,2,1,0:T(8,128)(2,1)S(1)} %turn_windows.1.refs_6_.refs_1_, f32[4,224,128]{2,1,0:T(8,128)S(1)} %get-tuple-element.112.refs_2_), custom_call_target="tpu_custom_call" | custom-call | flops 1207959552 | bytes 1048576 | tf_op jit(solution)/shard_map/early_grad_rest_own/pallas_call | solution.py:23
  47.3 0.9 %collective-permute-done.16.refs_2_ = bf16[192,128]{1,0:T(8,128)(2,1)S(1)} collective-permute-done((bf16[192,128]{1,0:T(8,128)(2,1)S(1)}, bf16[192,128]{1,0:T(8,128)(2,1)S(1)}, u32[]{:S(2)}, u32[]{:S(2)}) %collective-permute-start.16) | collective-permute-done | bytes 49184 | tf_op jit(solution)/shard_map/ppermute | solution.py:406
  48.2 0.8 %collective-permute-done.17.refs_3_ = bf16[192,128]{1,0:T(8,128)(2,1)S(1)} collective-permute-done((bf16[192,128]{1,0:T(8,128)(2,1)S(1)}, bf16[192,128]{1,0:T(8,128)(2,1)S(1)}, u32[]{:S(2)}, u32[]{:S(2)}) %collective-permute-start.17) | collective-permute-done | bytes 49184 | tf_op jit(solution)/shard_map/ppermute | solution.py:406
  49.0 1.3 %collective-permute-start.18 = (bf16[464,128]{1,0:T(8,128)(2,1)S(1)}, bf16[464,128]{1,0:T(8,128)(2,1)S(1)}, u32[]{:S(2)}, u32[]{:S(2)}) collective-permute-start(bf16[464,128]{1,0:T(8,128)(2,1)S(1)} %get-tuple-element.123), channel_id=1, source_target_pairs={{0,24},{4,28},{8,16},{12,20},{16,8},{20,12},{24,0},{28,4},{1,25},{... | collective-permute-start | bytes 356360 | tf_op jit(solution)/shard_map/ppermute | solution.py:406
  50.3 1.0 %collective-permute-start.19 = (bf16[464,128]{1,0:T(8,128)(2,1)S(1)}, bf16[464,128]{1,0:T(8,128)(2,1)S(1)}, u32[]{:S(2)}, u32[]{:S(2)}) collective-permute-start(bf16[464,128]{1,0:T(8,128)(2,1)S(1)} %get-tuple-element.124), channel_id=1, source_target_pairs={{0,16},{4,20},{8,24},{12,28},{16,0},{20,4},{24,8},{28,12},{1,17},{... | collective-permute-start | bytes 356360 | tf_op jit(solution)/shard_map/ppermute | solution.py:406
  51.3 1.2 %collective-permute-start.20 = (bf16[464,128]{1,0:T(8,128)(2,1)S(1)}, bf16[464,128]{1,0:T(8,128)(2,1)S(1)}, u32[]{:S(2)}, u32[]{:S(2)}) collective-permute-start(bf16[464,128]{1,0:T(8,128)(2,1)S(1)} %get-tuple-element.125), channel_id=1, source_target_pairs={{0,8},{4,12},{8,0},{12,4},{16,24},{20,28},{24,16},{28,20},{1,9},{5... | collective-permute-start | bytes 356360 | tf_op jit(solution)/shard_map/ppermute | solution.py:406
  52.5 2.7 %collective-permute-start.21 = (bf16[192,128]{1,0:T(8,128)(2,1)S(1)}, bf16[192,128]{1,0:T(8,128)(2,1)S(1)}, u32[]{:S(2)}, u32[]{:S(2)}) collective-permute-start(bf16[192,128]{1,0:T(8,128)(2,1)S(1)} %chip_sum.1.refs_0_), channel_id=1, source_target_pairs={{0,3},{1,2},{2,1},{3,0},{4,7},{5,6},{6,5},{7,4},{8,11},{9,10},{10,... | collective-permute-start | bytes 147464 | tf_op jit(solution)/shard_map/ppermute | solution.py:406
  55.2 0.8 %collective-permute-done.18.refs_1_ = bf16[464,128]{1,0:T(8,128)(2,1)S(1)} collective-permute-done((bf16[464,128]{1,0:T(8,128)(2,1)S(1)}, bf16[464,128]{1,0:T(8,128)(2,1)S(1)}, u32[]{:S(2)}, u32[]{:S(2)}) %collective-permute-start.18) | collective-permute-done | bytes 118816 | tf_op jit(solution)/shard_map/ppermute | solution.py:406
  56.0 0.9 %collective-permute-start.23 = (bf16[192,128]{1,0:T(8,128)(2,1)S(1)}, bf16[192,128]{1,0:T(8,128)(2,1)S(1)}, u32[]{:S(2)}, u32[]{:S(2)}) collective-permute-start(bf16[192,128]{1,0:T(8,128)(2,1)S(1)} %chip_sum.1.refs_0_), channel_id=1, source_target_pairs={{0,1},{1,0},{2,3},{3,2},{4,5},{5,4},{6,7},{7,6},{8,9},{9,8},{10,11... | collective-permute-start | bytes 147464 | tf_op jit(solution)/shard_map/ppermute | solution.py:406
  57.0 2.7 %collective-permute-start.24 = (bf16[240,128]{1,0:T(8,128)(2,1)S(1)}, bf16[240,128]{1,0:T(8,128)(2,1)S(1)}, u32[]{:S(2)}, u32[]{:S(2)}) collective-permute-start(bf16[240,128]{1,0:T(8,128)(2,1)S(1)} %get-tuple-element.143.refs_0_), channel_id=1, source_target_pairs={{0,3},{1,2},{2,1},{3,0},{4,7},{5,6},{6,5},{7,4},{8,11},{9,10},{10,... | collective-permute-start | bytes 184328 | tf_op jit(solution)/shard_map/ppermute | solution.py:406
  59.7 1.7 %collective-permute-start.26 = (bf16[240,128]{1,0:T(8,128)(2,1)S(1)}, bf16[240,128]{1,0:T(8,128)(2,1)S(1)}, u32[]{:S(2)}, u32[]{:S(2)}) collective-permute-start(bf16[240,128]{1,0:T(8,128)(2,1)S(1)} %get-tuple-element.143.refs_0_), channel_id=1, source_target_pairs={{0,1},{1,0},{2,3},{3,2},{4,5},{5,4},{6,7},{7,6},{8,9},{9,8},{10,11... | collective-permute-start | bytes 184328 | tf_op jit(solution)/shard_map/ppermute | solution.py:406
  61.7 0.9 %collective-permute-start.27 = (bf16[416,128]{1,0:T(8,128)(2,1)S(1)}, bf16[416,128]{1,0:T(8,128)(2,1)S(1)}, u32[]{:S(2)}, u32[]{:S(2)}) collective-permute-start(bf16[416,128]{1,0:T(8,128)(2,1)S(1)} %filt_sum.1.refs_0_), channel_id=1, source_target_pairs={{0,8},{4,12},{8,0},{12,4},{16,24},{20,28},{24,16},{28,20},{1,9},{5... | collective-permute-start | bytes 319496 | tf_op jit(solution)/shard_map/ppermute | solution.py:406
  62.6 0.9 %collective-permute-start.28 = (bf16[416,128]{1,0:T(8,128)(2,1)S(1)}, bf16[416,128]{1,0:T(8,128)(2,1)S(1)}, u32[]{:S(2)}, u32[]{:S(2)}) collective-permute-start(bf16[416,128]{1,0:T(8,128)(2,1)S(1)} %filt_sum.1.refs_0_), channel_id=1, source_target_pairs={{0,16},{4,20},{8,24},{12,28},{16,0},{20,4},{24,8},{28,12},{1,17},{... | collective-permute-start | bytes 319496 | tf_op jit(solution)/shard_map/ppermute | solution.py:406
  63.5 1.8 %collective-permute-start.29 = (bf16[416,128]{1,0:T(8,128)(2,1)S(1)}, bf16[416,128]{1,0:T(8,128)(2,1)S(1)}, u32[]{:S(2)}, u32[]{:S(2)}) collective-permute-start(bf16[416,128]{1,0:T(8,128)(2,1)S(1)} %filt_sum.1.refs_0_), channel_id=1, source_target_pairs={{0,24},{4,28},{8,16},{12,20},{16,8},{20,12},{24,0},{28,4},{1,25},{... | collective-permute-start | bytes 319496 | tf_op jit(solution)/shard_map/ppermute | solution.py:406
  65.5 0.8 %collective-permute-start.31 = (bf16[240,128]{1,0:T(8,128)(2,1)S(1)}, bf16[240,128]{1,0:T(8,128)(2,1)S(1)}, u32[]{:S(2)}, u32[]{:S(2)}) collective-permute-start(bf16[240,128]{1,0:T(8,128)(2,1)S(1)} %filt_sum_rest.1.refs_4_), channel_id=1, source_target_pairs={{0,16},{4,20},{8,24},{12,28},{16,0},{20,4},{24,8},{28,12},{1,17},{... | collective-permute-start | bytes 184328 | tf_op jit(solution)/shard_map/ppermute | solution.py:406
  66.3 1.8 %collective-permute-start.32 = (bf16[240,128]{1,0:T(8,128)(2,1)S(1)}, bf16[240,128]{1,0:T(8,128)(2,1)S(1)}, u32[]{:S(2)}, u32[]{:S(2)}) collective-permute-start(bf16[240,128]{1,0:T(8,128)(2,1)S(1)} %filt_sum_rest.1.refs_4_), channel_id=1, source_target_pairs={{0,24},{4,28},{8,16},{12,20},{16,8},{20,12},{24,0},{28,4},{1,25},{... | collective-permute-start | bytes 184328 | tf_op jit(solution)/shard_map/ppermute | solution.py:406
  68.0 1.0 %collective-permute-start.30 = (bf16[240,128]{1,0:T(8,128)(2,1)S(1)}, bf16[240,128]{1,0:T(8,128)(2,1)S(1)}, u32[]{:S(2)}, u32[]{:S(2)}) collective-permute-start(bf16[240,128]{1,0:T(8,128)(2,1)S(1)} %filt_sum_rest.1.refs_4_), channel_id=1, source_target_pairs={{0,8},{4,12},{8,0},{12,4},{16,24},{20,28},{24,16},{28,20},{1,9},{5... | collective-permute-start | bytes 184328 | tf_op jit(solution)/shard_map/ppermute | solution.py:406
  69.6 2.0 %collective-permute-done.31.refs_6_ = bf16[240,128]{1,0:T(8,128)(2,1)S(1)} collective-permute-done((bf16[240,128]{1,0:T(8,128)(2,1)S(1)}, bf16[240,128]{1,0:T(8,128)(2,1)S(1)}, u32[]{:S(2)}, u32[]{:S(2)}) %collective-permute-start.31) | collective-permute-done | bytes 61472 | tf_op jit(solution)/shard_map/ppermute | solution.py:406
  71.5 0.7 collective-permute-done.30.refs_5_
  72.4 1.1 %finish_own.1 = (f32[27,128,128]{2,1,0:T(8,128)}, f32[27,64,128]{2,1,0:T(8,128)}) custom-call(bf16[4,656,128]{2,1,0:T(8,128)(2,1)S(1)} %stack.1.pieces), custom_call_target="tpu_custom_call" | custom-call | bytes 1048576 | tf_op jit(solution)/shard_map/finish_own/pallas_call | solution.py:23
  73.6 1.0 %collective-permute-done.33.pieces = bf16[4,656,128]{2,1,0:T(8,128)(2,1)S(1)} collective-permute-done((bf16[4,656,128]{2,1,0:T(8,128)(2,1)S(1)}, bf16[4,656,128]{2,1,0:T(8,128)(2,1)S(1)}, u32[]{:S(2)}, u32[]{:S(2)}) %collective-permute-start.33) | collective-permute-done | bytes 671776 | tf_op jit(solution)/shard_map/ppermute | solution.py:413
  74.5 1.1 %finish_other.1 = (f32[27,128,128]{2,1,0:T(8,128)}, f32[27,64,128]{2,1,0:T(8,128)}) custom-call(bf16[4,656,128]{2,1,0:T(8,128)(2,1)S(1)} %collective-permute-done.33.pieces, f32[27,128,128]{2,1,0:T(8,128)} %get-tuple-element.149.refs_0_, f32[27,64,128]{2,1,0:T(8,128)} %get-tuple-element.150.refs_1_), custom_call_target="tpu_custom_call", output_to_operand_aliasing={{0}: (1, {}), {1}: (2, {})} | custom-call | bytes 1048576 | tf_op jit(solution)/shard_map/finish_other/pallas_call | solution.py:23
  (50 shorter events, 3.3 us)
Async XLA Ops:
  1.4 8.8 %copy-start = (bf16[4,16,16,128]{3,2,1,0:T(8,128)(2,1)S(1)}, bf16[4,16,16,128]{3,2,1,0:T(8,128)(2,1)}, u32[]{:S(2)}) copy-start(bf16[4,16,16,128]{3,2,1,0:T(8,128)(2,1)} %center.1) | copy-start | bytes 786436
  1.4 11.5 %copy-start.1 = (bf16[27,128,128]{2,1,0:T(8,128)(2,1)S(1)}, bf16[27,128,128]{2,1,0:T(8,128)(2,1)}, u32[]{:S(2)}) copy-start(bf16[27,128,128]{2,1,0:T(8,128)(2,1)} %w.1) | copy-start | bytes 2654212
  1.4 5.6 %collective-permute-start = (bf16[4,2,16,128]{3,2,1,0:T(8,128)(2,1)S(1)}, bf16[4,2,16,128]{3,2,1,0:T(8,128)(2,1)S(1)}, u32[]{:S(2)}, u32[]{:S(2)}) collective-permute-start(bf16[4,2,16,128]{3,2,1,0:T(8,128)(2,1)S(1)} %edges.1), channel_id=1, source_target_pairs={{0,1},{2,3},{1,0},{3,2},{4,5},{6,7},{5,4},{7,6},{8,9},{10,11},{9,8... | collective-permute-start | bytes 98312 | tf_op jit(solution)/shard_map/ppermute | solution.py:423
  4.5 5.7 %collective-permute-start.1 = (bf16[4,2,16,128]{3,2,1,0:T(8,128)(2,1)S(1)}, bf16[4,2,16,128]{3,2,1,0:T(8,128)(2,1)S(1)}, u32[]{:S(2)}, u32[]{:S(2)}) collective-permute-start(bf16[4,2,16,128]{3,2,1,0:T(8,128)(2,1)S(1)} %edges.1), channel_id=1, source_target_pairs={{1,2},{3,0},{2,1},{0,3},{5,6},{7,4},{6,5},{4,7},{9,10},{11,8},{10,... | collective-permute-start | bytes 98312 | tf_op jit(solution)/shard_map/ppermute | solution.py:423
  10.3 2.6 %collective-permute-start.2 = (bf16[3,18,16,128]{3,2,1,0:T(8,128)(2,1)S(1)}, bf16[3,18,16,128]{3,2,1,0:T(8,128)(2,1)S(1)}, u32[]{:S(2)}, u32[]{:S(2)}) collective-permute-start(bf16[3,18,16,128]{3,2,1,0:T(8,128)(2,1)S(1)} %get-tuple-element.80), channel_id=1, source_target_pairs={{0,4},{8,12},{16,20},{24,28},{4,0},{12,8},{20,16},{28,24},{1,5},{9... | collective-permute-start | bytes 663560 | tf_op jit(solution)/shard_map/ppermute | solution.py:423
  10.4 9.2 %collective-permute-start.3 = (bf16[3,18,16,128]{3,2,1,0:T(8,128)(2,1)S(1)}, bf16[3,18,16,128]{3,2,1,0:T(8,128)(2,1)S(1)}, u32[]{:S(2)}, u32[]{:S(2)}) collective-permute-start(bf16[3,18,16,128]{3,2,1,0:T(8,128)(2,1)S(1)} %get-tuple-element.82), channel_id=1, source_target_pairs={{4,8},{12,16},{20,24},{28,0},{8,4},{16,12},{24,20},{0,28},{5,9},{1... | collective-permute-start | bytes 663560 | tf_op jit(solution)/shard_map/ppermute | solution.py:423
  15.1 9.0 %collective-permute-start.7 = (bf16[2,64,128]{2,1,0:T(8,128)(2,1)S(1)}, bf16[2,64,128]{2,1,0:T(8,128)(2,1)S(1)}, u32[]{:S(2)}, u32[]{:S(2)}) collective-permute-start(bf16[2,64,128]{2,1,0:T(8,128)(2,1)S(1)} %get-tuple-element.92.refs_4_), channel_id=1, source_target_pairs={{0,3},{1,2},{2,1},{3,0},{4,7},{5,6},{6,5},{7,4},{8,11},{9,10},{10,... | collective-permute-start | bytes 98312 | tf_op jit(solution)/shard_map/ppermute | solution.py:406
  17.7 8.3 %collective-permute-start.8 = (bf16[2,64,128]{2,1,0:T(8,128)(2,1)S(1)}, bf16[2,64,128]{2,1,0:T(8,128)(2,1)S(1)}, u32[]{:S(2)}, u32[]{:S(2)}) collective-permute-start(bf16[2,64,128]{2,1,0:T(8,128)(2,1)S(1)} %get-tuple-element.92.refs_4_), channel_id=1, source_target_pairs={{0,2},{1,3},{2,0},{3,1},{4,6},{5,7},{6,4},{7,5},{8,10},{9,11},{10,... | collective-permute-start | bytes 98312 | tf_op jit(solution)/shard_map/ppermute | solution.py:406
  17.7 8.3 %collective-permute-start.9 = (bf16[2,64,128]{2,1,0:T(8,128)(2,1)S(1)}, bf16[2,64,128]{2,1,0:T(8,128)(2,1)S(1)}, u32[]{:S(2)}, u32[]{:S(2)}) collective-permute-start(bf16[2,64,128]{2,1,0:T(8,128)(2,1)S(1)} %get-tuple-element.92.refs_4_), channel_id=1, source_target_pairs={{0,1},{1,0},{2,3},{3,2},{4,5},{5,4},{6,7},{7,6},{8,9},{9,8},{10,11... | collective-permute-start | bytes 98312 | tf_op jit(solution)/shard_map/ppermute | solution.py:406
  21.5 5.8 %collective-permute-start.4 = (bf16[2,64,128]{2,1,0:T(8,128)(2,1)S(1)}, bf16[2,64,128]{2,1,0:T(8,128)(2,1)S(1)}, u32[]{:S(2)}, u32[]{:S(2)}) collective-permute-start(bf16[2,64,128]{2,1,0:T(8,128)(2,1)S(1)} %get-tuple-element.88.refs_0_), channel_id=1, source_target_pairs={{0,3},{1,2},{2,1},{3,0},{4,7},{5,6},{6,5},{7,4},{8,11},{9,10},{10,... | collective-permute-start | bytes 98312 | tf_op jit(solution)/shard_map/ppermute | solution.py:406
  24.1 4.8 %collective-permute-start.5 = (bf16[2,64,128]{2,1,0:T(8,128)(2,1)S(1)}, bf16[2,64,128]{2,1,0:T(8,128)(2,1)S(1)}, u32[]{:S(2)}, u32[]{:S(2)}) collective-permute-start(bf16[2,64,128]{2,1,0:T(8,128)(2,1)S(1)} %get-tuple-element.88.refs_0_), channel_id=1, source_target_pairs={{0,2},{1,3},{2,0},{3,1},{4,6},{5,7},{6,4},{7,5},{8,10},{9,11},{10,... | collective-permute-start | bytes 98312 | tf_op jit(solution)/shard_map/ppermute | solution.py:406
  24.1 4.8 %collective-permute-start.6 = (bf16[2,64,128]{2,1,0:T(8,128)(2,1)S(1)}, bf16[2,64,128]{2,1,0:T(8,128)(2,1)S(1)}, u32[]{:S(2)}, u32[]{:S(2)}) collective-permute-start(bf16[2,64,128]{2,1,0:T(8,128)(2,1)S(1)} %get-tuple-element.88.refs_0_), channel_id=1, source_target_pairs={{0,1},{1,0},{2,3},{3,2},{4,5},{5,4},{6,7},{7,6},{8,9},{9,8},{10,11... | collective-permute-start | bytes 98312 | tf_op jit(solution)/shard_map/ppermute | solution.py:406
  26.0 2.9 %copy-start.2 = (bf16[27,128,64]{1,2,0:T(8,128)(2,1)S(1)}, bf16[27,128,64]{1,2,0:T(8,128)(2,1)}, u32[]{:S(2)}) copy-start(bf16[27,128,64]{1,2,0:T(8,128)(2,1)} %param.6) | copy-start | bytes 1327108
  26.0 2.9 %copy-start.3 = (bf16[2,32,8,64]{3,2,1,0:T(8,128)(2,1)S(1)}, bf16[2,32,8,64]{3,2,1,0:T(8,128)(2,1)}, u32[]{:S(2)}) copy-start(bf16[2,32,8,64]{3,2,1,0:T(8,128)(2,1)} %refs_9_.1) | copy-start | bytes 196612
  31.0 6.1 %collective-permute-start.10 = (bf16[4,64,128]{2,1,0:T(8,128)(2,1)S(1)}, bf16[4,64,128]{2,1,0:T(8,128)(2,1)S(1)}, u32[]{:S(2)}, u32[]{:S(2)}) collective-permute-start(bf16[4,64,128]{2,1,0:T(8,128)(2,1)S(1)} %get-tuple-element.101), channel_id=1, source_target_pairs={{0,3},{1,2},{2,1},{3,0},{4,7},{5,6},{6,5},{7,4},{8,11},{9,10},{10,... | collective-permute-start | bytes 196616 | tf_op jit(solution)/shard_map/ppermute | solution.py:406
  32.9 5.9 %collective-permute-start.11 = (bf16[4,64,128]{2,1,0:T(8,128)(2,1)S(1)}, bf16[4,64,128]{2,1,0:T(8,128)(2,1)S(1)}, u32[]{:S(2)}, u32[]{:S(2)}) collective-permute-start(bf16[4,64,128]{2,1,0:T(8,128)(2,1)S(1)} %get-tuple-element.103), channel_id=1, source_target_pairs={{0,2},{1,3},{2,0},{3,1},{4,6},{5,7},{6,4},{7,5},{8,10},{9,11},{10,... | collective-permute-start | bytes 196616 | tf_op jit(solution)/shard_map/ppermute | solution.py:406
  33.6 5.2 %collective-permute-start.12 = (bf16[4,64,128]{2,1,0:T(8,128)(2,1)S(1)}, bf16[4,64,128]{2,1,0:T(8,128)(2,1)S(1)}, u32[]{:S(2)}, u32[]{:S(2)}) collective-permute-start(bf16[4,64,128]{2,1,0:T(8,128)(2,1)S(1)} %get-tuple-element.104), channel_id=1, source_target_pairs={{0,1},{1,0},{2,3},{3,2},{4,5},{5,4},{6,7},{7,6},{8,9},{9,8},{10,11... | collective-permute-start | bytes 196616 | tf_op jit(solution)/shard_map/ppermute | solution.py:406
  39.6 1.5 %collective-permute-start.13 = (bf16[4,192,128]{2,1,0:T(8,128)(2,1)S(1)}, bf16[4,192,128]{2,1,0:T(8,128)(2,1)S(1)}, u32[]{:S(2)}, u32[]{:S(2)}) collective-permute-start(bf16[4,192,128]{2,1,0:T(8,128)(2,1)S(1)} %get-tuple-element.109), channel_id=1, source_target_pairs={{0,4},{4,0},{8,12},{12,8},{16,20},{20,16},{24,28},{28,24},{1,5},{5... | collective-permute-start | bytes 589832 | tf_op jit(solution)/shard_map/ppermute | solution.py:413
  42.0 4.6 %collective-permute-start.14 = (bf16[4,464,128]{2,1,0:T(8,128)(2,1)S(1)}, bf16[4,464,128]{2,1,0:T(8,128)(2,1)S(1)}, u32[]{:S(2)}, u32[]{:S(2)}) collective-permute-start(bf16[4,464,128]{2,1,0:T(8,128)(2,1)S(1)} %early_grad_rest.1), channel_id=1, source_target_pairs={{0,4},{4,0},{8,12},{12,8},{16,20},{20,16},{24,28},{28,24},{1,5},{5... | collective-permute-start | bytes 1425416 | tf_op jit(solution)/shard_map/ppermute | solution.py:413
  42.2 5.1 %collective-permute-start.15 = (bf16[192,128]{1,0:T(8,128)(2,1)S(1)}, bf16[192,128]{1,0:T(8,128)(2,1)S(1)}, u32[]{:S(2)}, u32[]{:S(2)}) collective-permute-start(bf16[192,128]{1,0:T(8,128)(2,1)S(1)} %get-tuple-element.119), channel_id=1, source_target_pairs={{0,24},{4,28},{8,16},{12,20},{16,8},{20,12},{24,0},{28,4},{1,25},{... | collective-permute-start | bytes 147464 | tf_op jit(solution)/shard_map/ppermute | solution.py:406
  43.9 4.3 %collective-permute-start.16 = (bf16[192,128]{1,0:T(8,128)(2,1)S(1)}, bf16[192,128]{1,0:T(8,128)(2,1)S(1)}, u32[]{:S(2)}, u32[]{:S(2)}) collective-permute-start(bf16[192,128]{1,0:T(8,128)(2,1)S(1)} %get-tuple-element.120), channel_id=1, source_target_pairs={{0,16},{4,20},{8,24},{12,28},{16,0},{20,4},{24,8},{28,12},{1,17},{... | collective-permute-start | bytes 147464 | tf_op jit(solution)/shard_map/ppermute | solution.py:406
  44.9 4.1 %collective-permute-start.17 = (bf16[192,128]{1,0:T(8,128)(2,1)S(1)}, bf16[192,128]{1,0:T(8,128)(2,1)S(1)}, u32[]{:S(2)}, u32[]{:S(2)}) collective-permute-start(bf16[192,128]{1,0:T(8,128)(2,1)S(1)} %get-tuple-element.121), channel_id=1, source_target_pairs={{0,8},{4,12},{8,0},{12,4},{16,24},{20,28},{24,16},{28,20},{1,9},{5... | collective-permute-start | bytes 147464 | tf_op jit(solution)/shard_map/ppermute | solution.py:406
  49.0 7.1 %collective-permute-start.18 = (bf16[464,128]{1,0:T(8,128)(2,1)S(1)}, bf16[464,128]{1,0:T(8,128)(2,1)S(1)}, u32[]{:S(2)}, u32[]{:S(2)}) collective-permute-start(bf16[464,128]{1,0:T(8,128)(2,1)S(1)} %get-tuple-element.123), channel_id=1, source_target_pairs={{0,24},{4,28},{8,16},{12,20},{16,8},{20,12},{24,0},{28,4},{1,25},{... | collective-permute-start | bytes 356360 | tf_op jit(solution)/shard_map/ppermute | solution.py:406
  50.3 6.6 %collective-permute-start.19 = (bf16[464,128]{1,0:T(8,128)(2,1)S(1)}, bf16[464,128]{1,0:T(8,128)(2,1)S(1)}, u32[]{:S(2)}, u32[]{:S(2)}) collective-permute-start(bf16[464,128]{1,0:T(8,128)(2,1)S(1)} %get-tuple-element.124), channel_id=1, source_target_pairs={{0,16},{4,20},{8,24},{12,28},{16,0},{20,4},{24,8},{28,12},{1,17},{... | collective-permute-start | bytes 356360 | tf_op jit(solution)/shard_map/ppermute | solution.py:406
  51.3 5.7 %collective-permute-start.20 = (bf16[464,128]{1,0:T(8,128)(2,1)S(1)}, bf16[464,128]{1,0:T(8,128)(2,1)S(1)}, u32[]{:S(2)}, u32[]{:S(2)}) collective-permute-start(bf16[464,128]{1,0:T(8,128)(2,1)S(1)} %get-tuple-element.125), channel_id=1, source_target_pairs={{0,8},{4,12},{8,0},{12,4},{16,24},{20,28},{24,16},{28,20},{1,9},{5... | collective-permute-start | bytes 356360 | tf_op jit(solution)/shard_map/ppermute | solution.py:406
  52.5 7.2 %collective-permute-start.21 = (bf16[192,128]{1,0:T(8,128)(2,1)S(1)}, bf16[192,128]{1,0:T(8,128)(2,1)S(1)}, u32[]{:S(2)}, u32[]{:S(2)}) collective-permute-start(bf16[192,128]{1,0:T(8,128)(2,1)S(1)} %chip_sum.1.refs_0_), channel_id=1, source_target_pairs={{0,3},{1,2},{2,1},{3,0},{4,7},{5,6},{6,5},{7,4},{8,11},{9,10},{10,... | collective-permute-start | bytes 147464 | tf_op jit(solution)/shard_map/ppermute | solution.py:406
  55.2 6.4 %collective-permute-start.22 = (bf16[192,128]{1,0:T(8,128)(2,1)S(1)}, bf16[192,128]{1,0:T(8,128)(2,1)S(1)}, u32[]{:S(2)}, u32[]{:S(2)}) collective-permute-start(bf16[192,128]{1,0:T(8,128)(2,1)S(1)} %chip_sum.1.refs_0_), channel_id=1, source_target_pairs={{0,2},{1,3},{2,0},{3,1},{4,6},{5,7},{6,4},{7,5},{8,10},{9,11},{10,... | collective-permute-start | bytes 147464 | tf_op jit(solution)/shard_map/ppermute | solution.py:406
  56.0 5.6 %collective-permute-start.23 = (bf16[192,128]{1,0:T(8,128)(2,1)S(1)}, bf16[192,128]{1,0:T(8,128)(2,1)S(1)}, u32[]{:S(2)}, u32[]{:S(2)}) collective-permute-start(bf16[192,128]{1,0:T(8,128)(2,1)S(1)} %chip_sum.1.refs_0_), channel_id=1, source_target_pairs={{0,1},{1,0},{2,3},{3,2},{4,5},{5,4},{6,7},{7,6},{8,9},{9,8},{10,11... | collective-permute-start | bytes 147464 | tf_op jit(solution)/shard_map/ppermute | solution.py:406
  57.0 6.5 %collective-permute-start.24 = (bf16[240,128]{1,0:T(8,128)(2,1)S(1)}, bf16[240,128]{1,0:T(8,128)(2,1)S(1)}, u32[]{:S(2)}, u32[]{:S(2)}) collective-permute-start(bf16[240,128]{1,0:T(8,128)(2,1)S(1)} %get-tuple-element.143.refs_0_), channel_id=1, source_target_pairs={{0,3},{1,2},{2,1},{3,0},{4,7},{5,6},{6,5},{7,4},{8,11},{9,10},{10,... | collective-permute-start | bytes 184328 | tf_op jit(solution)/shard_map/ppermute | solution.py:406
  59.7 5.7 %collective-permute-start.25 = (bf16[240,128]{1,0:T(8,128)(2,1)S(1)}, bf16[240,128]{1,0:T(8,128)(2,1)S(1)}, u32[]{:S(2)}, u32[]{:S(2)}) collective-permute-start(bf16[240,128]{1,0:T(8,128)(2,1)S(1)} %get-tuple-element.143.refs_0_), channel_id=1, source_target_pairs={{0,2},{1,3},{2,0},{3,1},{4,6},{5,7},{6,4},{7,5},{8,10},{9,11},{10,... | collective-permute-start | bytes 184328 | tf_op jit(solution)/shard_map/ppermute | solution.py:406
  59.7 5.7 %collective-permute-start.26 = (bf16[240,128]{1,0:T(8,128)(2,1)S(1)}, bf16[240,128]{1,0:T(8,128)(2,1)S(1)}, u32[]{:S(2)}, u32[]{:S(2)}) collective-permute-start(bf16[240,128]{1,0:T(8,128)(2,1)S(1)} %get-tuple-element.143.refs_0_), channel_id=1, source_target_pairs={{0,1},{1,0},{2,3},{3,2},{4,5},{5,4},{6,7},{7,6},{8,9},{9,8},{10,11... | collective-permute-start | bytes 184328 | tf_op jit(solution)/shard_map/ppermute | solution.py:406
  61.7 6.3 %collective-permute-start.27 = (bf16[416,128]{1,0:T(8,128)(2,1)S(1)}, bf16[416,128]{1,0:T(8,128)(2,1)S(1)}, u32[]{:S(2)}, u32[]{:S(2)}) collective-permute-start(bf16[416,128]{1,0:T(8,128)(2,1)S(1)} %filt_sum.1.refs_0_), channel_id=1, source_target_pairs={{0,8},{4,12},{8,0},{12,4},{16,24},{20,28},{24,16},{28,20},{1,9},{5... | collective-permute-start | bytes 319496 | tf_op jit(solution)/shard_map/ppermute | solution.py:406
  62.6 6.5 %collective-permute-start.28 = (bf16[416,128]{1,0:T(8,128)(2,1)S(1)}, bf16[416,128]{1,0:T(8,128)(2,1)S(1)}, u32[]{:S(2)}, u32[]{:S(2)}) collective-permute-start(bf16[416,128]{1,0:T(8,128)(2,1)S(1)} %filt_sum.1.refs_0_), channel_id=1, source_target_pairs={{0,16},{4,20},{8,24},{12,28},{16,0},{20,4},{24,8},{28,12},{1,17},{... | collective-permute-start | bytes 319496 | tf_op jit(solution)/shard_map/ppermute | solution.py:406
  63.5 6.1 %collective-permute-start.29 = (bf16[416,128]{1,0:T(8,128)(2,1)S(1)}, bf16[416,128]{1,0:T(8,128)(2,1)S(1)}, u32[]{:S(2)}, u32[]{:S(2)}) collective-permute-start(bf16[416,128]{1,0:T(8,128)(2,1)S(1)} %filt_sum.1.refs_0_), channel_id=1, source_target_pairs={{0,24},{4,28},{8,16},{12,20},{16,8},{20,12},{24,0},{28,4},{1,25},{... | collective-permute-start | bytes 319496 | tf_op jit(solution)/shard_map/ppermute | solution.py:406
  65.5 6.0 %collective-permute-start.31 = (bf16[240,128]{1,0:T(8,128)(2,1)S(1)}, bf16[240,128]{1,0:T(8,128)(2,1)S(1)}, u32[]{:S(2)}, u32[]{:S(2)}) collective-permute-start(bf16[240,128]{1,0:T(8,128)(2,1)S(1)} %filt_sum_rest.1.refs_4_), channel_id=1, source_target_pairs={{0,16},{4,20},{8,24},{12,28},{16,0},{20,4},{24,8},{28,12},{1,17},{... | collective-permute-start | bytes 184328 | tf_op jit(solution)/shard_map/ppermute | solution.py:406
  66.3 5.3 %collective-permute-start.32 = (bf16[240,128]{1,0:T(8,128)(2,1)S(1)}, bf16[240,128]{1,0:T(8,128)(2,1)S(1)}, u32[]{:S(2)}, u32[]{:S(2)}) collective-permute-start(bf16[240,128]{1,0:T(8,128)(2,1)S(1)} %filt_sum_rest.1.refs_4_), channel_id=1, source_target_pairs={{0,24},{4,28},{8,16},{12,20},{16,8},{20,12},{24,0},{28,4},{1,25},{... | collective-permute-start | bytes 184328 | tf_op jit(solution)/shard_map/ppermute | solution.py:406
  68.0 4.2 %collective-permute-start.30 = (bf16[240,128]{1,0:T(8,128)(2,1)S(1)}, bf16[240,128]{1,0:T(8,128)(2,1)S(1)}, u32[]{:S(2)}, u32[]{:S(2)}) collective-permute-start(bf16[240,128]{1,0:T(8,128)(2,1)S(1)} %filt_sum_rest.1.refs_4_), channel_id=1, source_target_pairs={{0,8},{4,12},{8,0},{12,4},{16,24},{20,28},{24,16},{28,20},{1,9},{5... | collective-permute-start | bytes 184328 | tf_op jit(solution)/shard_map/ppermute | solution.py:406
  72.3 2.2 %collective-permute-start.33 = (bf16[4,656,128]{2,1,0:T(8,128)(2,1)S(1)}, bf16[4,656,128]{2,1,0:T(8,128)(2,1)S(1)}, u32[]{:S(2)}, u32[]{:S(2)}) collective-permute-start(bf16[4,656,128]{2,1,0:T(8,128)(2,1)S(1)} %stack.1.pieces), channel_id=1, source_target_pairs={{0,4},{4,0},{8,12},{12,8},{16,20},{20,16},{24,28},{28,24},{1,5},{5... | collective-permute-start | bytes 2015240 | tf_op jit(solution)/shard_map/ppermute | solution.py:413
